TPU v7x, 512 devices: a whole 4x4x16 slice. The times are simulated.
512 devices in a mesh: row: 64 (over z_lo, y, x), col: 8 (over z_hi, core).
Axes of the slice: x: 4, y: 4, z: 16 (z_hi: 4, z_lo: 4; z = z_hi * 4 + z_lo), core: 2. Of those that a mesh axis runs over, the one named last changes fastest.
Arguments:
- left: bfloat16 [128, 1024, 1024], P(None, 'row', 'col'), may hold values from -6 to 6
- right: bfloat16 [128, 1024, 1024], P(None, 'row', 'col'), may hold values from -6 to 6
- gate_out: bfloat16 [128, 1024, 1024], P(None, 'row', 'col'), may hold values from 0.019897461 to 1
- out_grad: bfloat16 [128, 1024, 1024], P(None, 'row', 'col'), may hold values from -6 to 6
- norm_gain: float32 [128], replicated, may hold values from 0.1 to 1.9
- out_weight: bfloat16 [128, 128], replicated, may hold values from -0.5 to 0.5
- token_mask: int32 [1024], replicated, may hold values 0 or 1
Outputs:
- left_grad: bfloat16 [128, 1024, 1024], P(None, 'row', 'col')
- right_grad: bfloat16 [128, 1024, 1024], P(None, 'row', 'col')
Inputs may be any that keep to these rules, and one draw needn't show every extreme that they name: `token_mask`: 1 marks a real token, 0 a padding token.
All inputs are finite; a program needn't handle non-finite values.
Results may differ from a plain program's by a relative error of at most 0.0058.
Values may be sent and summed in bfloat16 or wider, within the bound.
No kernel may reach another device: no remote copies, remote signals or barrier semaphores. Data moves between devices by JAX's collectives and lax.ppermute only.
A program may use at most 64 MiB of HBM per device.

v0:
```python
import jax
import jax.numpy as jnp
from jax import lax
from jax.sharding import PartitionSpec as P

norm_eps = 1e-05


def on_device(left, right, gate_out, out_grad, norm_gain, out_weight, token_mask):
    hidden_all = left.shape[0]
    row_count = left.shape[1]
    col_count = left.shape[2]
    row_start = lax.axis_index("row") * row_count
    col_start = lax.axis_index("col") * col_count
    mask_float = token_mask.astype(jnp.float32)
    row_mask = lax.dynamic_slice_in_dim(mask_float, row_start, row_count)
    col_mask = lax.dynamic_slice_in_dim(mask_float, col_start, col_count)
    tile_mask = (row_mask[:, None] * col_mask[None, :]).astype(jnp.bfloat16)[None]
    left_masked = left * tile_mask
    right_masked = right * tile_mask
    left_chan, right_chan = (
        lax.all_to_all(left_masked, "row", split_axis=0, concat_axis=1, tiled=True),
        lax.all_to_all(right_masked, "row", split_axis=0, concat_axis=1, tiled=True),
    )
    right_rows = lax.all_to_all(right_chan, "col", split_axis=1, concat_axis=2, tiled=True)
    left_whole = lax.all_gather(left_chan, "col", axis=2, tiled=True)
    product = jnp.einsum("cik,cjk->cij", left_whole, right_rows, preferred_element_type=jnp.float32)
    product_tile = lax.all_to_all(
        product.astype(jnp.bfloat16), "row", split_axis=1, concat_axis=0, tiled=True
    )
    floats = product_tile.astype(jnp.float32)
    center = floats - jnp.mean(floats, axis=0, keepdims=True)
    inv_std = lax.rsqrt(jnp.mean(center * center, axis=0, keepdims=True) + norm_eps)
    normed = center * inv_std
    gated_grad = (gate_out.astype(jnp.float32) * out_grad.astype(jnp.float32)).astype(jnp.bfloat16)
    linear = jnp.dot(
        out_weight, gated_grad.reshape(gated_grad.shape[0], -1), preferred_element_type=jnp.float32
    )
    linear = linear.reshape(hidden_all, row_count, col_count)
    scaled = norm_gain[:, None, None] * linear
    prod_grad = inv_std * (
        scaled
        - jnp.mean(scaled, axis=0, keepdims=True)
        - normed * jnp.mean(scaled * normed, axis=0, keepdims=True)
    )
    grad_chan = lax.all_to_all(
        prod_grad.astype(jnp.bfloat16), "row", split_axis=0, concat_axis=1, tiled=True
    )
    left_sum = jnp.einsum(
        "cij,cjk->cik",
        lax.all_gather(grad_chan, "col", axis=2, tiled=True),
        right_chan,
        preferred_element_type=jnp.float32,
    )
    right_part = jnp.einsum(
        "cij,cik->cjk", grad_chan, left_whole, preferred_element_type=jnp.float32
    )
    right_sum = lax.all_to_all(
        right_part.astype(jnp.bfloat16), "col", split_axis=2, concat_axis=1, tiled=True
    )
    left_home, right_home = (
        lax.all_to_all(
            left_sum.astype(jnp.bfloat16), "row", split_axis=1, concat_axis=0, tiled=True
        ),
        lax.all_to_all(right_sum, "row", split_axis=1, concat_axis=0, tiled=True),
    )
    return (left_home * tile_mask, right_home * tile_mask)


def solution(mesh):
    in_specs = (
        P(None, "row", "col"),
        P(None, "row", "col"),
        P(None, "row", "col"),
        P(None, "row", "col"),
        P(),
        P(),
        P(),
    )
    out_specs = (P(None, "row", "col"), P(None, "row", "col"))
    return jax.shard_map(
        on_device, mesh=mesh, in_specs=in_specs, out_specs=out_specs, check_vma=False
    )
```

profile of v0, /device:TPU:128, one launch (start us, length us, event | category | flops | bytes accessed | tf_op | source)
XLA Modules:
  0.0 385.1 jit_solution(15483346798397341045)
XLA Ops:
  8.1 1.3 broadcast_multiply_fusion
  9.4 29.8 %all_to_all.135 = bf16[128,16,128]{2,1,0:T(8,128)(2,1)S(1)} all-to-all(bf16[128,16,128]{2,1,0:T(8,128)(2,1)S(1)} %get-tuple-element.13), channel_id=1, replica_groups=mesh['row'=64,'col'=8] {'row'}, dimensions={0} | all-to-all | bytes 1048576 | tf_op jit(solution)/shard_map/all_to_all | solution.py:22
  40.1 21.9 %all_to_all.136 = bf16[128,16,128]{2,1,0:T(8,128)(2,1)S(1)} all-to-all(bf16[128,16,128]{2,1,0:T(8,128)(2,1)S(1)} %get-tuple-element.12), channel_id=1, replica_groups=mesh['row'=64,'col'=8] {'row'}, dimensions={0} | all-to-all | bytes 1048576 | tf_op jit(solution)/shard_map/all_to_all | solution.py:23
  62.6 66.8 %all_to_all.137 = bf16[2,1024,128]{2,0,1:T(2,128)(2,1)S(1)} all-to-all(bf16[2,1024,128]{2,0,1:T(2,128)(2,1)S(1)} %copy.54), channel_id=1, replica_groups=mesh['row'=64,'col'=8] {'col'}, dimensions={1} | all-to-all | bytes 1048576 | tf_op jit(solution)/shard_map/all_to_all | solution.py:25
  130.0 18.9 %all-gather.3.cloned.1.call-done = bf16[2,1024,1024]{2,1,0:T(8,128)(2,1)} async-done(((bf16[2,1024,128]{2,1,0:T(8,128)(2,1)}), bf16[2,1024,1024]{2,1,0:T(8,128)(2,1)}) %all-gather.3.cloned.1.call-update) | async-done | bytes 4194320 | tf_op jit(solution)/shard_map/all_gather | solution.py:26
  148.9 3.4 convolution_convert_fusion.2
  152.3 1.3 copy.56
  153.6 15.8 %all-to-all-start.3 = ((bf16[2,1024,128]{2,0,1:T(2,128)(2,1)}), bf16[2,1024,128]{2,0,1:T(2,128)(2,1)S(1)}, u32[]{:S(2)}, u32[]{:S(2)}) async-start(bf16[2,1024,128]{2,0,1:T(2,128)(2,1)} %copy.56), calls=%async_computation.3 | async-start | bytes 1048576 | tf_op jit(solution)/shard_map/all_to_all | solution.py:28
  169.6 18.2 %all-to-all-done.3 = bf16[2,1024,128]{2,0,1:T(2,128)(2,1)S(1)} async-done(((bf16[2,1024,128]{2,0,1:T(2,128)(2,1)}), bf16[2,1024,128]{2,0,1:T(2,128)(2,1)S(1)}, u32[]{:S(2)}, u32[]{:S(2)}) %all-to-all-start.3) | async-done | bytes 524320 | tf_op jit(solution)/shard_map/all_to_all | solution.py:28
  188.5 1.3 copy.85
  189.9 1.5 copy.61
  191.4 2.4 fusion.5
  193.8 1.7 copy.58
  195.9 22.1 %all_to_all.138 = bf16[128,16,128]{2,1,0:T(8,128)(2,1)S(1)} all-to-all(bf16[128,16,128]{2,1,0:T(8,128)(2,1)S(1)} %fusion.4), channel_id=1, replica_groups=mesh['row'=64,'col'=8] {'row'}, dimensions={0} | all-to-all | bytes 1048576 | tf_op jit(solution)/shard_map/all_to_all | solution.py:46
  218.9 3.1 convolution_convert_fusion
  222.4 55.9 %all_to_all.139 = bf16[2,128,1024]{1,0,2:T(2,128)(2,1)S(1)} all-to-all(bf16[2,128,1024]{1,0,2:T(2,128)(2,1)S(1)} %copy.66), channel_id=1, replica_groups=mesh['row'=64,'col'=8] {'col'}, dimensions={2} | all-to-all | bytes 1048576 | tf_op jit(solution)/shard_map/all_to_all | solution.py:58
  278.7 1.3 copy.69
  280.1 7.1 %all-to-all-start.7 = ((bf16[2,1024,128]{2,0,1:T(2,128)(2,1)}), bf16[2,1024,128]{2,0,1:T(2,128)(2,1)S(1)}, u32[]{:S(2)}, u32[]{:S(2)}) async-start(bf16[2,1024,128]{2,0,1:T(2,128)(2,1)} %copy.69), calls=%async_computation.7 | async-start | bytes 1048576 | tf_op jit(solution)/shard_map/all_to_all | solution.py:65
  287.1 37.2 %all-gather.5.cloned.1.call-done = bf16[2,1024,1024]{2,1,0:T(8,128)(2,1)} async-done(((bf16[2,1024,128]{2,1,0:T(8,128)(2,1)}), bf16[2,1024,1024]{2,1,0:T(8,128)(2,1)}) %all-gather.5.cloned.1.call-update) | async-done | bytes 4194320 | tf_op jit(solution)/shard_map/all_gather | solution.py:51
  324.3 3.4 convolution_convert_fusion.1
  327.7 1.3 copy.63
  329.1 8.1 %all-to-all-done.7 = bf16[2,1024,128]{2,0,1:T(2,128)(2,1)S(1)} async-done(((bf16[2,1024,128]{2,0,1:T(2,128)(2,1)}), bf16[2,1024,128]{2,0,1:T(2,128)(2,1)S(1)}, u32[]{:S(2)}, u32[]{:S(2)}) %all-to-all-start.7) | async-done | bytes 524320 | tf_op jit(solution)/shard_map/all_to_all | solution.py:65
  337.2 21.4 %all-to-all-start.5 = ((bf16[2,1024,128]{2,0,1:T(2,128)(2,1)}), bf16[2,1024,128]{2,0,1:T(2,128)(2,1)S(1)}, u32[]{:S(2)}, u32[]{:S(2)}) async-start(bf16[2,1024,128]{2,0,1:T(2,128)(2,1)} %copy.63), calls=%async_computation.5 | async-start | bytes 1048576 | tf_op jit(solution)/shard_map/all_to_all | solution.py:62
  358.7 18.3 %all-to-all-done.5 = bf16[2,1024,128]{2,0,1:T(2,128)(2,1)S(1)} async-done(((bf16[2,1024,128]{2,0,1:T(2,128)(2,1)}), bf16[2,1024,128]{2,0,1:T(2,128)(2,1)S(1)}, u32[]{:S(2)}, u32[]{:S(2)}) %all-to-all-start.5) | async-done | bytes 524320 | tf_op jit(solution)/shard_map/all_to_all | solution.py:62
  (38 shorter events, 7.0 us)
Async XLA Ops:
  7.2 184.2 %copy-start = (bf16[128,128]{1,0:T(8,128)(2,1)S(1)}, bf16[128,128]{1,0:T(8,128)(2,1)}, u32[]{:S(2)}) copy-start(bf16[128,128]{1,0:T(8,128)(2,1)} %param.12) | copy-start | bytes 98308
  7.2 141.7 %all-gather.3.cloned.1.call-start = ((), (), s32[]{:S(2)}) async-start(), calls=%async_computation.8 | async-start | bytes 4718592 | tf_op jit(solution)/shard_map/all_gather | solution.py:26
  129.7 39.7 %copy-start.1 = (bf16[128,16,128]{2,1,0:T(8,128)(2,1)S(1)}, bf16[128,16,128]{2,1,0:T(8,128)(2,1)}, u32[]{:S(2)}) copy-start(bf16[128,16,128]{2,1,0:T(8,128)(2,1)} %param.10) | copy-start | bytes 1572868
  129.8 39.7 %copy-start.2 = (bf16[128,16,128]{2,1,0:T(8,128)(2,1)S(1)}, bf16[128,16,128]{2,1,0:T(8,128)(2,1)}, u32[]{:S(2)}) copy-start(bf16[128,16,128]{2,1,0:T(8,128)(2,1)} %param.9) | copy-start | bytes 1572868
  153.6 34.2 %all-to-all-start.3 = ((bf16[2,1024,128]{2,0,1:T(2,128)(2,1)}), bf16[2,1024,128]{2,0,1:T(2,128)(2,1)S(1)}, u32[]{:S(2)}, u32[]{:S(2)}) async-start(bf16[2,1024,128]{2,0,1:T(2,128)(2,1)} %copy.56), calls=%async_computation.3 | async-start | bytes 1048576 | tf_op jit(solution)/shard_map/all_to_all | solution.py:28
  169.4 154.9 %all-gather.5.cloned.1.call-start = ((), (), s32[]{:S(2)}) async-start(), calls=%async_computation.9 | async-start | bytes 4718592 | tf_op jit(solution)/shard_map/all_gather | solution.py:51
  188.0 3.4 copy-start.3
  280.1 57.1 %all-to-all-start.7 = ((bf16[2,1024,128]{2,0,1:T(2,128)(2,1)}), bf16[2,1024,128]{2,0,1:T(2,128)(2,1)S(1)}, u32[]{:S(2)}, u32[]{:S(2)}) async-start(bf16[2,1024,128]{2,0,1:T(2,128)(2,1)} %copy.69), calls=%async_computation.7 | async-start | bytes 1048576 | tf_op jit(solution)/shard_map/all_to_all | solution.py:65
  337.2 39.9 %all-to-all-start.5 = ((bf16[2,1024,128]{2,0,1:T(2,128)(2,1)}), bf16[2,1024,128]{2,0,1:T(2,128)(2,1)S(1)}, u32[]{:S(2)}, u32[]{:S(2)}) async-start(bf16[2,1024,128]{2,0,1:T(2,128)(2,1)} %copy.63), calls=%async_computation.5 | async-start | bytes 1048576 | tf_op jit(solution)/shard_map/all_to_all | solution.py:62
Sparse Core Ops, SparseCore 0:
  40.2 108.5 all-gather.2
  219.0 105.2 all-gather.4
where the time goes:
time: 386 us; the launch traced here: 385 us
  blocking collectives  197 us (51%)
  waiting for transfers between devices  101 us (26%)
  starting transfers between devices  44.3 us (11%)
  between operations  14.3 us (4%)
  local copies, waits for them, and re-layouts  12.7 us (3%)
  matrix products  12.4 us (3%)
  other arithmetic  4.07 us (1%)
    all_to_all x1, blocking collectives, on_device(): lax.all_to_all(right_chan, 'col', split_axis=1, concat_axis=2, tiled=True)  66.8 us
    all_to_all x1, blocking collectives, on_device(): lax.all_to_all(right_part.astype(jnp.bfloat16), 'col', split_axis=2, conc...  55.9 us
    all_gather x1, waiting for transfers between devices, on_device(): lax.all_gather(grad_chan, 'col', axis=2, tiled=True)  37.2 us
    all_to_all x1, blocking collectives, on_device(): lax.all_to_all(left_masked, 'row', split_axis=0, concat_axis=1, tiled=True)  29.8 us
    all_to_all x1, blocking collectives, on_device(): lax.all_to_all(prod_grad.astype(jnp.bfloat16), 'row', split_axis=0, conca...  22.1 us
    all_to_all x1, blocking collectives, on_device(): lax.all_to_all(right_masked, 'row', split_axis=0, concat_axis=1, tiled=True)  21.9 us
    all_to_all x1, starting transfers between devices, on_device(): lax.all_to_all(left_sum.astype(jnp.bfloat16), 'row', split_axis=1, concat...  21.4 us
    all_gather x1, waiting for transfers between devices, on_device(): left_whole = lax.all_gather(left_chan, 'col', axis=2, tiled=True)  18.9 us
  transfers between devices with their start and end apart: 5, of which 5 were waited for; matrix products, arithmetic and copies ran while one was open for 3% of the time, Pallas kernels for 0%

commit v1 on v0

v1 whole, which is shorter than its diff:
```python
import functools

import jax
import jax.numpy as jnp
from jax import lax
from jax.experimental import pallas as pl
from jax.experimental.pallas import tpu as pltpu
from jax.sharding import Mesh, PartitionSpec as P

norm_eps = 1e-05

AXES = ("zl", "y", "xh", "xl", "zh", "c")
SIZES = (4, 4, 2, 2, 4, 2)
ROW = ("zl", "y", "xh", "xl")
COL = ("zh", "c")
OWNERS = ("zl", "y", "xh", "zh")
BF16 = jnp.bfloat16
F32 = jnp.float32
VMEM_LIMIT = 32 * 1024 * 1024


def gather_left(both_ref):
    return jnp.concatenate(
        [both_ref[:, z, 0:16, :].reshape(512, 128) for z in range(4)], axis=1
    )


def fill_right(x_lo, both_ref, other_ref, right):
    for z in range(4):
        cols = slice(z * 128, (z + 1) * 128)
        mine = both_ref[:, z, 16:32, :].reshape(4, 2, 4, 16, 128)
        other = other_ref[:, z, :, :].reshape(4, 2, 4, 16, 128)
        for yh in range(2):
            right[yh, :, :, x_lo, :, cols] = mine[:, yh]
            right[yh, :, :, 1 - x_lo, :, cols] = other[:, yh]


def product_kernel(place_ref, both_ref, other_ref, keep_ref, send_ref, right):
    x_lo, core = place_ref[0], place_ref[1]
    fill_right(x_lo, both_ref, other_ref, right)
    left = gather_left(both_ref)
    for out_ref, which in ((keep_ref, core), (send_ref, 1 - core)):
        part = lax.dot_general(
            left,
            right[which].reshape(512, 512),
            (((1,), (1,)), ((), ())),
            preferred_element_type=F32,
        )
        for z in range(4):
            out_ref[:, z, :, :] = (
                part[:, z * 128 : (z + 1) * 128].reshape(32, 16, 128).astype(out_ref.dtype)
            )


def grads_kernel(
    place_ref, both_ref, other_ref, grad_ref, grad_other_ref, left_ref, keep_ref, send_ref, right, grad, parts
):
    x_lo, core = place_ref[0], place_ref[1]
    fill_right(x_lo, both_ref, other_ref, right)
    left = gather_left(both_ref)
    for z in range(4):
        cols = slice(z * 128, (z + 1) * 128)
        grad[core, :, :, cols] = grad_ref[:, z, :, :]
        grad[1 - core, :, :, cols] = grad_other_ref[:, z, :, :]
    total = jnp.zeros((512, 512), F32)
    for which in range(2):
        block = grad[which].reshape(512, 512)
        total += jnp.dot(block, right[which].reshape(512, 512), preferred_element_type=F32)
        part = lax.dot_general(
            block, left, (((0,), (0,)), ((), ())), preferred_element_type=F32
        ).reshape(4, 4, 2, 16, 512)
        for half in range(2):
            parts[half, :, which] = part[:, :, half]
    for z in range(4):
        cols = slice(z * 128, (z + 1) * 128)
        left_ref[:, z, :, :] = total[:, cols].reshape(32, 16, 128).astype(BF16)
        keep_ref[:, z, :, :] = parts[x_lo, :, :, :, :, cols].reshape(32, 16, 128)
        send_ref[:, z, :, :] = parts[1 - x_lo, :, :, :, :, cols].reshape(32, 16, 128).astype(BF16)


def norm_kernel(product_ref, scaled_ref, grad_ref):
    count = product_ref.shape[0]

    def load(c):
        return product_ref[c].astype(F32)

    zeros = jnp.zeros(product_ref.shape[1:], F32)

    def sums(c, carry):
        return carry[0] + load(c), carry[1] + scaled_ref[c]

    total, scaled_total = lax.fori_loop(0, count, sums, (zeros, zeros), unroll=8)
    mean = total * (1.0 / count)
    scaled_mean = scaled_total * (1.0 / count)

    def squares(c, carry):
        center = load(c) - mean
        return carry[0] + center * center, carry[1] + scaled_ref[c] * center

    square, cross = lax.fori_loop(0, count, squares, (zeros, zeros), unroll=8)
    inv_std = lax.rsqrt(square * (1.0 / count) + norm_eps)
    slope = inv_std * inv_std * cross * (1.0 / count)

    def write(c, carry):
        center = load(c) - mean
        grad_ref[c] = (inv_std * (scaled_ref[c] - scaled_mean - center * slope)).astype(BF16)
        return carry

    lax.fori_loop(0, count, write, 0, unroll=8)


def vmem():
    return pl.BlockSpec(memory_space=pltpu.VMEM)


def smem():
    return pl.BlockSpec(memory_space=pltpu.SMEM)


def blocks(dtype):
    return jax.ShapeDtypeStruct((32, 4, 16, 128), dtype)


def call(kernel, outs, operands, scratch, flops, scalars=1):
    moved = sum(o.size * o.dtype.itemsize for o in (*operands, *outs))
    return pl.pallas_call(
        kernel,
        out_shape=outs,
        in_specs=[smem()] * scalars + [vmem()] * (len(operands) - scalars),
        out_specs=[vmem()] * len(outs),
        scratch_shapes=scratch,
        compiler_params=pltpu.CompilerParams(vmem_limit_bytes=VMEM_LIMIT),
        cost_estimate=pl.CostEstimate(flops=flops, bytes_accessed=moved, transcendentals=0),
    )(*operands)


def swap(x, axis):
    return lax.ppermute(x, axis, [(0, 1), (1, 0)])


def to_owners(x):
    return lax.all_to_all(x, OWNERS, split_axis=0, concat_axis=0, tiled=True)


def on_device(left, right, gate_out, out_grad, norm_gain, out_weight, token_mask):
    row_count, col_count = left.shape[1:]
    row_start = lax.axis_index(ROW) * row_count
    col_start = lax.axis_index(COL) * col_count
    mask_float = token_mask.astype(F32)
    row_mask = lax.dynamic_slice_in_dim(mask_float, row_start, row_count)
    col_mask = lax.dynamic_slice_in_dim(mask_float, col_start, col_count)
    tile_mask = (row_mask[:, None] * col_mask[None, :]).astype(BF16)[None]
    place = jnp.stack([lax.axis_index("xl"), lax.axis_index("c")]).astype(jnp.int32)

    both = to_owners(jnp.concatenate([left * tile_mask, right * tile_mask], axis=1))

    gated_grad = (gate_out.astype(F32) * out_grad.astype(F32)).astype(BF16)
    linear = jnp.dot(
        out_weight, gated_grad.reshape(gated_grad.shape[0], -1), preferred_element_type=F32
    )
    scaled = norm_gain[:, None, None] * linear.reshape(left.shape)

    both = both.reshape(32, 4, 32, 128)
    other = swap(both[:, :, 16:, :], "xl")
    flops = 2 * 512 * 512 * 1024
    right_scratch = pltpu.VMEM((2, 4, 4, 2, 16, 512), BF16)
    keep, send = call(
        product_kernel, [blocks(F32), blocks(BF16)], [place, both, other], [right_scratch], flops
    )
    product = (keep + swap(send, "c").astype(F32)).astype(BF16)
    product = to_owners(product.reshape(128, 16, 128))

    (grad,) = call(
        norm_kernel,
        [jax.ShapeDtypeStruct(product.shape, BF16)],
        [product, scaled],
        [],
        20 * product.size,
        scalars=0,
    )
    grad = to_owners(grad).reshape(32, 4, 16, 128)
    left_sum, keep, send = call(
        grads_kernel,
        [blocks(BF16), blocks(F32), blocks(BF16)],
        [place, both, other, grad, swap(grad, "c")],
        [
            right_scratch,
            pltpu.VMEM((2, 32, 16, 512), BF16),
            pltpu.VMEM((2, 4, 2, 4, 16, 512), F32),
        ],
        2 * flops,
    )
    right_sum = (keep + swap(send, "xl").astype(F32)).astype(BF16)
    sums = jnp.concatenate([left_sum, right_sum], axis=2).reshape(128, 32, 128)
    home = to_owners(sums)
    return (home[:, :16] * tile_mask, home[:, 16:] * tile_mask)


def solution(mesh):
    fine = Mesh(mesh.devices.reshape(SIZES), AXES)
    tile = P(None, ROW, COL)
    return jax.shard_map(
        on_device,
        mesh=fine,
        in_specs=(tile, tile, tile, tile, P(), P(), P()),
        out_specs=(tile, tile),
        check_vma=False,
    )
```

time: 386 us -> 273 us (0.71)
  the two profiles are of different devices: /device:TPU:128 before, /device:TPU:64 now
where the time goes in v1:
time: 273 us
  blocking collectives  182 us (67%)
  waiting for transfers between devices  59.7 us (22%)
  starting transfers between devices  17.3 us (6%)
  other arithmetic  5.99 us (2%)
  Pallas kernels  4.65 us (2%)
    all_to_all x3, blocking collectives, to_owners(): return lax.all_to_all(x, OWNERS, split_axis=0, concat_axis=0, tiled=True)  182 us
    all_to_all x1, waiting for transfers between devices, to_owners(): return lax.all_to_all(x, OWNERS, split_axis=0, concat_axis=0, tiled=True)  31 us
    ppermute x4, waiting for transfers between devices, swap(): return lax.ppermute(x, axis, [(0, 1), (1, 0)])  28.8 us
    ppermute x4, starting transfers between devices, swap(): return lax.ppermute(x, axis, [(0, 1), (1, 0)])  8.84 us
    all_to_all x1, starting transfers between devices, to_owners(): return lax.all_to_all(x, OWNERS, split_axis=0, concat_axis=0, tiled=True)  8.41 us
  transfers between devices with their start and end apart: 5, of which 5 were waited for; matrix products, arithmetic and copies ran while one was open for 1% of the time, Pallas kernels for 0%

profile of v1, /device:TPU:64, one launch (start us, length us, event | category | flops | bytes accessed | tf_op | source)
XLA Modules:
  0.0 272.6 jit_solution(13014243848083685199)
XLA Ops:
  0.7 0.7 convert_element_type.31
  1.6 1.3 broadcast_multiply_fusion.2
  2.9 77.9 %all_to_all.20 = bf16[128,32,128]{2,1,0:T(8,128)(2,1)S(1)} all-to-all(bf16[128,32,128]{2,1,0:T(8,128)(2,1)S(1)} %pad_maximum_fusion), channel_id=1, replica_groups=mesh['zl'=4,'y'=4,'xh'=2,'xl'=2,'zh'=4,'c'=2] {'zl','y','xh','zh'}, dimensions={0} | all-to-all | bytes 2097152 | tf_op jit(solution)/shard_map/all_to_all | solution.py:142
  80.9 2.5 collective-permute-start
  83.5 11.7 %collective-permute-done.other_ref = bf16[32,4,16,128]{3,2,1,0:T(8,128)(2,1)S(1)} collective-permute-done((bf16[32,4,16,128]{3,2,1,0:T(8,128)(2,1)S(1)}, bf16[32,4,16,128]{3,2,1,0:T(8,128)(2,1)S(1)}, u32[]{:S(2)}, u32[]{:S(2)}) %collective-permute-start) | collective-permute-done | bytes 524320 | tf_op jit(solution)/shard_map/ppermute | solution.py:138
  95.2 1.5 shard_map.86
  96.7 1.9 collective-permute-start.1
  98.6 1.9 collective-permute-done.1
  100.5 1.0 add_convert_fusion.1
  101.4 8.4 %all-to-all-start.1 = ((bf16[128,16,128]{2,1,0:T(8,128)(2,1)}), bf16[128,16,128]{2,1,0:T(8,128)(2,1)S(1)}, u32[]{:S(2)}, u32[]{:S(2)}) async-start(bf16[128,16,128]{2,1,0:T(8,128)(2,1)} %bitcast.3), calls=%async_computation.1 | async-start | bytes 1048576 | tf_op jit(solution)/shard_map/all_to_all | solution.py:142
  110.0 0.3 fusion
  110.4 1.4 copy.10
  111.8 1.4 broadcast_multiply_fusion.scaled_ref
  113.2 31.0 %all-to-all-done.1.product_ref = bf16[128,16,128]{2,1,0:T(8,128)(2,1)S(1)} async-done(((bf16[128,16,128]{2,1,0:T(8,128)(2,1)}), bf16[128,16,128]{2,1,0:T(8,128)(2,1)S(1)}, u32[]{:S(2)}, u32[]{:S(2)}) %all-to-all-start.1) | async-done | bytes 524320 | tf_op jit(solution)/shard_map/all_to_all | solution.py:142
  144.1 0.8 shard_map.87
  144.9 41.2 %all_to_all.21 = bf16[128,16,128]{2,1,0:T(8,128)(2,1)S(1)} all-to-all(bf16[128,16,128]{2,1,0:T(8,128)(2,1)S(1)} %shard_map.87), channel_id=1, replica_groups=mesh['zl'=4,'y'=4,'xh'=2,'xl'=2,'zh'=4,'c'=2] {'zl','y','xh','zh'}, dimensions={0} | all-to-all | bytes 1048576 | tf_op jit(solution)/shard_map/all_to_all | solution.py:142
  186.1 1.9 collective-permute-start.2
  188.1 1.9 collective-permute-done.2.grad_other_ref
  189.9 2.4 shard_map.88
  192.3 2.5 collective-permute-start.3
  194.8 13.3 %collective-permute-done.3 = bf16[32,4,16,128]{3,2,1,0:T(8,128)(2,1)S(1)} collective-permute-done((bf16[32,4,16,128]{3,2,1,0:T(8,128)(2,1)S(1)}, bf16[32,4,16,128]{3,2,1,0:T(8,128)(2,1)S(1)}, u32[]{:S(2)}, u32[]{:S(2)}) %collective-permute-start.3) | collective-permute-done | bytes 524320 | tf_op jit(solution)/shard_map/ppermute | solution.py:138
  208.2 0.2 add_convert_fusion
  208.4 63.2 %all_to_all.22 = bf16[128,32,128]{2,1,0:T(8,128)(2,1)S(1)} all-to-all(bf16[128,32,128]{2,1,0:T(8,128)(2,1)S(1)} %bitcast.19), channel_id=1, replica_groups=mesh['zl'=4,'y'=4,'xh'=2,'xl'=2,'zh'=4,'c'=2] {'zl','y','xh','zh'}, dimensions={0} | all-to-all | bytes 2097152 | tf_op jit(solution)/shard_map/all_to_all | solution.py:142
  271.6 1.0 slice_multiply_fusion
  (16 shorter events, 0.7 us)
Async XLA Ops:
  0.6 109.4 %copy-start = (bf16[128,128]{1,0:T(8,128)(2,1)S(1)}, bf16[128,128]{1,0:T(8,128)(2,1)}, u32[]{:S(2)}) copy-start(bf16[128,128]{1,0:T(8,128)(2,1)} %param.12) | copy-start | bytes 98308
  80.9 14.3 %collective-permute-start = (bf16[32,4,16,128]{3,2,1,0:T(8,128)(2,1)S(1)}, bf16[32,4,16,128]{3,2,1,0:T(8,128)(2,1)S(1)}, u32[]{:S(2)}, u32[]{:S(2)}) collective-permute-start(bf16[32,4,16,128]{3,2,1,0:T(8,128)(2,1)S(1)} %slice.12), channel_id=1, source_target_pairs={{0,8},{8,0},{1,9},{9,1},{2,10},{10,2},{3,11},{11,3},{4,12},{12,4},... | collective-permute-start | bytes 1572872 | tf_op jit(solution)/shard_map/ppermute | solution.py:138
  96.7 3.8 %collective-permute-start.1 = (bf16[32,4,16,128]{3,2,1,0:T(8,128)(2,1)S(1)}, bf16[32,4,16,128]{3,2,1,0:T(8,128)(2,1)S(1)}, u32[]{:S(2)}, u32[]{:S(2)}) collective-permute-start(bf16[32,4,16,128]{3,2,1,0:T(8,128)(2,1)S(1)} %get-tuple-element.8), channel_id=1, source_target_pairs={{0,1},{1,0},{2,3},{3,2},{4,5},{5,4},{6,7},{7,6},{8,9},{9,8},{10,11... | collective-permute-start | bytes 1572872 | tf_op jit(solution)/shard_map/ppermute | solution.py:138
  101.4 8.4 %copy-start.1 = (bf16[128,16,128]{2,1,0:T(8,128)(2,1)S(1)}, bf16[128,16,128]{2,1,0:T(8,128)(2,1)}, u32[]{:S(2)}) copy-start(bf16[128,16,128]{2,1,0:T(8,128)(2,1)} %param.10) | copy-start | bytes 1572868
  101.4 8.4 %copy-start.2 = (bf16[128,16,128]{2,1,0:T(8,128)(2,1)S(1)}, bf16[128,16,128]{2,1,0:T(8,128)(2,1)}, u32[]{:S(2)}) copy-start(bf16[128,16,128]{2,1,0:T(8,128)(2,1)} %param.9) | copy-start | bytes 1572868
  101.4 42.7 %all-to-all-start.1 = ((bf16[128,16,128]{2,1,0:T(8,128)(2,1)}), bf16[128,16,128]{2,1,0:T(8,128)(2,1)S(1)}, u32[]{:S(2)}, u32[]{:S(2)}) async-start(bf16[128,16,128]{2,1,0:T(8,128)(2,1)} %bitcast.3), calls=%async_computation.1 | async-start | bytes 1048576 | tf_op jit(solution)/shard_map/all_to_all | solution.py:142
  110.4 1.4 copy-start.3
  186.1 3.8 %collective-permute-start.2 = (bf16[32,4,16,128]{3,2,1,0:T(8,128)(2,1)S(1)}, bf16[32,4,16,128]{3,2,1,0:T(8,128)(2,1)S(1)}, u32[]{:S(2)}, u32[]{:S(2)}) collective-permute-start(bf16[32,4,16,128]{3,2,1,0:T(8,128)(2,1)S(1)} %bitcast.17), channel_id=1, source_target_pairs={{0,1},{1,0},{2,3},{3,2},{4,5},{5,4},{6,7},{7,6},{8,9},{9,8},{10,11... | collective-permute-start | bytes 1572872 | tf_op jit(solution)/shard_map/ppermute | solution.py:138
  192.3 15.9 %collective-permute-start.3 = (bf16[32,4,16,128]{3,2,1,0:T(8,128)(2,1)S(1)}, bf16[32,4,16,128]{3,2,1,0:T(8,128)(2,1)S(1)}, u32[]{:S(2)}, u32[]{:S(2)}) collective-permute-start(bf16[32,4,16,128]{3,2,1,0:T(8,128)(2,1)S(1)} %get-tuple-element.11), channel_id=1, source_target_pairs={{0,8},{8,0},{1,9},{9,1},{2,10},{10,2},{3,11},{11,3},{4,12},{12,4},... | collective-permute-start | bytes 1572872 | tf_op jit(solution)/shard_map/ppermute | solution.py:138

commit v2 on v1

v2 whole, which is shorter than its diff:
```python
import jax
import jax.numpy as jnp
from jax import lax
from jax.experimental import pallas as pl
from jax.experimental.pallas import tpu as pltpu
from jax.sharding import Mesh, PartitionSpec as P

norm_eps = 1e-05

AXES = ("zl", "y", "xh", "xl", "zh", "c")
SIZES = (4, 4, 2, 2, 4, 2)
ROW = ("zl", "y", "xh", "xl")
COL = ("zh", "c")
PAIR = "xh"
OWNERS = ("zl", "y", "xl", "zh")
BF16 = jnp.bfloat16
F32 = jnp.float32
VMEM_LIMIT = 32 * 1024 * 1024


def lanes(z, half=0):
    return slice(512 * half + 128 * z, 512 * half + 128 * (z + 1))


def whole_left(both_ref, left_other_ref):
    parts = [both_ref[:, z, 0:16, :].reshape(512, 128) for z in range(4)]
    parts += [left_other_ref[:, z, :, :].reshape(512, 128) for z in range(4)]
    return jnp.concatenate(parts, axis=1)


def whole_grad(grad_ref):
    return jnp.concatenate([grad_ref[:, z, :, :].reshape(512, 128) for z in range(4)], axis=1)


def product_kernel(
    place_ref, both_ref, left_other_ref, mine_ref, other_ref, far_mine_ref, far_other_ref, out_ref, right_ref
):
    pair = place_ref[0]
    for z in range(4):
        for half, (near, far) in enumerate(((mine_ref, far_mine_ref), (other_ref, far_other_ref))):
            cols = lanes(z, half)
            right_ref[:, :, pair, :, :, cols] = near[:, z, :, :].reshape(4, 2, 2, 16, 128)
            right_ref[:, :, 1 - pair, :, :, cols] = far[:, z, :, :].reshape(4, 2, 2, 16, 128)
    product = lax.dot_general(
        whole_left(both_ref, left_other_ref),
        right_ref[...].reshape(512, 1024),
        (((1,), (1,)), ((), ())),
        preferred_element_type=F32,
    )
    for z in range(4):
        out_ref[:, z, :, :] = product[:, lanes(z)].reshape(32, 16, 128).astype(BF16)


def right_grad_kernel(place_ref, both_ref, left_other_ref, grad_ref, send_other_ref, send_mine_ref, keep_ref, parts):
    pair = place_ref[0]
    part = lax.dot_general(
        whole_grad(grad_ref),
        whole_left(both_ref, left_other_ref),
        (((0,), (0,)), ((), ())),
        preferred_element_type=F32,
    ).reshape(8, 2, 2, 16, 1024)
    for bit in range(2):
        parts[bit] = part[:, bit]
    for z in range(4):
        for half, send_ref in enumerate((send_mine_ref, send_other_ref)):
            cols = lanes(z, half)
            send_ref[:, z, :, :] = parts[1 - pair, :, :, :, cols].reshape(16, 16, 128).astype(BF16)
            keep_ref[half, :, z, :, :] = parts[pair, :, :, :, cols].reshape(16, 16, 128)


def left_grad_kernel(grad_ref, right_ref, send_ref, keep_ref):
    part = jnp.dot(
        whole_grad(grad_ref), right_ref[...].reshape(512, 1024), preferred_element_type=F32
    )
    for z in range(4):
        keep_ref[:, z, :, :] = part[:, lanes(z)].reshape(32, 16, 128)
        send_ref[:, z, :, :] = part[:, lanes(z, 1)].reshape(32, 16, 128).astype(BF16)


def gather_kernel(place_ref, left_keep_ref, left_got_ref, right_keep_ref, right_got_ref, right_other_ref, out_ref):
    core = place_ref[1]
    out_ref[:, :, :, :, 0:16, :] = (
        (left_keep_ref[...] + left_got_ref[...].astype(F32)).astype(BF16).reshape(4, 2, 4, 4, 16, 128)
    )
    out_ref[:, core, :, :, 16:32, :] = (
        (right_keep_ref[...] + right_got_ref[...].astype(F32)).astype(BF16).reshape(4, 4, 4, 16, 128)
    )
    out_ref[:, 1 - core, :, :, 16:32, :] = right_other_ref[...].reshape(4, 4, 4, 16, 128)


def norm_kernel(product_ref, scaled_ref, grad_ref):
    count = product_ref.shape[0]

    def load(c):
        return product_ref[c].astype(F32)

    zeros = jnp.zeros(product_ref.shape[1:], F32)

    def sums(c, carry):
        return carry[0] + load(c), carry[1] + scaled_ref[c]

    total, scaled_total = lax.fori_loop(0, count, sums, (zeros, zeros), unroll=8)
    mean = total * (1.0 / count)
    scaled_mean = scaled_total * (1.0 / count)

    def squares(c, carry):
        center = load(c) - mean
        return carry[0] + center * center, carry[1] + scaled_ref[c] * center

    square, cross = lax.fori_loop(0, count, squares, (zeros, zeros), unroll=8)
    inv_std = lax.rsqrt(square * (1.0 / count) + norm_eps)
    slope = inv_std * inv_std * cross * (1.0 / count)

    def write(c, carry):
        center = load(c) - mean
        grad_ref[c] = (inv_std * (scaled_ref[c] - scaled_mean - center * slope)).astype(BF16)
        return carry

    lax.fori_loop(0, count, write, 0, unroll=8)


def vmem():
    return pl.BlockSpec(memory_space=pltpu.VMEM)


def smem():
    return pl.BlockSpec(memory_space=pltpu.SMEM)


def shape(dims, dtype):
    return jax.ShapeDtypeStruct(dims, dtype)


def call(kernel, outs, operands, scratch=(), flops=0, scalars=1):
    moved = sum(o.size * o.dtype.itemsize for o in (*operands, *outs))
    return pl.pallas_call(
        kernel,
        out_shape=outs,
        in_specs=[smem()] * scalars + [vmem()] * (len(operands) - scalars),
        out_specs=[vmem()] * len(outs),
        scratch_shapes=scratch,
        compiler_params=pltpu.CompilerParams(vmem_limit_bytes=VMEM_LIMIT),
        cost_estimate=pl.CostEstimate(flops=flops, bytes_accessed=moved, transcendentals=0),
    )(*operands)


def swap(x, axis):
    return lax.ppermute(x, axis, [(0, 1), (1, 0)])


def to_owners(x):
    return lax.all_to_all(x, OWNERS, split_axis=0, concat_axis=0, tiled=True)


def on_device(left, right, gate_out, out_grad, norm_gain, out_weight, token_mask):
    row_count, col_count = left.shape[1:]
    row_start = lax.axis_index(ROW) * row_count
    col_start = lax.axis_index(COL) * col_count
    row_mask = lax.dynamic_slice_in_dim(token_mask, row_start, row_count)
    col_mask = lax.dynamic_slice_in_dim(token_mask, col_start, col_count)
    tile_mask = (row_mask[:, None] * col_mask[None, :]).astype(BF16)[None]
    core = lax.axis_index("c")
    place = jnp.stack([lax.axis_index(PAIR), core]).astype(jnp.int32)

    both = to_owners(jnp.concatenate([left * tile_mask, right * tile_mask], axis=1))
    both, gate_out, out_grad = lax.optimization_barrier((both, gate_out, out_grad))

    rows = both.reshape(4, 2, 4, 4, 32, 128)[:, :, :, :, 16:, :]
    mine = lax.dynamic_index_in_dim(rows, core, 1, keepdims=False).reshape(16, 4, 16, 128)
    far_mine = swap(mine, PAIR)
    other = swap(lax.dynamic_index_in_dim(rows, 1 - core, 1, keepdims=False).reshape(16, 4, 16, 128), "c")
    far_other = swap(other, PAIR)
    both = both.reshape(32, 4, 32, 128)
    left_other = swap(both[:, :, :16, :], "c")

    gated_grad = (gate_out.astype(F32) * out_grad.astype(F32)).astype(BF16)
    linear = jnp.dot(
        out_weight, gated_grad.reshape(gated_grad.shape[0], -1), preferred_element_type=F32
    )
    scaled = norm_gain[:, None, None] * linear.reshape(left.shape)
    far_other, scaled = lax.optimization_barrier((far_other, scaled))

    flops = 2 * 512 * 512 * 1024
    blocks = (32, 4, 16, 128)
    product, right_whole = call(
        product_kernel,
        [shape(blocks, BF16), shape((4, 2, 2, 2, 16, 1024), BF16)],
        [place, both, left_other, mine, other, far_mine, far_other],
        flops=flops,
    )
    product = to_owners(product.reshape(left.shape))
    (grad,) = call(
        norm_kernel,
        [shape(left.shape, BF16)],
        [product, scaled],
        flops=20 * product.size,
        scalars=0,
    )
    grad = to_owners(grad).reshape(blocks)

    half = (16, 4, 16, 128)
    send_other, send_mine, keep = call(
        right_grad_kernel,
        [shape(half, BF16), shape(half, BF16), shape((2, *half), F32)],
        [place, both, left_other, grad],
        [pltpu.VMEM((2, 8, 2, 16, 1024), F32)],
        flops=flops,
    )
    right_other = (keep[1] + swap(send_other, PAIR).astype(F32)).astype(BF16)
    right_got = swap(send_mine, PAIR)
    left_send, left_keep = call(
        left_grad_kernel, [shape(blocks, BF16), shape(blocks, F32)], [grad, right_whole], flops=flops, scalars=0
    )
    (sums,) = call(
        gather_kernel,
        [shape((4, 2, 4, 4, 32, 128), BF16)],
        [place, left_keep, swap(left_send, "c"), keep[0], right_got, swap(right_other, "c")],
    )
    home = to_owners(sums.reshape(128, 32, 128))
    return (home[:, :16] * tile_mask, home[:, 16:] * tile_mask)


def solution(mesh):
    fine = Mesh(mesh.devices.reshape(SIZES), AXES)
    tile = P(None, ROW, COL)
    return jax.shard_map(
        on_device,
        mesh=fine,
        in_specs=(tile, tile, tile, tile, P(), P(), P()),
        out_specs=(tile, tile),
        check_vma=False,
    )
```

time: 273 us -> 271 us (level)
  blocking collectives: 182 us -> 140 us
  starting transfers between devices: 17.3 us -> 43.1 us
  waiting for transfers between devices: 59.7 us -> 71.8 us
    all_to_all x3, blocking collectives: 182 us -> 140 us  [to_owners(): return lax.all_to_all(x, OWNERS, split_axis=0, concat_axis=0, tiled=True)]
    all_to_all x1, waiting for transfers between devices: 31 us -> 55 us  [to_owners(): return lax.all_to_all(x, OWNERS, split_axis=0, concat_axis=0, tiled=True)]
    ppermute x4 -> x8, starting transfers between devices: 8.84 us -> 23.2 us  [swap(): return lax.ppermute(x, axis, [(0, 1), (1, 0)])]
    ppermute x4 -> x8, waiting for transfers between devices: 28.8 us -> 16.8 us  [swap(): return lax.ppermute(x, axis, [(0, 1), (1, 0)])]
    all_to_all x1, starting transfers between devices: 8.41 us -> 20 us  [to_owners(): return lax.all_to_all(x, OWNERS, split_axis=0, concat_axis=0, tiled=True)]
  transfers between devices with their start and end apart: 5 -> 9, of which waited for: 5 -> 3; matrix products, arithmetic and copies ran while one was open for 1% -> 2% of each run, Pallas kernels for 0% -> 0%
where the time goes in v2:
time: 271 us
  blocking collectives  140 us (52%)
  waiting for transfers between devices  71.8 us (26%)
  starting transfers between devices  43.1 us (16%)
  Pallas kernels  5.27 us (2%)
  local copies, waits for them, and re-layouts  4.22 us (2%)
  other arithmetic  3.93 us (1%)
    all_to_all x3, blocking collectives, to_owners(): return lax.all_to_all(x, OWNERS, split_axis=0, concat_axis=0, tiled=True)  140 us
    all_to_all x1, waiting for transfers between devices, to_owners(): return lax.all_to_all(x, OWNERS, split_axis=0, concat_axis=0, tiled=True)  55 us
    ppermute x8, starting transfers between devices, swap(): return lax.ppermute(x, axis, [(0, 1), (1, 0)])  23.2 us
    all_to_all x1, starting transfers between devices, to_owners(): return lax.all_to_all(x, OWNERS, split_axis=0, concat_axis=0, tiled=True)  20 us
    ppermute x8, waiting for transfers between devices, swap(): return lax.ppermute(x, axis, [(0, 1), (1, 0)])  16.8 us
  transfers between devices with their start and end apart: 9, of which 3 were waited for; matrix products, arithmetic and copies ran while one was open for 2% of the time, Pallas kernels for 0%

profile of v2, /device:TPU:64, one launch (start us, length us, event | category | flops | bytes accessed | tf_op | source)
XLA Modules:
  0.0 270.6 jit_solution(18194962941832815246)
XLA Ops:
  2.3 1.3 broadcast_multiply_fusion.2
  3.5 1.1 pad_maximum_fusion
  4.6 20.0 %all-to-all-start = ((bf16[128,32,128]{2,1,0:T(8,128)(2,1)}), bf16[128,32,128]{2,1,0:T(8,128)(2,1)S(1)}, u32[]{:S(2)}, u32[]{:S(2)}) async-start(bf16[128,32,128]{2,1,0:T(8,128)(2,1)} %pad_maximum_fusion), calls=%async_computation | async-start | bytes 2097152 | tf_op jit(solution)/shard_map/all_to_all | solution.py:152
  24.6 55.0 %all-to-all-done = bf16[128,32,128]{2,1,0:T(8,128)(2,1)S(1)} async-done(((bf16[128,32,128]{2,1,0:T(8,128)(2,1)}), bf16[128,32,128]{2,1,0:T(8,128)(2,1)S(1)}, u32[]{:S(2)}, u32[]{:S(2)}) %all-to-all-start) | async-done | bytes 1048608 | tf_op jit(solution)/shard_map/all_to_all | solution.py:152
  79.8 2.1 collective-permute-start.1
  81.9 0.8 slice.24
  82.7 2.4 collective-permute-start
  85.3 1.3 fusion
  86.6 1.7 copy.11
  88.3 4.6 %collective-permute-start.2 = (bf16[16,4,16,128]{3,2,1,0:T(8,128)(2,1)S(1)}, bf16[16,4,16,128]{3,2,1,0:T(8,128)(2,1)S(1)}, u32[]{:S(2)}, u32[]{:S(2)}) collective-permute-start(bf16[16,4,16,128]{3,2,1,0:T(8,128)(2,1)S(1)} %bitcast.34), channel_id=1, source_target_pairs={{0,16},{16,0},{1,17},{17,1},{2,18},{18,2},{3,19},{19,3},{4,20},{20... | collective-permute-start | bytes 786440 | tf_op jit(solution)/shard_map/ppermute | solution.py:148
  93.0 2.7 %collective-permute-start.3 = (bf16[16,4,16,128]{3,2,1,0:T(8,128)(2,1)S(1)}, bf16[16,4,16,128]{3,2,1,0:T(8,128)(2,1)S(1)}, u32[]{:S(2)}, u32[]{:S(2)}) collective-permute-start(bf16[16,4,16,128]{3,2,1,0:T(8,128)(2,1)S(1)} %collective-permute-done.1.other_ref), channel_id=1, source_target_pairs={{0,16},{16,0},{1,17},{17,1},{2,18},{18,2},{3,19},{19,3},{4,20},{20... | collective-permute-start | bytes 786440 | tf_op jit(solution)/shard_map/ppermute | solution.py:148
  95.9 9.6 %collective-permute-done.3.far_other_ref = bf16[16,4,16,128]{3,2,1,0:T(8,128)(2,1)S(1)} collective-permute-done((bf16[16,4,16,128]{3,2,1,0:T(8,128)(2,1)S(1)}, bf16[16,4,16,128]{3,2,1,0:T(8,128)(2,1)S(1)}, u32[]{:S(2)}, u32[]{:S(2)}) %collective-permute-start.3) | collective-permute-done | bytes 262176 | tf_op jit(solution)/shard_map/ppermute | solution.py:148
  105.6 1.6 shard_map.86
  107.2 39.4 %all_to_all.20.product_ref = bf16[128,16,128]{2,1,0:T(8,128)(2,1)S(1)} all-to-all(bf16[128,16,128]{2,1,0:T(8,128)(2,1)S(1)} %bitcast.36), channel_id=1, replica_groups=mesh['zl'=4,'y'=4,'xh'=2,'xl'=2,'zh'=4,'c'=2] {'zl','y','xl','zh'}, dimensions={0} | all-to-all | bytes 1048576 | tf_op jit(solution)/shard_map/all_to_all | solution.py:152
  146.5 0.8 shard_map.87
  147.3 38.7 %all_to_all.21 = bf16[128,16,128]{2,1,0:T(8,128)(2,1)S(1)} all-to-all(bf16[128,16,128]{2,1,0:T(8,128)(2,1)S(1)} %shard_map.87), channel_id=1, replica_groups=mesh['zl'=4,'y'=4,'xh'=2,'xl'=2,'zh'=4,'c'=2] {'zl','y','xl','zh'}, dimensions={0} | all-to-all | bytes 1048576 | tf_op jit(solution)/shard_map/all_to_all | solution.py:152
  186.0 1.5 shard_map.89
  187.5 4.7 %collective-permute-start.6 = (bf16[16,4,16,128]{3,2,1,0:T(8,128)(2,1)S(1)}, bf16[16,4,16,128]{3,2,1,0:T(8,128)(2,1)S(1)}, u32[]{:S(2)}, u32[]{:S(2)}) collective-permute-start(bf16[16,4,16,128]{3,2,1,0:T(8,128)(2,1)S(1)} %get-tuple-element.25), channel_id=1, source_target_pairs={{0,16},{16,0},{1,17},{17,1},{2,18},{18,2},{3,19},{19,3},{4,20},{20... | collective-permute-start | bytes 786440 | tf_op jit(solution)/shard_map/ppermute | solution.py:148
  192.9 1.9 collective-permute-start.4
  194.8 2.7 collective-permute-start.5
  197.6 2.1 collective-permute-start.7
  199.8 7.1 %collective-permute-done.5.right_got_ref = bf16[16,4,16,128]{3,2,1,0:T(8,128)(2,1)S(1)} collective-permute-done((bf16[16,4,16,128]{3,2,1,0:T(8,128)(2,1)S(1)}, bf16[16,4,16,128]{3,2,1,0:T(8,128)(2,1)S(1)}, u32[]{:S(2)}, u32[]{:S(2)}) %collective-permute-start.5) | collective-permute-done | bytes 262176 | tf_op jit(solution)/shard_map/ppermute | solution.py:148
  207.6 62.0 %all_to_all.22 = bf16[128,32,128]{2,1,0:T(8,128)(2,1)S(1)} all-to-all(bf16[128,32,128]{2,1,0:T(8,128)(2,1)S(1)} %bitcast.31), channel_id=1, replica_groups=mesh['zl'=4,'y'=4,'xh'=2,'xl'=2,'zh'=4,'c'=2] {'zl','y','xl','zh'}, dimensions={0} | all-to-all | bytes 2097152 | tf_op jit(solution)/shard_map/all_to_all | solution.py:152
  269.6 1.0 slice_multiply_fusion
  (26 shorter events, 3.7 us)
Async XLA Ops:
  0.6 84.6 %copy-start = (bf16[128,128]{1,0:T(8,128)(2,1)S(1)}, bf16[128,128]{1,0:T(8,128)(2,1)}, u32[]{:S(2)}) copy-start(bf16[128,128]{1,0:T(8,128)(2,1)} %param.12) | copy-start | bytes 98308
  4.6 75.1 %all-to-all-start = ((bf16[128,32,128]{2,1,0:T(8,128)(2,1)}), bf16[128,32,128]{2,1,0:T(8,128)(2,1)S(1)}, u32[]{:S(2)}, u32[]{:S(2)}) async-start(bf16[128,32,128]{2,1,0:T(8,128)(2,1)} %pad_maximum_fusion), calls=%async_computation | async-start | bytes 2097152 | tf_op jit(solution)/shard_map/all_to_all | solution.py:152
  79.7 5.4 %copy-start.1 = (bf16[128,16,128]{2,1,0:T(8,128)(2,1)S(1)}, bf16[128,16,128]{2,1,0:T(8,128)(2,1)}, u32[]{:S(2)}) copy-start(bf16[128,16,128]{2,1,0:T(8,128)(2,1)} %param.10) | copy-start | bytes 1572868
  79.7 5.4 %copy-start.2 = (bf16[128,16,128]{2,1,0:T(8,128)(2,1)S(1)}, bf16[128,16,128]{2,1,0:T(8,128)(2,1)}, u32[]{:S(2)}) copy-start(bf16[128,16,128]{2,1,0:T(8,128)(2,1)} %param.9) | copy-start | bytes 1572868
  79.8 13.2 %collective-permute-start.1 = (bf16[16,4,16,128]{3,2,1,0:T(8,128)(2,1)S(1)}, bf16[16,4,16,128]{3,2,1,0:T(8,128)(2,1)S(1)}, u32[]{:S(2)}, u32[]{:S(2)}) collective-permute-start(bf16[16,4,16,128]{3,2,1,0:T(8,128)(2,1)S(1)} %bitcast.39), channel_id=1, source_target_pairs={{0,1},{1,0},{2,3},{3,2},{4,5},{5,4},{6,7},{7,6},{8,9},{9,8},{10,11... | collective-permute-start | bytes 786440 | tf_op jit(solution)/shard_map/ppermute | solution.py:148
  82.7 22.9 %collective-permute-start = (bf16[32,4,16,128]{3,2,1,0:T(8,128)(2,1)}, bf16[32,4,16,128]{3,2,1,0:T(8,128)(2,1)S(1)}, u32[]{:S(2)}, u32[]{:S(2)}) collective-permute-start(bf16[32,4,16,128]{3,2,1,0:T(8,128)(2,1)} %slice.24), channel_id=1, source_target_pairs={{0,1},{1,0},{2,3},{3,2},{4,5},{5,4},{6,7},{7,6},{8,9},{9,8},{10,11... | collective-permute-start | bytes 1572872 | tf_op jit(solution)/shard_map/ppermute | solution.py:148
  86.6 9.1 %copy-start.3 = (f32[128]{0:T(128)S(1)}, f32[128]{0:T(128)}, u32[]{:S(2)}) copy-start(f32[128]{0:T(128)} %param.11) | copy-start | bytes 1540
  88.3 17.2 %collective-permute-start.2 = (bf16[16,4,16,128]{3,2,1,0:T(8,128)(2,1)S(1)}, bf16[16,4,16,128]{3,2,1,0:T(8,128)(2,1)S(1)}, u32[]{:S(2)}, u32[]{:S(2)}) collective-permute-start(bf16[16,4,16,128]{3,2,1,0:T(8,128)(2,1)S(1)} %bitcast.34), channel_id=1, source_target_pairs={{0,16},{16,0},{1,17},{17,1},{2,18},{18,2},{3,19},{19,3},{4,20},{20... | collective-permute-start | bytes 786440 | tf_op jit(solution)/shard_map/ppermute | solution.py:148
  93.0 12.6 %collective-permute-start.3 = (bf16[16,4,16,128]{3,2,1,0:T(8,128)(2,1)S(1)}, bf16[16,4,16,128]{3,2,1,0:T(8,128)(2,1)S(1)}, u32[]{:S(2)}, u32[]{:S(2)}) collective-permute-start(bf16[16,4,16,128]{3,2,1,0:T(8,128)(2,1)S(1)} %collective-permute-done.1.other_ref), channel_id=1, source_target_pairs={{0,16},{16,0},{1,17},{17,1},{2,18},{18,2},{3,19},{19,3},{4,20},{20... | collective-permute-start | bytes 786440 | tf_op jit(solution)/shard_map/ppermute | solution.py:148
  187.5 10.0 %collective-permute-start.6 = (bf16[16,4,16,128]{3,2,1,0:T(8,128)(2,1)S(1)}, bf16[16,4,16,128]{3,2,1,0:T(8,128)(2,1)S(1)}, u32[]{:S(2)}, u32[]{:S(2)}) collective-permute-start(bf16[16,4,16,128]{3,2,1,0:T(8,128)(2,1)S(1)} %get-tuple-element.25), channel_id=1, source_target_pairs={{0,16},{16,0},{1,17},{17,1},{2,18},{18,2},{3,19},{19,3},{4,20},{20... | collective-permute-start | bytes 786440 | tf_op jit(solution)/shard_map/ppermute | solution.py:148
  192.9 14.0 %collective-permute-start.4 = (bf16[32,4,16,128]{3,2,1,0:T(8,128)(2,1)S(1)}, bf16[32,4,16,128]{3,2,1,0:T(8,128)(2,1)S(1)}, u32[]{:S(2)}, u32[]{:S(2)}) collective-permute-start(bf16[32,4,16,128]{3,2,1,0:T(8,128)(2,1)S(1)} %get-tuple-element.22), channel_id=1, source_target_pairs={{0,1},{1,0},{2,3},{3,2},{4,5},{5,4},{6,7},{7,6},{8,9},{9,8},{10,11... | collective-permute-start | bytes 1572872 | tf_op jit(solution)/shard_map/ppermute | solution.py:148
  194.8 12.1 %collective-permute-start.5 = (bf16[16,4,16,128]{3,2,1,0:T(8,128)(2,1)S(1)}, bf16[16,4,16,128]{3,2,1,0:T(8,128)(2,1)S(1)}, u32[]{:S(2)}, u32[]{:S(2)}) collective-permute-start(bf16[16,4,16,128]{3,2,1,0:T(8,128)(2,1)S(1)} %get-tuple-element.24), channel_id=1, source_target_pairs={{0,16},{16,0},{1,17},{17,1},{2,18},{18,2},{3,19},{19,3},{4,20},{20... | collective-permute-start | bytes 786440 | tf_op jit(solution)/shard_map/ppermute | solution.py:148
  197.6 9.3 %collective-permute-start.7 = (bf16[16,4,16,128]{3,2,1,0:T(8,128)(2,1)S(1)}, bf16[16,4,16,128]{3,2,1,0:T(8,128)(2,1)S(1)}, u32[]{:S(2)}, u32[]{:S(2)}) collective-permute-start(bf16[16,4,16,128]{3,2,1,0:T(8,128)(2,1)S(1)} %fusion.3), channel_id=1, source_target_pairs={{0,1},{1,0},{2,3},{3,2},{4,5},{5,4},{6,7},{7,6},{8,9},{9,8},{10,11... | collective-permute-start | bytes 786440 | tf_op jit(solution)/shard_map/ppermute | solution.py:148

commit v3 on v2

--- a/solution.py
+++ b/solution.py
@@ -33,14 +33,26 @@
 
 
 def product_kernel(
-    place_ref, both_ref, left_other_ref, mine_ref, other_ref, far_mine_ref, far_other_ref, out_ref, right_ref
+    place_ref, both_ref, left_other_ref, near_ref, far_0_ref, far_1_ref, out_ref, right_ref
 ):
-    pair = place_ref[0]
-    for z in range(4):
-        for half, (near, far) in enumerate(((mine_ref, far_mine_ref), (other_ref, far_other_ref))):
-            cols = lanes(z, half)
-            right_ref[:, :, pair, :, :, cols] = near[:, z, :, :].reshape(4, 2, 2, 16, 128)
-            right_ref[:, :, 1 - pair, :, :, cols] = far[:, z, :, :].reshape(4, 2, 2, 16, 128)
+    pair, core = place_ref[0], place_ref[1]
+
+    def place(near, source):
+        for z in range(4):
+            for half in range(2):
+                rows = source[half, :, z, :, :].reshape(4, 2, 2, 16, 128)
+                right_ref[:, :, near, :, :, lanes(z, half)] = rows
+
+    place(pair, near_ref)
+
+    @pl.when(core == 0)
+    def _():
+        place(1 - pair, far_0_ref)
+
+    @pl.when(core == 1)
+    def _():
+        place(1 - pair, far_1_ref)
+
     product = lax.dot_general(
         whole_left(both_ref, left_other_ref),
         right_ref[...].reshape(512, 1024),
@@ -51,10 +63,14 @@
         out_ref[:, z, :, :] = product[:, lanes(z)].reshape(32, 16, 128).astype(BF16)
 
 
-def right_grad_kernel(place_ref, both_ref, left_other_ref, grad_ref, send_other_ref, send_mine_ref, keep_ref, parts):
+def grads_kernel(
+    place_ref, both_ref, left_other_ref, grad_ref, right_ref,
+    send_other_ref, send_mine_ref, keep_ref, left_send_ref, left_keep_ref, parts,
+):
     pair = place_ref[0]
+    grad = whole_grad(grad_ref)
     part = lax.dot_general(
-        whole_grad(grad_ref),
+        grad,
         whole_left(both_ref, left_other_ref),
         (((0,), (0,)), ((), ())),
         preferred_element_type=F32,
@@ -66,15 +82,10 @@
             cols = lanes(z, half)
             send_ref[:, z, :, :] = parts[1 - pair, :, :, :, cols].reshape(16, 16, 128).astype(BF16)
             keep_ref[half, :, z, :, :] = parts[pair, :, :, :, cols].reshape(16, 16, 128)
-
-
-def left_grad_kernel(grad_ref, right_ref, send_ref, keep_ref):
-    part = jnp.dot(
-        whole_grad(grad_ref), right_ref[...].reshape(512, 1024), preferred_element_type=F32
-    )
+    part = jnp.dot(grad, right_ref[...].reshape(512, 1024), preferred_element_type=F32)
     for z in range(4):
-        keep_ref[:, z, :, :] = part[:, lanes(z)].reshape(32, 16, 128)
-        send_ref[:, z, :, :] = part[:, lanes(z, 1)].reshape(32, 16, 128).astype(BF16)
+        left_keep_ref[:, z, :, :] = part[:, lanes(z)].reshape(32, 16, 128)
+        left_send_ref[:, z, :, :] = part[:, lanes(z, 1)].reshape(32, 16, 128).astype(BF16)
 
 
 def gather_kernel(place_ref, left_keep_ref, left_got_ref, right_keep_ref, right_got_ref, right_other_ref, out_ref):
@@ -148,44 +159,50 @@
     return lax.ppermute(x, axis, [(0, 1), (1, 0)])
 
 
+def swap_pair(x, core):
+    at = [2 * bit + core for bit in range(2)]
+    return lax.ppermute(x, (PAIR, "c"), [(at[0], at[1]), (at[1], at[0])])
+
+
 def to_owners(x):
     return lax.all_to_all(x, OWNERS, split_axis=0, concat_axis=0, tiled=True)
 
 
 def on_device(left, right, gate_out, out_grad, norm_gain, out_weight, token_mask):
-    row_count, col_count = left.shape[1:]
-    row_start = lax.axis_index(ROW) * row_count
-    col_start = lax.axis_index(COL) * col_count
-    row_mask = lax.dynamic_slice_in_dim(token_mask, row_start, row_count)
-    col_mask = lax.dynamic_slice_in_dim(token_mask, col_start, col_count)
-    tile_mask = (row_mask[:, None] * col_mask[None, :]).astype(BF16)[None]
     core = lax.axis_index("c")
     place = jnp.stack([lax.axis_index(PAIR), core]).astype(jnp.int32)
+    row_count, col_count = left.shape[1:]
+    mask_float = token_mask.astype(F32)
+    row_mask = lax.dynamic_slice_in_dim(mask_float, lax.axis_index(ROW) * row_count, row_count)
+    col_mask = lax.dynamic_slice_in_dim(mask_float, lax.axis_index(COL) * col_count, col_count)
+    tile_mask = (row_mask[:, None] * col_mask[None, :]).astype(BF16)[None]
 
     both = to_owners(jnp.concatenate([left * tile_mask, right * tile_mask], axis=1))
-    both, gate_out, out_grad = lax.optimization_barrier((both, gate_out, out_grad))
 
     rows = both.reshape(4, 2, 4, 4, 32, 128)[:, :, :, :, 16:, :]
-    mine = lax.dynamic_index_in_dim(rows, core, 1, keepdims=False).reshape(16, 4, 16, 128)
-    far_mine = swap(mine, PAIR)
-    other = swap(lax.dynamic_index_in_dim(rows, 1 - core, 1, keepdims=False).reshape(16, 4, 16, 128), "c")
-    far_other = swap(other, PAIR)
+    half = (16, 4, 16, 128)
+    mine = lax.dynamic_index_in_dim(rows, core, 1, keepdims=False).reshape(half)
+    other = swap(lax.dynamic_index_in_dim(rows, 1 - core, 1, keepdims=False).reshape(half), "c")
+    near = jnp.stack([mine, other])
     both = both.reshape(32, 4, 32, 128)
-    left_other = swap(both[:, :, :16, :], "c")
+    left_mine, near, gate_out, out_grad = lax.optimization_barrier((both[:, :, :16, :], near, gate_out, out_grad))
+    far_1 = swap_pair(near, 1)
+    left_other = swap(left_mine, "c")
 
     gated_grad = (gate_out.astype(F32) * out_grad.astype(F32)).astype(BF16)
     linear = jnp.dot(
         out_weight, gated_grad.reshape(gated_grad.shape[0], -1), preferred_element_type=F32
     )
     scaled = norm_gain[:, None, None] * linear.reshape(left.shape)
-    far_other, scaled = lax.optimization_barrier((far_other, scaled))
+    near_0, far_1, left_other, scaled = lax.optimization_barrier((near, far_1, left_other, scaled))
+    far_0 = swap_pair(near_0, 0)
 
     flops = 2 * 512 * 512 * 1024
     blocks = (32, 4, 16, 128)
     product, right_whole = call(
         product_kernel,
         [shape(blocks, BF16), shape((4, 2, 2, 2, 16, 1024), BF16)],
-        [place, both, left_other, mine, other, far_mine, far_other],
+        [place, both, left_other, near, far_0, far_1],
         flops=flops,
     )
     product = to_owners(product.reshape(left.shape))
@@ -199,18 +216,15 @@
     grad = to_owners(grad).reshape(blocks)
 
     half = (16, 4, 16, 128)
-    send_other, send_mine, keep = call(
-        right_grad_kernel,
-        [shape(half, BF16), shape(half, BF16), shape((2, *half), F32)],
-        [place, both, left_other, grad],
+    send_other, send_mine, keep, left_send, left_keep = call(
+        grads_kernel,
+        [shape(half, BF16), shape(half, BF16), shape((2, *half), F32), shape(blocks, BF16), shape(blocks, F32)],
+        [place, both, left_other, grad, right_whole],
         [pltpu.VMEM((2, 8, 2, 16, 1024), F32)],
-        flops=flops,
+        flops=2 * flops,
     )
     right_other = (keep[1] + swap(send_other, PAIR).astype(F32)).astype(BF16)
     right_got = swap(send_mine, PAIR)
-    left_send, left_keep = call(
-        left_grad_kernel, [shape(blocks, BF16), shape(blocks, F32)], [grad, right_whole], flops=flops, scalars=0
-    )
     (sums,) = call(
         gather_kernel,
         [shape((4, 2, 4, 4, 32, 128), BF16)],

time: 271 us -> 261 us (0.963)
  blocking collectives: 140 us -> 132 us
    all_to_all x3, blocking collectives: 140 us -> 132 us  [to_owners(): return lax.all_to_all(x, OWNERS, split_axis=0, concat_axis=0, tiled=True)]
    ppermute x8 -> x6, starting transfers between devices: 23.2 us -> 15.2 us  [swap(): return lax.ppermute(x, axis, [(0, 1), (1, 0)])]
    ppermute x8 -> x6, waiting for transfers between devices: 16.8 us -> 8.77 us  [swap(): return lax.ppermute(x, axis, [(0, 1), (1, 0)])]
    ppermute x0 -> x2, waiting for transfers between devices: none -> 7.85 us  [swap_pair(): return lax.ppermute(x, (PAIR, 'c'), [(at[0], at[1]), (at[1], at[0])])]
    ppermute x0 -> x2, starting transfers between devices: none -> 5.34 us  [swap_pair(): return lax.ppermute(x, (PAIR, 'c'), [(at[0], at[1]), (at[1], at[0])])]
  transfers between devices with their start and end apart: 9 -> 9, of which waited for: 3 -> 5; matrix products, arithmetic and copies ran while one was open for 2% -> 2% of each run, Pallas kernels for 0% -> 0%
where the time goes in v3:
time: 261 us; the launch traced here: 260 us
  blocking collectives  132 us (51%)
  waiting for transfers between devices  71.7 us (27%)
  starting transfers between devices  40.4 us (15%)
  other arithmetic  5.89 us (2%)
  Pallas kernels  5.11 us (2%)
  local copies, waits for them, and re-layouts  2.98 us (1%)
    all_to_all x3, blocking collectives, to_owners(): return lax.all_to_all(x, OWNERS, split_axis=0, concat_axis=0, tiled=True)  132 us
    all_to_all x1, waiting for transfers between devices, to_owners(): return lax.all_to_all(x, OWNERS, split_axis=0, concat_axis=0, tiled=True)  55.1 us
    all_to_all x1, starting transfers between devices, to_owners(): return lax.all_to_all(x, OWNERS, split_axis=0, concat_axis=0, tiled=True)  20 us
    ppermute x6, starting transfers between devices, swap(): return lax.ppermute(x, axis, [(0, 1), (1, 0)])  15.2 us
    ppermute x6, waiting for transfers between devices, swap(): return lax.ppermute(x, axis, [(0, 1), (1, 0)])  8.77 us
    ppermute x2, waiting for transfers between devices, swap_pair(): return lax.ppermute(x, (PAIR, 'c'), [(at[0], at[1]), (at[1], at[0])])  7.85 us
    ppermute x2, starting transfers between devices, swap_pair(): return lax.ppermute(x, (PAIR, 'c'), [(at[0], at[1]), (at[1], at[0])])  5.34 us
  transfers between devices with their start and end apart: 9, of which 5 were waited for; matrix products, arithmetic and copies ran while one was open for 2% of the time, Pallas kernels for 0%

profile of v3, /device:TPU:64, one launch (start us, length us, event | category | flops | bytes accessed | tf_op | source)
XLA Modules:
  0.0 260.0 jit_solution(8261815783117636235)
XLA Ops:
  1.6 1.3 broadcast_multiply_fusion.2
  2.9 1.1 pad_maximum_fusion
  3.9 20.0 %all-to-all-start = ((bf16[128,32,128]{2,1,0:T(8,128)(2,1)}), bf16[128,32,128]{2,1,0:T(8,128)(2,1)S(1)}, u32[]{:S(2)}, u32[]{:S(2)}) async-start(bf16[128,32,128]{2,1,0:T(8,128)(2,1)} %pad_maximum_fusion), calls=%async_computation | async-start | bytes 2097152 | tf_op jit(solution)/shard_map/all_to_all | solution.py:168
  23.9 55.1 %all-to-all-done = bf16[128,32,128]{2,1,0:T(8,128)(2,1)S(1)} async-done(((bf16[128,32,128]{2,1,0:T(8,128)(2,1)}), bf16[128,32,128]{2,1,0:T(8,128)(2,1)S(1)}, u32[]{:S(2)}, u32[]{:S(2)}) %all-to-all-start) | async-done | bytes 1048608 | tf_op jit(solution)/shard_map/all_to_all | solution.py:168
  79.1 1.9 collective-permute-start
  81.1 1.4 collective-permute-done
  82.6 2.0 collective-permute-start.2
  85.5 1.3 fusion
  86.8 2.6 %copy.11 = f32[128,16,128]{2,1,0:T(8,128)} copy(f32[128,16,128]{0,2,1:T(8,128)} %bitcast.35) | data formatting | bytes 2097152 | tf_op jit(solution)/shard_map/reshape | solution.py:196
  89.5 1.4 broadcast_multiply_fusion.scaled_ref
  90.9 4.6 %collective-permute-start.3 = (bf16[2,16,4,16,128]{4,3,2,1,0:T(8,128)(2,1)S(1)}, bf16[2,16,4,16,128]{4,3,2,1,0:T(8,128)(2,1)S(1)}, u32[]{:S(2)}, u32[]{:S(2)}) collective-permute-start(bf16[2,16,4,16,128]{4,3,2,1,0:T(8,128)(2,1)S(1)} %pad_maximum_fusion.1.near_ref), channel_id=1, source_target_pairs={{0,16},{16,0},{2,18},{18,2},{4,20},{20,4},{6,22},{22,6},{8,24},{24... | collective-permute-start | bytes 1572872 | tf_op jit(solution)/shard_map/ppermute | solution.py:164
  95.7 7.9 %collective-permute-done.3.far_0_ref = bf16[2,16,4,16,128]{4,3,2,1,0:T(8,128)(2,1)S(1)} collective-permute-done((bf16[2,16,4,16,128]{4,3,2,1,0:T(8,128)(2,1)S(1)}, bf16[2,16,4,16,128]{4,3,2,1,0:T(8,128)(2,1)S(1)}, u32[]{:S(2)}, u32[]{:S(2)}) %collective-permute-start.3) | collective-permute-done | bytes 524320 | tf_op jit(solution)/shard_map/ppermute | solution.py:164
  103.5 1.6 shard_map.86
  105.1 33.8 %all_to_all.20.product_ref = bf16[128,16,128]{2,1,0:T(8,128)(2,1)S(1)} all-to-all(bf16[128,16,128]{2,1,0:T(8,128)(2,1)S(1)} %bitcast.34), channel_id=1, replica_groups=mesh['zl'=4,'y'=4,'xh'=2,'xl'=2,'zh'=4,'c'=2] {'zl','y','xl','zh'}, dimensions={0} | all-to-all | bytes 1048576 | tf_op jit(solution)/shard_map/all_to_all | solution.py:168
  138.9 0.8 shard_map.87
  139.7 35.7 %all_to_all.21 = bf16[128,16,128]{2,1,0:T(8,128)(2,1)S(1)} all-to-all(bf16[128,16,128]{2,1,0:T(8,128)(2,1)S(1)} %shard_map.87), channel_id=1, replica_groups=mesh['zl'=4,'y'=4,'xh'=2,'xl'=2,'zh'=4,'c'=2] {'zl','y','xl','zh'}, dimensions={0} | all-to-all | bytes 1048576 | tf_op jit(solution)/shard_map/all_to_all | solution.py:168
  175.4 2.0 shard_map.88
  177.5 4.6 %collective-permute-start.6 = (bf16[16,4,16,128]{3,2,1,0:T(8,128)(2,1)S(1)}, bf16[16,4,16,128]{3,2,1,0:T(8,128)(2,1)S(1)}, u32[]{:S(2)}, u32[]{:S(2)}) collective-permute-start(bf16[16,4,16,128]{3,2,1,0:T(8,128)(2,1)S(1)} %get-tuple-element.31), channel_id=1, source_target_pairs={{0,16},{16,0},{1,17},{17,1},{2,18},{18,2},{3,19},{19,3},{4,20},{20... | collective-permute-start | bytes 786440 | tf_op jit(solution)/shard_map/ppermute | solution.py:159
  182.1 1.9 collective-permute-start.4
  184.1 2.7 %collective-permute-start.5 = (bf16[16,4,16,128]{3,2,1,0:T(8,128)(2,1)S(1)}, bf16[16,4,16,128]{3,2,1,0:T(8,128)(2,1)S(1)}, u32[]{:S(2)}, u32[]{:S(2)}) collective-permute-start(bf16[16,4,16,128]{3,2,1,0:T(8,128)(2,1)S(1)} %get-tuple-element.30), channel_id=1, source_target_pairs={{0,16},{16,0},{1,17},{17,1},{2,18},{18,2},{3,19},{19,3},{4,20},{20... | collective-permute-start | bytes 786440 | tf_op jit(solution)/shard_map/ppermute | solution.py:159
  187.3 1.9 collective-permute-start.7
  189.3 6.9 %collective-permute-done.5.right_got_ref = bf16[16,4,16,128]{3,2,1,0:T(8,128)(2,1)S(1)} collective-permute-done((bf16[16,4,16,128]{3,2,1,0:T(8,128)(2,1)S(1)}, bf16[16,4,16,128]{3,2,1,0:T(8,128)(2,1)S(1)}, u32[]{:S(2)}, u32[]{:S(2)}) %collective-permute-start.5) | collective-permute-done | bytes 262176 | tf_op jit(solution)/shard_map/ppermute | solution.py:159
  196.9 62.1 %all_to_all.22 = bf16[128,32,128]{2,1,0:T(8,128)(2,1)S(1)} all-to-all(bf16[128,32,128]{2,1,0:T(8,128)(2,1)S(1)} %bitcast.32), channel_id=1, replica_groups=mesh['zl'=4,'y'=4,'xh'=2,'xl'=2,'zh'=4,'c'=2] {'zl','y','xl','zh'}, dimensions={0} | all-to-all | bytes 2097152 | tf_op jit(solution)/shard_map/all_to_all | solution.py:168
  258.9 1.0 slice_multiply_fusion
  (27 shorter events, 3.3 us)
Async XLA Ops:
  0.6 84.9 %copy-start = (bf16[128,128]{1,0:T(8,128)(2,1)S(1)}, bf16[128,128]{1,0:T(8,128)(2,1)}, u32[]{:S(2)}) copy-start(bf16[128,128]{1,0:T(8,128)(2,1)} %param.12) | copy-start | bytes 98308
  3.9 75.1 %all-to-all-start = ((bf16[128,32,128]{2,1,0:T(8,128)(2,1)}), bf16[128,32,128]{2,1,0:T(8,128)(2,1)S(1)}, u32[]{:S(2)}, u32[]{:S(2)}) async-start(bf16[128,32,128]{2,1,0:T(8,128)(2,1)} %pad_maximum_fusion), calls=%async_computation | async-start | bytes 2097152 | tf_op jit(solution)/shard_map/all_to_all | solution.py:168
  79.1 3.4 %collective-permute-start = (bf16[16,4,16,128]{3,2,1,0:T(8,128)(2,1)S(1)}, bf16[16,4,16,128]{3,2,1,0:T(8,128)(2,1)S(1)}, u32[]{:S(2)}, u32[]{:S(2)}) collective-permute-start(bf16[16,4,16,128]{3,2,1,0:T(8,128)(2,1)S(1)} %bitcast.38), channel_id=1, source_target_pairs={{0,1},{1,0},{2,3},{3,2},{4,5},{5,4},{6,7},{7,6},{8,9},{9,8},{10,11... | collective-permute-start | bytes 786440 | tf_op jit(solution)/shard_map/ppermute | solution.py:159
  81.0 4.3 %copy-start.1 = (bf16[128,16,128]{2,1,0:T(8,128)(2,1)S(1)}, bf16[128,16,128]{2,1,0:T(8,128)(2,1)}, u32[]{:S(2)}) copy-start(bf16[128,16,128]{2,1,0:T(8,128)(2,1)} %param.10) | copy-start | bytes 1572868
  81.0 4.3 %copy-start.2 = (bf16[128,16,128]{2,1,0:T(8,128)(2,1)S(1)}, bf16[128,16,128]{2,1,0:T(8,128)(2,1)}, u32[]{:S(2)}) copy-start(bf16[128,16,128]{2,1,0:T(8,128)(2,1)} %param.9) | copy-start | bytes 1572868
  82.6 8.3 %collective-permute-start.2 = (bf16[32,4,16,128]{3,2,1,0:T(8,128)(2,1)S(1)}, bf16[32,4,16,128]{3,2,1,0:T(8,128)(2,1)S(1)}, u32[]{:S(2)}, u32[]{:S(2)}) collective-permute-start(bf16[32,4,16,128]{3,2,1,0:T(8,128)(2,1)S(1)} %slice.24), channel_id=1, source_target_pairs={{0,1},{1,0},{2,3},{3,2},{4,5},{5,4},{6,7},{7,6},{8,9},{9,8},{10,11... | collective-permute-start | bytes 1572872 | tf_op jit(solution)/shard_map/ppermute | solution.py:159
  84.6 6.3 %collective-permute-start.1 = (bf16[2,16,4,16,128]{4,3,2,1,0:T(8,128)(2,1)S(1)}, bf16[2,16,4,16,128]{4,3,2,1,0:T(8,128)(2,1)S(1)}, u32[]{:S(2)}, u32[]{:S(2)}) collective-permute-start(bf16[2,16,4,16,128]{4,3,2,1,0:T(8,128)(2,1)S(1)} %pad_maximum_fusion.1.near_ref), channel_id=1, source_target_pairs={{1,17},{17,1},{3,19},{19,3},{5,21},{21,5},{7,23},{23,7},{9,25},{25... | collective-permute-start | bytes 1572872 | tf_op jit(solution)/shard_map/ppermute | solution.py:164
  86.8 2.6 %copy-start.3 = (f32[128]{0:T(128)S(1)}, f32[128]{0:T(128)}, u32[]{:S(2)}) copy-start(f32[128]{0:T(128)} %param.11) | copy-start | bytes 1540
  90.9 12.6 %collective-permute-start.3 = (bf16[2,16,4,16,128]{4,3,2,1,0:T(8,128)(2,1)S(1)}, bf16[2,16,4,16,128]{4,3,2,1,0:T(8,128)(2,1)S(1)}, u32[]{:S(2)}, u32[]{:S(2)}) collective-permute-start(bf16[2,16,4,16,128]{4,3,2,1,0:T(8,128)(2,1)S(1)} %pad_maximum_fusion.1.near_ref), channel_id=1, source_target_pairs={{0,16},{16,0},{2,18},{18,2},{4,20},{20,4},{6,22},{22,6},{8,24},{24... | collective-permute-start | bytes 1572872 | tf_op jit(solution)/shard_map/ppermute | solution.py:164
  177.5 9.8 %collective-permute-start.6 = (bf16[16,4,16,128]{3,2,1,0:T(8,128)(2,1)S(1)}, bf16[16,4,16,128]{3,2,1,0:T(8,128)(2,1)S(1)}, u32[]{:S(2)}, u32[]{:S(2)}) collective-permute-start(bf16[16,4,16,128]{3,2,1,0:T(8,128)(2,1)S(1)} %get-tuple-element.31), channel_id=1, source_target_pairs={{0,16},{16,0},{1,17},{17,1},{2,18},{18,2},{3,19},{19,3},{4,20},{20... | collective-permute-start | bytes 786440 | tf_op jit(solution)/shard_map/ppermute | solution.py:159
  182.1 14.0 %collective-permute-start.4 = (bf16[32,4,16,128]{3,2,1,0:T(8,128)(2,1)S(1)}, bf16[32,4,16,128]{3,2,1,0:T(8,128)(2,1)S(1)}, u32[]{:S(2)}, u32[]{:S(2)}) collective-permute-start(bf16[32,4,16,128]{3,2,1,0:T(8,128)(2,1)S(1)} %get-tuple-element.28), channel_id=1, source_target_pairs={{0,1},{1,0},{2,3},{3,2},{4,5},{5,4},{6,7},{7,6},{8,9},{9,8},{10,11... | collective-permute-start | bytes 1572872 | tf_op jit(solution)/shard_map/ppermute | solution.py:159
  184.1 12.1 %collective-permute-start.5 = (bf16[16,4,16,128]{3,2,1,0:T(8,128)(2,1)S(1)}, bf16[16,4,16,128]{3,2,1,0:T(8,128)(2,1)S(1)}, u32[]{:S(2)}, u32[]{:S(2)}) collective-permute-start(bf16[16,4,16,128]{3,2,1,0:T(8,128)(2,1)S(1)} %get-tuple-element.30), channel_id=1, source_target_pairs={{0,16},{16,0},{1,17},{17,1},{2,18},{18,2},{3,19},{19,3},{4,20},{20... | collective-permute-start | bytes 786440 | tf_op jit(solution)/shard_map/ppermute | solution.py:159
  187.3 8.8 %collective-permute-start.7 = (bf16[16,4,16,128]{3,2,1,0:T(8,128)(2,1)S(1)}, bf16[16,4,16,128]{3,2,1,0:T(8,128)(2,1)S(1)}, u32[]{:S(2)}, u32[]{:S(2)}) collective-permute-start(bf16[16,4,16,128]{3,2,1,0:T(8,128)(2,1)S(1)} %fusion.3), channel_id=1, source_target_pairs={{0,1},{1,0},{2,3},{3,2},{4,5},{5,4},{6,7},{7,6},{8,9},{9,8},{10,11... | collective-permute-start | bytes 786440 | tf_op jit(solution)/shard_map/ppermute | solution.py:159

commit v4 on v3

v4 whole, which is shorter than its diff:
```python
import jax
import jax.numpy as jnp
from jax import lax
from jax.experimental import pallas as pl
from jax.experimental.pallas import tpu as pltpu
from jax.sharding import Mesh, PartitionSpec as P

norm_eps = 1e-05

AXES = ("zl", "y", "xh", "xl", "zh", "c")
SIZES = (4, 4, 2, 2, 4, 2)
ROW = ("zl", "y", "xh", "xl")
COL = ("zh", "c")
PAIR = "xh"
OWNERS = ("zl", "y", "xl", "zh")
BF16 = jnp.bfloat16
F32 = jnp.float32
VMEM_LIMIT = 32 * 1024 * 1024


def lanes(z, half=0):
    return slice(512 * half + 128 * z, 512 * half + 128 * (z + 1))


def whole_left(both_ref, left_low_ref, left_high_ref, i_mask_ref, k_mask_ref):
    parts = [both_ref[:, z, 0:16, :].reshape(512, 128) for z in range(4)]
    for z in range(4):
        ends = [ref[:, z, :, :].reshape(256, 128) for ref in (left_low_ref, left_high_ref)]
        parts.append(jnp.concatenate(ends, axis=0))
    i_mask = i_mask_ref[...]
    masks = [i_mask * k_mask_ref[0:1, 128 * n : 128 * (n + 1)] for n in range(8)]
    return jnp.concatenate([part * mask for part, mask in zip(parts, masks)], axis=1)


def whole_grad(grad_ref):
    return jnp.concatenate([grad_ref[:, z, :, :].reshape(512, 128) for z in range(4)], axis=1)


def product_kernel(
    place_ref, i_mask_ref, j_mask_ref, k_mask_ref, both_ref, left_low_ref, left_high_ref, near_ref, far_0_ref, far_1_ref,
    out_ref, right_ref,
):
    pair, core = place_ref[0], place_ref[1]

    j_masks = j_mask_ref[...].reshape(4, 2, 2, 2, 16, 128)

    def place(bit, source):
        mask = jnp.where(bit == 0, j_masks[:, :, 0], j_masks[:, :, 1])
        for z in range(4):
            for half in range(2):
                rows = source[half, :, z, :, :].reshape(4, 2, 2, 16, 128)
                right_ref[:, :, bit, :, :, lanes(z, half)] = rows * mask

    place(pair, near_ref)

    @pl.when(core == 0)
    def _():
        place(1 - pair, far_0_ref)

    @pl.when(core == 1)
    def _():
        place(1 - pair, far_1_ref)

    product = lax.dot_general(
        whole_left(both_ref, left_low_ref, left_high_ref, i_mask_ref, k_mask_ref),
        right_ref[...].reshape(512, 1024),
        (((1,), (1,)), ((), ())),
        preferred_element_type=F32,
    )
    for z in range(4):
        out_ref[:, z, :, :] = product[:, lanes(z)].reshape(32, 16, 128).astype(BF16)


def right_grad_kernel(
    place_ref, i_mask_ref, k_mask_ref, both_ref, left_low_ref, left_high_ref, grad_ref, send_ref, keep_ref
):
    pair = place_ref[0]
    part = lax.dot_general(
        whole_grad(grad_ref),
        whole_left(both_ref, left_low_ref, left_high_ref, i_mask_ref, k_mask_ref),
        (((0,), (0,)), ((), ())),
        preferred_element_type=F32,
    ).reshape(8, 2, 2, 16, 1024)
    send = jnp.where(pair == 0, part[:, 1], part[:, 0]).astype(BF16)
    keep = jnp.where(pair == 0, part[:, 0], part[:, 1])
    for z in range(4):
        for half in range(2):
            cols = lanes(z, half)
            send_ref[half, :, z, :, :] = send[..., cols].reshape(16, 16, 128)
            keep_ref[half, :, z, :, :] = keep[..., cols].reshape(16, 16, 128)


def left_grad_kernel(place_ref, grad_ref, right_ref, send_ref, keep_ref):
    part = jnp.dot(
        whole_grad(grad_ref), right_ref[...].reshape(512, 1024), preferred_element_type=F32
    )
    for z in range(4):
        keep_ref[:, z, :, :] = part[:, lanes(z)].reshape(32, 16, 128)
        send_ref[:, z, :, :] = part[:, lanes(z, 1)].reshape(32, 16, 128).astype(BF16)


def gather_kernel(place_ref, left_keep_ref, left_got_ref, right_keep_ref, right_got_ref, right_other_ref, out_ref):
    core = place_ref[1]
    out_ref[:, :, :, :, 0:16, :] = (
        (left_keep_ref[...] + left_got_ref[...].astype(F32)).astype(BF16).reshape(4, 2, 4, 4, 16, 128)
    )
    out_ref[:, core, :, :, 16:32, :] = (
        (right_keep_ref[0] + right_got_ref[0].astype(F32)).astype(BF16).reshape(4, 4, 4, 16, 128)
    )
    out_ref[:, 1 - core, :, :, 16:32, :] = right_other_ref[...].reshape(4, 4, 4, 16, 128)


def norm_kernel(product_ref, scaled_ref, grad_ref):
    count = product_ref.shape[0]

    def load(c):
        return product_ref[c].astype(F32)

    zeros = jnp.zeros(product_ref.shape[1:], F32)

    def sums(c, carry):
        return carry[0] + load(c), carry[1] + scaled_ref[c]

    total, scaled_total = lax.fori_loop(0, count, sums, (zeros, zeros), unroll=8)
    mean = total * (1.0 / count)
    scaled_mean = scaled_total * (1.0 / count)

    def squares(c, carry):
        center = load(c) - mean
        return carry[0] + center * center, carry[1] + scaled_ref[c] * center

    square, cross = lax.fori_loop(0, count, squares, (zeros, zeros), unroll=8)
    inv_std = lax.rsqrt(square * (1.0 / count) + norm_eps)
    slope = inv_std * inv_std * cross * (1.0 / count)

    def write(c, carry):
        center = load(c) - mean
        grad_ref[c] = (inv_std * (scaled_ref[c] - scaled_mean - center * slope)).astype(BF16)
        return carry

    lax.fori_loop(0, count, write, 0, unroll=8)


def vmem():
    return pl.BlockSpec(memory_space=pltpu.VMEM)


def smem():
    return pl.BlockSpec(memory_space=pltpu.SMEM)


def shape(dims, dtype):
    return jax.ShapeDtypeStruct(dims, dtype)


def call(kernel, outs, operands, scratch=(), flops=0, scalars=1):
    moved = sum(o.size * o.dtype.itemsize for o in (*operands, *outs))
    return pl.pallas_call(
        kernel,
        out_shape=outs,
        in_specs=[smem()] * scalars + [vmem()] * (len(operands) - scalars),
        out_specs=[vmem()] * len(outs),
        scratch_shapes=scratch,
        compiler_params=pltpu.CompilerParams(vmem_limit_bytes=VMEM_LIMIT),
        cost_estimate=pl.CostEstimate(flops=flops, bytes_accessed=moved, transcendentals=0),
    )(*operands)


def swap(x, axis):
    return lax.ppermute(x, axis, [(0, 1), (1, 0)])


def swap_pair(x, core):
    at = [2 * bit + core for bit in range(2)]
    return lax.ppermute(x, (PAIR, "c"), [(at[0], at[1]), (at[1], at[0])])


def to_owners(x):
    return lax.all_to_all(x, OWNERS, split_axis=0, concat_axis=0, tiled=True)


def on_device(left, right, gate_out, out_grad, norm_gain, out_weight, token_mask):
    core = lax.axis_index("c")
    place = jnp.stack([lax.axis_index(PAIR), core]).astype(jnp.int32)
    pair = lax.axis_index(PAIR)
    both = to_owners(jnp.concatenate([left, right], axis=1))

    tokens = token_mask.astype(BF16)
    i_mask = lax.dynamic_index_in_dim(tokens.reshape(16, 2, 32), pair, 1, keepdims=False).reshape(512, 1)
    halves = tokens.reshape(4, 2, 128)
    mine_mask = lax.dynamic_index_in_dim(halves, core, 1, keepdims=False).reshape(512)
    other_mask = lax.dynamic_index_in_dim(halves, 1 - core, 1, keepdims=False).reshape(512)
    i_mask = jnp.broadcast_to(i_mask, (512, 128))
    j_mask = jnp.broadcast_to(mine_mask[:, None], (512, 128))
    k_mask = jnp.broadcast_to(jnp.concatenate([mine_mask, other_mask])[None], (16, 1024))
    row_mask = lax.dynamic_slice_in_dim(tokens, lax.axis_index(ROW) * 16, 16)
    col_mask = lax.dynamic_slice_in_dim(tokens, lax.axis_index(COL) * 128, 128)
    tile_mask = (row_mask[:, None] * col_mask[None, :])[None]
    gated_grad = (gate_out.astype(F32) * out_grad.astype(F32)).astype(BF16)
    linear = jnp.dot(
        out_weight, gated_grad.reshape(gated_grad.shape[0], -1), preferred_element_type=F32
    )
    scaled = norm_gain[:, None, None] * linear.reshape(left.shape)
    both, i_mask, j_mask, k_mask, tile_mask, scaled = lax.optimization_barrier(
        (both, i_mask, j_mask, k_mask, tile_mask, scaled)
    )

    half = (16, 4, 16, 128)
    rows = both.reshape(4, 2, 4, 4, 32, 128)[:, :, :, :, 16:, :]
    mine = lax.dynamic_index_in_dim(rows, core, 1, keepdims=False).reshape(half)
    other = swap(lax.dynamic_index_in_dim(rows, 1 - core, 1, keepdims=False).reshape(half), "c")
    near = jnp.stack([mine, other])
    far_1 = swap_pair(near, 1)
    both = both.reshape(32, 4, 32, 128)
    left_low, left_high, near = lax.optimization_barrier((both[:16, :, :16, :], both[16:, :, :16, :], near))
    left_low, left_high = swap(left_low, "c"), swap(left_high, "c")
    near_0, far_1, left_low, left_high = lax.optimization_barrier((near, far_1, left_low, left_high))
    far_0 = swap_pair(near_0, 0)

    flops = 2 * 512 * 512 * 1024
    blocks = (32, 4, 16, 128)
    product, right_whole = call(
        product_kernel,
        [shape(blocks, BF16), shape((4, 2, 2, 2, 16, 1024), BF16)],
        [place, i_mask, j_mask, k_mask, both, left_low, left_high, near, far_0, far_1],
        flops=flops,
    )
    product = to_owners(product.reshape(left.shape))
    (grad,) = call(
        norm_kernel,
        [shape(left.shape, BF16)],
        [product, scaled],
        flops=20 * product.size,
        scalars=0,
    )
    grad = to_owners(grad).reshape(blocks)

    half = (16, 4, 16, 128)
    right_send, right_keep = call(
        right_grad_kernel,
        [shape((2, *half), BF16), shape((2, *half), F32)],
        [place, i_mask, k_mask, both, left_low, left_high, grad],
        flops=flops,
    )
    right_got = swap(right_send, PAIR)
    right_other = (right_keep[1] + right_got[1].astype(F32)).astype(BF16)
    left_send, left_keep = call(
        left_grad_kernel, [shape(blocks, BF16), shape(blocks, F32)], [place, grad, right_whole], flops=flops
    )
    (sums,) = call(
        gather_kernel,
        [shape((4, 2, 4, 4, 32, 128), BF16)],
        [place, left_keep, swap(left_send, "c"), right_keep, right_got, swap(right_other, "c")],
    )
    home = to_owners(sums.reshape(128, 32, 128))
    return (home[:, :16] * tile_mask, home[:, 16:] * tile_mask)


def solution(mesh):
    fine = Mesh(mesh.devices.reshape(SIZES), AXES)
    tile = P(None, ROW, COL)
    return jax.shard_map(
        on_device,
        mesh=fine,
        in_specs=(tile, tile, tile, tile, P(), P(), P()),
        out_specs=(tile, tile),
        check_vma=False,
    )
```

time: 261 us -> 250 us (0.958)
  the two profiles are of different devices: /device:TPU:64 before, /device:TPU:4 now
where the time goes in v4:
time: 250 us; the launch traced here: 249 us
  blocking collectives  125 us (50%)
  waiting for transfers between devices  71.4 us (29%)
  starting transfers between devices  40.5 us (16%)
  Pallas kernels  5.62 us (2%)
  other arithmetic  3.9 us (2%)
    all_to_all x3, blocking collectives, to_owners(): return lax.all_to_all(x, OWNERS, split_axis=0, concat_axis=0, tiled=True)  125 us
    all_to_all x1, waiting for transfers between devices, to_owners(): return lax.all_to_all(x, OWNERS, split_axis=0, concat_axis=0, tiled=True)  52.6 us
    all_to_all x1, starting transfers between devices, to_owners(): return lax.all_to_all(x, OWNERS, split_axis=0, concat_axis=0, tiled=True)  20.7 us
    ppermute x6, starting transfers between devices, swap(): return lax.ppermute(x, axis, [(0, 1), (1, 0)])  14.4 us
    ppermute x6, waiting for transfers between devices, swap(): return lax.ppermute(x, axis, [(0, 1), (1, 0)])  10.9 us
    ppermute x2, waiting for transfers between devices, swap_pair(): return lax.ppermute(x, (PAIR, 'c'), [(at[0], at[1]), (at[1], at[0])])  7.86 us
    pallas_call x5, Pallas kernels, call(): pl.pallas_call(kernel, out_shape=outs, in_specs=[smem()] * scalars + [vme...  5.62 us
    ppermute x2, starting transfers between devices, swap_pair(): return lax.ppermute(x, (PAIR, 'c'), [(at[0], at[1]), (at[1], at[0])])  5.32 us
  transfers between devices with their start and end apart: 9, of which 6 were waited for; matrix products, arithmetic and copies ran while one was open for 1% of the time, Pallas kernels for 1%

profile of v4, /device:TPU:4, one launch (start us, length us, event | category | flops | bytes accessed | tf_op | source)
XLA Modules:
  0.0 249.4 jit_solution(10681984023030392308)
XLA Ops:
  0.6 2.3 pad_maximum_fusion
  2.9 20.7 %all-to-all-start = ((bf16[128,32,128]{2,1,0:T(8,128)(2,1)}), bf16[128,32,128]{2,1,0:T(8,128)(2,1)S(1)}, u32[]{:S(2)}, u32[]{:S(2)}) async-start(bf16[128,32,128]{2,1,0:T(8,128)(2,1)} %pad_maximum_fusion), calls=%async_computation | async-start | bytes 2097152 | tf_op jit(solution)/shard_map/all_to_all | solution.py:179
  25.4 52.6 %all-to-all-done = bf16[128,32,128]{2,1,0:T(8,128)(2,1)S(1)} async-done(((bf16[128,32,128]{2,1,0:T(8,128)(2,1)}), bf16[128,32,128]{2,1,0:T(8,128)(2,1)S(1)}, u32[]{:S(2)}, u32[]{:S(2)}) %all-to-all-start) | async-done | bytes 1048608 | tf_op jit(solution)/shard_map/all_to_all | solution.py:179
  78.4 1.9 collective-permute-start
  80.3 1.5 collective-permute-done
  81.9 0.7 collective-permute-start.1
  82.6 3.8 %collective-permute-start.2 = (bf16[16,4,16,128]{3,2,1,0:T(8,128)(2,1)S(1)}, bf16[16,4,16,128]{3,2,1,0:T(8,128)(2,1)S(1)}, u32[]{:S(2)}, u32[]{:S(2)}) collective-permute-start(bf16[16,4,16,128]{3,2,1,0:T(8,128)(2,1)S(1)} %get-tuple-element.26), channel_id=1, source_target_pairs={{0,1},{1,0},{2,3},{3,2},{4,5},{5,4},{6,7},{7,6},{8,9},{9,8},{10,11... | collective-permute-start | bytes 786440 | tf_op jit(solution)/shard_map/ppermute | solution.py:170
  86.4 1.9 collective-permute-start.3
  88.3 1.5 collective-permute-done.3.left_high_ref
  89.8 4.6 %collective-permute-start.4 = (bf16[2,16,4,16,128]{4,3,2,1,0:T(8,128)(2,1)S(1)}, bf16[2,16,4,16,128]{4,3,2,1,0:T(8,128)(2,1)S(1)}, u32[]{:S(2)}, u32[]{:S(2)}) collective-permute-start(bf16[2,16,4,16,128]{4,3,2,1,0:T(8,128)(2,1)S(1)} %pad_maximum_fusion.1.near_ref), channel_id=1, source_target_pairs={{0,16},{16,0},{2,18},{18,2},{4,20},{20,4},{6,22},{22,6},{8,24},{24... | collective-permute-start | bytes 1572872 | tf_op jit(solution)/shard_map/ppermute | solution.py:175
  94.5 7.9 %collective-permute-done.4.far_0_ref = bf16[2,16,4,16,128]{4,3,2,1,0:T(8,128)(2,1)S(1)} collective-permute-done((bf16[2,16,4,16,128]{4,3,2,1,0:T(8,128)(2,1)S(1)}, bf16[2,16,4,16,128]{4,3,2,1,0:T(8,128)(2,1)S(1)}, u32[]{:S(2)}, u32[]{:S(2)}) %collective-permute-start.4) | collective-permute-done | bytes 524320 | tf_op jit(solution)/shard_map/ppermute | solution.py:175
  102.4 1.6 shard_map.86
  104.0 31.7 %all_to_all.20.product_ref = bf16[128,16,128]{2,1,0:T(8,128)(2,1)S(1)} all-to-all(bf16[128,16,128]{2,1,0:T(8,128)(2,1)S(1)} %bitcast.35), channel_id=1, replica_groups=mesh['zl'=4,'y'=4,'xh'=2,'xl'=2,'zh'=4,'c'=2] {'zl','y','xl','zh'}, dimensions={0} | all-to-all | bytes 1048576 | tf_op jit(solution)/shard_map/all_to_all | solution.py:179
  135.7 0.8 shard_map.87
  136.5 30.9 %all_to_all.21 = bf16[128,16,128]{2,1,0:T(8,128)(2,1)S(1)} all-to-all(bf16[128,16,128]{2,1,0:T(8,128)(2,1)S(1)} %shard_map.87), channel_id=1, replica_groups=mesh['zl'=4,'y'=4,'xh'=2,'xl'=2,'zh'=4,'c'=2] {'zl','y','xl','zh'}, dimensions={0} | all-to-all | bytes 1048576 | tf_op jit(solution)/shard_map/all_to_all | solution.py:179
  167.3 1.3 shard_map.89
  168.6 3.0 %collective-permute-start.6 = (bf16[2,16,4,16,128]{4,3,2,1,0:T(8,128)(2,1)S(1)}, bf16[2,16,4,16,128]{4,3,2,1,0:T(8,128)(2,1)S(1)}, u32[]{:S(2)}, u32[]{:S(2)}) collective-permute-start(bf16[2,16,4,16,128]{4,3,2,1,0:T(8,128)(2,1)S(1)} %get-tuple-element.38), channel_id=1, source_target_pairs={{0,16},{16,0},{1,17},{17,1},{2,18},{18,2},{3,19},{19,3},{4,20},{20... | collective-permute-start | bytes 1572872 | tf_op jit(solution)/shard_map/ppermute | solution.py:170
  171.6 1.2 shard_map.88
  172.9 1.9 collective-permute-start.5
  174.8 6.4 %collective-permute-done.6.right_got_ref = bf16[2,16,4,16,128]{4,3,2,1,0:T(8,128)(2,1)S(1)} collective-permute-done((bf16[2,16,4,16,128]{4,3,2,1,0:T(8,128)(2,1)S(1)}, bf16[2,16,4,16,128]{4,3,2,1,0:T(8,128)(2,1)S(1)}, u32[]{:S(2)}, u32[]{:S(2)}) %collective-permute-start.6) | collective-permute-done | bytes 524320 | tf_op jit(solution)/shard_map/ppermute | solution.py:170
  181.3 1.9 collective-permute-start.7
  183.2 1.5 collective-permute-done.7.right_other_ref
  185.4 62.9 %all_to_all.22 = bf16[128,32,128]{2,1,0:T(8,128)(2,1)S(1)} all-to-all(bf16[128,32,128]{2,1,0:T(8,128)(2,1)S(1)} %bitcast.32), channel_id=1, replica_groups=mesh['zl'=4,'y'=4,'xh'=2,'xl'=2,'zh'=4,'c'=2] {'zl','y','xl','zh'}, dimensions={0} | all-to-all | bytes 2097152 | tf_op jit(solution)/shard_map/all_to_all | solution.py:179
  248.3 1.0 slice_multiply_fusion
  (36 shorter events, 3.0 us)
Async XLA Ops:
  0.6 23.5 %copy-start = (bf16[128,128]{1,0:T(8,128)(2,1)S(1)}, bf16[128,128]{1,0:T(8,128)(2,1)}, u32[]{:S(2)}) copy-start(bf16[128,128]{1,0:T(8,128)(2,1)} %param.12) | copy-start | bytes 98308
  2.9 20.7 %copy-start.3 = (s32[1024]{0:T(1024)S(1)}, s32[1024]{0:T(1024)}, u32[]{:S(2)}) copy-start(s32[1024]{0:T(1024)} %param.13) | copy-start | bytes 12292
  2.9 21.1 %copy-start.1 = (bf16[128,16,128]{2,1,0:T(8,128)(2,1)S(1)}, bf16[128,16,128]{2,1,0:T(8,128)(2,1)}, u32[]{:S(2)}) copy-start(bf16[128,16,128]{2,1,0:T(8,128)(2,1)} %param.10) | copy-start | bytes 1572868
  2.9 21.1 %copy-start.2 = (bf16[128,16,128]{2,1,0:T(8,128)(2,1)S(1)}, bf16[128,16,128]{2,1,0:T(8,128)(2,1)}, u32[]{:S(2)}) copy-start(bf16[128,16,128]{2,1,0:T(8,128)(2,1)} %param.9) | copy-start | bytes 1572868
  2.9 75.1 %all-to-all-start = ((bf16[128,32,128]{2,1,0:T(8,128)(2,1)}), bf16[128,32,128]{2,1,0:T(8,128)(2,1)S(1)}, u32[]{:S(2)}, u32[]{:S(2)}) async-start(bf16[128,32,128]{2,1,0:T(8,128)(2,1)} %pad_maximum_fusion), calls=%async_computation | async-start | bytes 2097152 | tf_op jit(solution)/shard_map/all_to_all | solution.py:179
  24.5 0.7 copy-start.4
  78.4 3.4 %collective-permute-start = (bf16[16,4,16,128]{3,2,1,0:T(8,128)(2,1)S(1)}, bf16[16,4,16,128]{3,2,1,0:T(8,128)(2,1)S(1)}, u32[]{:S(2)}, u32[]{:S(2)}) collective-permute-start(bf16[16,4,16,128]{3,2,1,0:T(8,128)(2,1)S(1)} %bitcast.39), channel_id=1, source_target_pairs={{0,1},{1,0},{2,3},{3,2},{4,5},{5,4},{6,7},{7,6},{8,9},{9,8},{10,11... | collective-permute-start | bytes 786440 | tf_op jit(solution)/shard_map/ppermute | solution.py:170
  81.9 8.0 %collective-permute-start.1 = (bf16[2,16,4,16,128]{4,3,2,1,0:T(8,128)(2,1)S(1)}, bf16[2,16,4,16,128]{4,3,2,1,0:T(8,128)(2,1)S(1)}, u32[]{:S(2)}, u32[]{:S(2)}) collective-permute-start(bf16[2,16,4,16,128]{4,3,2,1,0:T(8,128)(2,1)S(1)} %pad_maximum_fusion.1.near_ref), channel_id=1, source_target_pairs={{1,17},{17,1},{3,19},{19,3},{5,21},{21,5},{7,23},{23,7},{9,25},{25... | collective-permute-start | bytes 1572872 | tf_op jit(solution)/shard_map/ppermute | solution.py:175
  82.6 5.7 %collective-permute-start.2 = (bf16[16,4,16,128]{3,2,1,0:T(8,128)(2,1)S(1)}, bf16[16,4,16,128]{3,2,1,0:T(8,128)(2,1)S(1)}, u32[]{:S(2)}, u32[]{:S(2)}) collective-permute-start(bf16[16,4,16,128]{3,2,1,0:T(8,128)(2,1)S(1)} %get-tuple-element.26), channel_id=1, source_target_pairs={{0,1},{1,0},{2,3},{3,2},{4,5},{5,4},{6,7},{7,6},{8,9},{9,8},{10,11... | collective-permute-start | bytes 786440 | tf_op jit(solution)/shard_map/ppermute | solution.py:170
  86.4 3.4 %collective-permute-start.3 = (bf16[16,4,16,128]{3,2,1,0:T(8,128)(2,1)S(1)}, bf16[16,4,16,128]{3,2,1,0:T(8,128)(2,1)S(1)}, u32[]{:S(2)}, u32[]{:S(2)}) collective-permute-start(bf16[16,4,16,128]{3,2,1,0:T(8,128)(2,1)S(1)} %get-tuple-element.27), channel_id=1, source_target_pairs={{0,1},{1,0},{2,3},{3,2},{4,5},{5,4},{6,7},{7,6},{8,9},{9,8},{10,11... | collective-permute-start | bytes 786440 | tf_op jit(solution)/shard_map/ppermute | solution.py:170
  89.8 12.6 %collective-permute-start.4 = (bf16[2,16,4,16,128]{4,3,2,1,0:T(8,128)(2,1)S(1)}, bf16[2,16,4,16,128]{4,3,2,1,0:T(8,128)(2,1)S(1)}, u32[]{:S(2)}, u32[]{:S(2)}) collective-permute-start(bf16[2,16,4,16,128]{4,3,2,1,0:T(8,128)(2,1)S(1)} %pad_maximum_fusion.1.near_ref), channel_id=1, source_target_pairs={{0,16},{16,0},{2,18},{18,2},{4,20},{20,4},{6,22},{22,6},{8,24},{24... | collective-permute-start | bytes 1572872 | tf_op jit(solution)/shard_map/ppermute | solution.py:175
  168.6 12.6 %collective-permute-start.6 = (bf16[2,16,4,16,128]{4,3,2,1,0:T(8,128)(2,1)S(1)}, bf16[2,16,4,16,128]{4,3,2,1,0:T(8,128)(2,1)S(1)}, u32[]{:S(2)}, u32[]{:S(2)}) collective-permute-start(bf16[2,16,4,16,128]{4,3,2,1,0:T(8,128)(2,1)S(1)} %get-tuple-element.38), channel_id=1, source_target_pairs={{0,16},{16,0},{1,17},{17,1},{2,18},{18,2},{3,19},{19,3},{4,20},{20... | collective-permute-start | bytes 1572872 | tf_op jit(solution)/shard_map/ppermute | solution.py:170
  172.9 10.4 %collective-permute-start.5 = (bf16[32,4,16,128]{3,2,1,0:T(8,128)(2,1)S(1)}, bf16[32,4,16,128]{3,2,1,0:T(8,128)(2,1)S(1)}, u32[]{:S(2)}, u32[]{:S(2)}) collective-permute-start(bf16[32,4,16,128]{3,2,1,0:T(8,128)(2,1)S(1)} %get-tuple-element.36), channel_id=1, source_target_pairs={{0,1},{1,0},{2,3},{3,2},{4,5},{5,4},{6,7},{7,6},{8,9},{9,8},{10,11... | collective-permute-start | bytes 1572872 | tf_op jit(solution)/shard_map/ppermute | solution.py:170
  181.3 3.4 %collective-permute-start.7 = (bf16[16,4,16,128]{3,2,1,0:T(8,128)(2,1)S(1)}, bf16[16,4,16,128]{3,2,1,0:T(8,128)(2,1)S(1)}, u32[]{:S(2)}, u32[]{:S(2)}) collective-permute-start(bf16[16,4,16,128]{3,2,1,0:T(8,128)(2,1)S(1)} %fusion.3), channel_id=1, source_target_pairs={{0,1},{1,0},{2,3},{3,2},{4,5},{5,4},{6,7},{7,6},{8,9},{9,8},{10,11... | collective-permute-start | bytes 786440 | tf_op jit(solution)/shard_map/ppermute | solution.py:170

commit v5 on v4

--- a/solution.py
+++ b/solution.py
@@ -22,47 +22,49 @@
     return slice(512 * half + 128 * z, 512 * half + 128 * (z + 1))
 
 
-def whole_left(both_ref, left_low_ref, left_high_ref, i_mask_ref, k_mask_ref):
+def place_rows(bit, halves, j_mask_ref, right_ref):
+    j_masks = j_mask_ref[...].reshape(4, 2, 2, 2, 16, 128)
+    mask = jnp.where(bit == 0, j_masks[:, :, 0], j_masks[:, :, 1])
+    for z in range(4):
+        for half in range(2):
+            rows = halves[half, :, z, :, :].reshape(4, 2, 2, 16, 128)
+            right_ref[:, :, bit, :, :, lanes(z, half)] = rows * mask
+
+
+def near_kernel(
+    place_ref, i_mask_ref, j_mask_ref, k_mask_ref, both_ref, left_low_ref, left_high_ref, near_ref, out_ref, right_ref
+):
     parts = [both_ref[:, z, 0:16, :].reshape(512, 128) for z in range(4)]
     for z in range(4):
         ends = [ref[:, z, :, :].reshape(256, 128) for ref in (left_low_ref, left_high_ref)]
         parts.append(jnp.concatenate(ends, axis=0))
     i_mask = i_mask_ref[...]
-    masks = [i_mask * k_mask_ref[0:1, 128 * n : 128 * (n + 1)] for n in range(8)]
-    return jnp.concatenate([part * mask for part, mask in zip(parts, masks)], axis=1)
+    for n, part in enumerate(parts):
+        cols = slice(128 * n, 128 * (n + 1))
+        out_ref[:, cols] = part * (i_mask * k_mask_ref[0:1, cols])
+    place_rows(place_ref[0], near_ref, j_mask_ref, right_ref)
+    zeros = jnp.zeros((4, 2, 2, 16, 1024), BF16)
+    right_ref[:, :, 1 - place_ref[0], :, :, :] = zeros
 
 
 def whole_grad(grad_ref):
     return jnp.concatenate([grad_ref[:, z, :, :].reshape(512, 128) for z in range(4)], axis=1)
 
 
-def product_kernel(
-    place_ref, i_mask_ref, j_mask_ref, k_mask_ref, both_ref, left_low_ref, left_high_ref, near_ref, far_0_ref, far_1_ref,
-    out_ref, right_ref,
-):
+def product_kernel(place_ref, j_mask_ref, left_ref, far_0_ref, far_1_ref, right_in_ref, out_ref, right_ref):
     pair, core = place_ref[0], place_ref[1]
-
-    j_masks = j_mask_ref[...].reshape(4, 2, 2, 2, 16, 128)
-
-    def place(bit, source):
-        mask = jnp.where(bit == 0, j_masks[:, :, 0], j_masks[:, :, 1])
-        for z in range(4):
-            for half in range(2):
-                rows = source[half, :, z, :, :].reshape(4, 2, 2, 16, 128)
-                right_ref[:, :, bit, :, :, lanes(z, half)] = rows * mask
-
-    place(pair, near_ref)
+    del right_in_ref
 
     @pl.when(core == 0)
     def _():
-        place(1 - pair, far_0_ref)
+        place_rows(1 - pair, far_0_ref, j_mask_ref, right_ref)
 
     @pl.when(core == 1)
     def _():
-        place(1 - pair, far_1_ref)
+        place_rows(1 - pair, far_1_ref, j_mask_ref, right_ref)
 
     product = lax.dot_general(
-        whole_left(both_ref, left_low_ref, left_high_ref, i_mask_ref, k_mask_ref),
+        left_ref[...],
         right_ref[...].reshape(512, 1024),
         (((1,), (1,)), ((), ())),
         preferred_element_type=F32,
@@ -72,12 +74,12 @@
 
 
 def right_grad_kernel(
-    place_ref, i_mask_ref, k_mask_ref, both_ref, left_low_ref, left_high_ref, grad_ref, send_ref, keep_ref
+    place_ref, left_ref, grad_ref, send_ref, keep_ref
 ):
     pair = place_ref[0]
     part = lax.dot_general(
         whole_grad(grad_ref),
-        whole_left(both_ref, left_low_ref, left_high_ref, i_mask_ref, k_mask_ref),
+        left_ref[...],
         (((0,), (0,)), ((), ())),
         preferred_element_type=F32,
     ).reshape(8, 2, 2, 16, 1024)
@@ -99,15 +101,13 @@
         send_ref[:, z, :, :] = part[:, lanes(z, 1)].reshape(32, 16, 128).astype(BF16)
 
 
-def gather_kernel(place_ref, left_keep_ref, left_got_ref, right_keep_ref, right_got_ref, right_other_ref, out_ref):
+def gather_kernel(place_ref, left_keep_ref, left_got_ref, right_keep_ref, right_got_ref, out_ref):
     core = place_ref[1]
     out_ref[:, :, :, :, 0:16, :] = (
         (left_keep_ref[...] + left_got_ref[...].astype(F32)).astype(BF16).reshape(4, 2, 4, 4, 16, 128)
     )
-    out_ref[:, core, :, :, 16:32, :] = (
-        (right_keep_ref[0] + right_got_ref[0].astype(F32)).astype(BF16).reshape(4, 4, 4, 16, 128)
-    )
-    out_ref[:, 1 - core, :, :, 16:32, :] = right_other_ref[...].reshape(4, 4, 4, 16, 128)
+    right = (right_keep_ref[0] + right_got_ref[0].astype(F32)).astype(BF16).reshape(4, 4, 4, 16, 128)
+    out_ref[:, core, :, :, 16:32, :] = right
 
 
 def norm_kernel(product_ref, scaled_ref, grad_ref):
@@ -153,7 +153,7 @@
     return jax.ShapeDtypeStruct(dims, dtype)
 
 
-def call(kernel, outs, operands, scratch=(), flops=0, scalars=1):
+def call(kernel, outs, operands, scratch=(), flops=0, scalars=1, aliases=None):
     moved = sum(o.size * o.dtype.itemsize for o in (*operands, *outs))
     return pl.pallas_call(
         kernel,
@@ -161,6 +161,7 @@
         in_specs=[smem()] * scalars + [vmem()] * (len(operands) - scalars),
         out_specs=[vmem()] * len(outs),
         scratch_shapes=scratch,
+        input_output_aliases=aliases or {},
         compiler_params=pltpu.CompilerParams(vmem_limit_bytes=VMEM_LIMIT),
         cost_estimate=pl.CostEstimate(flops=flops, bytes_accessed=moved, transcendentals=0),
     )(*operands)
@@ -214,7 +215,12 @@
     both = both.reshape(32, 4, 32, 128)
     left_low, left_high, near = lax.optimization_barrier((both[:16, :, :16, :], both[16:, :, :16, :], near))
     left_low, left_high = swap(left_low, "c"), swap(left_high, "c")
-    near_0, far_1, left_low, left_high = lax.optimization_barrier((near, far_1, left_low, left_high))
+    left_whole, right_near = call(
+        near_kernel,
+        [shape((512, 1024), BF16), shape((4, 2, 2, 2, 16, 1024), BF16)],
+        [place, i_mask, j_mask, k_mask, both, left_low, left_high, near],
+    )
+    near_0, far_1, left_whole, right_near = lax.optimization_barrier((near, far_1, left_whole, right_near))
     far_0 = swap_pair(near_0, 0)
 
     flops = 2 * 512 * 512 * 1024
@@ -222,7 +228,8 @@
     product, right_whole = call(
         product_kernel,
         [shape(blocks, BF16), shape((4, 2, 2, 2, 16, 1024), BF16)],
-        [place, i_mask, j_mask, k_mask, both, left_low, left_high, near, far_0, far_1],
+        [place, j_mask, left_whole, far_0, far_1, right_near],
+        aliases={5: 1},
         flops=flops,
     )
     product = to_owners(product.reshape(left.shape))
@@ -239,7 +246,7 @@
     right_send, right_keep = call(
         right_grad_kernel,
         [shape((2, *half), BF16), shape((2, *half), F32)],
-        [place, i_mask, k_mask, both, left_low, left_high, grad],
+        [place, left_whole, grad],
         flops=flops,
     )
     right_got = swap(right_send, PAIR)
@@ -247,11 +254,13 @@
     left_send, left_keep = call(
         left_grad_kernel, [shape(blocks, BF16), shape(blocks, F32)], [place, grad, right_whole], flops=flops
     )
+    right_other = swap(right_other, "c").reshape(4, 1, 4, 4, 16, 128)
     (sums,) = call(
         gather_kernel,
         [shape((4, 2, 4, 4, 32, 128), BF16)],
-        [place, left_keep, swap(left_send, "c"), right_keep, right_got, swap(right_other, "c")],
-    )
+        [place, left_keep, swap(left_send, "c"), right_keep, right_got],
+    )
+    sums = lax.dynamic_update_slice(sums, right_other, (0, 1 - core, 0, 0, 16, 0))
     home = to_owners(sums.reshape(128, 32, 128))
     return (home[:, :16] * tile_mask, home[:, 16:] * tile_mask)
 

time: 250 us -> 249 us (level)
  the two profiles are of different devices: /device:TPU:4 before, /device:TPU:64 now
where the time goes in v5:
time: 249 us
  blocking collectives  122 us (49%)
  waiting for transfers between devices  72.9 us (29%)
  starting transfers between devices  40.5 us (16%)
  Pallas kernels  6.49 us (3%)
  other arithmetic  3.91 us (2%)
    all_to_all x3, blocking collectives, to_owners(): return lax.all_to_all(x, OWNERS, split_axis=0, concat_axis=0, tiled=True)  122 us
    all_to_all x1, waiting for transfers between devices, to_owners(): return lax.all_to_all(x, OWNERS, split_axis=0, concat_axis=0, tiled=True)  53.3 us
    all_to_all x1, starting transfers between devices, to_owners(): return lax.all_to_all(x, OWNERS, split_axis=0, concat_axis=0, tiled=True)  20.1 us
    ppermute x6, starting transfers between devices, swap(): return lax.ppermute(x, axis, [(0, 1), (1, 0)])  17 us
    ppermute x2, waiting for transfers between devices, swap_pair(): return lax.ppermute(x, (PAIR, 'c'), [(at[0], at[1]), (at[1], at[0])])  10 us
    ppermute x6, waiting for transfers between devices, swap(): return lax.ppermute(x, axis, [(0, 1), (1, 0)])  9.55 us
    pallas_call x6, Pallas kernels, call(): pl.pallas_call(kernel, out_shape=outs, in_specs=[smem()] * scalars + [vme...  6.49 us
  transfers between devices with their start and end apart: 9, of which 6 were waited for; matrix products, arithmetic and copies ran while one was open for 1% of the time, Pallas kernels for 1%

profile of v5, /device:TPU:64, one launch (start us, length us, event | category | flops | bytes accessed | tf_op | source)
XLA Modules:
  0.0 248.5 jit_solution(17514539067162601646)
XLA Ops:
  0.6 2.3 pad_maximum_fusion
  2.9 20.1 %all-to-all-start = ((bf16[128,32,128]{2,1,0:T(8,128)(2,1)}), bf16[128,32,128]{2,1,0:T(8,128)(2,1)S(1)}, u32[]{:S(2)}, u32[]{:S(2)}) async-start(bf16[128,32,128]{2,1,0:T(8,128)(2,1)} %pad_maximum_fusion), calls=%async_computation | async-start | bytes 2097152 | tf_op jit(solution)/shard_map/all_to_all | solution.py:180
  24.8 53.3 %all-to-all-done = bf16[128,32,128]{2,1,0:T(8,128)(2,1)S(1)} async-done(((bf16[128,32,128]{2,1,0:T(8,128)(2,1)}), bf16[128,32,128]{2,1,0:T(8,128)(2,1)S(1)}, u32[]{:S(2)}, u32[]{:S(2)}) %all-to-all-start) | async-done | bytes 1048608 | tf_op jit(solution)/shard_map/all_to_all | solution.py:180
  78.5 1.9 collective-permute-start
  80.4 1.5 collective-permute-done
  82.7 5.7 %collective-permute-start.2 = (bf16[16,4,16,128]{3,2,1,0:T(8,128)(2,1)S(1)}, bf16[16,4,16,128]{3,2,1,0:T(8,128)(2,1)S(1)}, u32[]{:S(2)}, u32[]{:S(2)}) collective-permute-start(bf16[16,4,16,128]{3,2,1,0:T(8,128)(2,1)S(1)} %get-tuple-element.28), channel_id=1, source_target_pairs={{0,1},{1,0},{2,3},{3,2},{4,5},{5,4},{6,7},{7,6},{8,9},{9,8},{10,11... | collective-permute-start | bytes 786440 | tf_op jit(solution)/shard_map/ppermute | solution.py:171
  88.5 1.9 collective-permute-start.3
  90.5 1.4 collective-permute-done.3.left_high_ref
  91.9 1.1 shard_map.86
  93.0 2.7 %collective-permute-start.4 = (bf16[2,16,4,16,128]{4,3,2,1,0:T(8,128)(2,1)S(1)}, bf16[2,16,4,16,128]{4,3,2,1,0:T(8,128)(2,1)S(1)}, u32[]{:S(2)}, u32[]{:S(2)}) collective-permute-start(bf16[2,16,4,16,128]{4,3,2,1,0:T(8,128)(2,1)S(1)} %pad_maximum_fusion.1.near_ref), channel_id=1, source_target_pairs={{0,16},{16,0},{2,18},{18,2},{4,20},{20,4},{6,22},{22,6},{8,24},{24... | collective-permute-start | bytes 1572872 | tf_op jit(solution)/shard_map/ppermute | solution.py:176
  95.7 10.0 %collective-permute-done.4.far_0_ref = bf16[2,16,4,16,128]{4,3,2,1,0:T(8,128)(2,1)S(1)} collective-permute-done((bf16[2,16,4,16,128]{4,3,2,1,0:T(8,128)(2,1)S(1)}, bf16[2,16,4,16,128]{4,3,2,1,0:T(8,128)(2,1)S(1)}, u32[]{:S(2)}, u32[]{:S(2)}) %collective-permute-start.4) | collective-permute-done | bytes 524320 | tf_op jit(solution)/shard_map/ppermute | solution.py:176
  105.7 1.4 shard_map.87
  107.1 29.8 %all_to_all.20.product_ref = bf16[128,16,128]{2,1,0:T(8,128)(2,1)S(1)} all-to-all(bf16[128,16,128]{2,1,0:T(8,128)(2,1)S(1)} %bitcast.37), channel_id=1, replica_groups=mesh['zl'=4,'y'=4,'xh'=2,'xl'=2,'zh'=4,'c'=2] {'zl','y','xl','zh'}, dimensions={0} | all-to-all | bytes 1048576 | tf_op jit(solution)/shard_map/all_to_all | solution.py:180
  136.9 0.8 shard_map.88
  137.7 30.2 %all_to_all.21 = bf16[128,16,128]{2,1,0:T(8,128)(2,1)S(1)} all-to-all(bf16[128,16,128]{2,1,0:T(8,128)(2,1)S(1)} %shard_map.88), channel_id=1, replica_groups=mesh['zl'=4,'y'=4,'xh'=2,'xl'=2,'zh'=4,'c'=2] {'zl','y','xl','zh'}, dimensions={0} | all-to-all | bytes 1048576 | tf_op jit(solution)/shard_map/all_to_all | solution.py:180
  167.8 1.3 shard_map.90
  169.1 3.6 %collective-permute-start.6 = (bf16[2,16,4,16,128]{4,3,2,1,0:T(8,128)(2,1)S(1)}, bf16[2,16,4,16,128]{4,3,2,1,0:T(8,128)(2,1)S(1)}, u32[]{:S(2)}, u32[]{:S(2)}) collective-permute-start(bf16[2,16,4,16,128]{4,3,2,1,0:T(8,128)(2,1)S(1)} %get-tuple-element.42), channel_id=1, source_target_pairs={{0,16},{16,0},{1,17},{17,1},{2,18},{18,2},{3,19},{19,3},{4,20},{20... | collective-permute-start | bytes 1572872 | tf_op jit(solution)/shard_map/ppermute | solution.py:171
  172.7 1.3 shard_map.89
  174.0 1.9 collective-permute-start.5
  175.9 5.8 %collective-permute-done.6.right_got_ref = bf16[2,16,4,16,128]{4,3,2,1,0:T(8,128)(2,1)S(1)} collective-permute-done((bf16[2,16,4,16,128]{4,3,2,1,0:T(8,128)(2,1)S(1)}, bf16[2,16,4,16,128]{4,3,2,1,0:T(8,128)(2,1)S(1)}, u32[]{:S(2)}, u32[]{:S(2)}) %collective-permute-start.6) | collective-permute-done | bytes 524320 | tf_op jit(solution)/shard_map/ppermute | solution.py:171
  181.8 1.9 collective-permute-start.7
  184.4 0.8 collective-permute-done.7
  185.2 62.3 %all_to_all.22 = bf16[128,32,128]{2,1,0:T(8,128)(2,1)S(1)} all-to-all(bf16[128,32,128]{2,1,0:T(8,128)(2,1)S(1)} %bitcast.34), channel_id=1, replica_groups=mesh['zl'=4,'y'=4,'xh'=2,'xl'=2,'zh'=4,'c'=2] {'zl','y','xl','zh'}, dimensions={0} | all-to-all | bytes 2097152 | tf_op jit(solution)/shard_map/all_to_all | solution.py:180
  247.5 1.0 slice_multiply_fusion
  (38 shorter events, 3.7 us)
Async XLA Ops:
  0.6 22.9 %copy-start = (bf16[128,128]{1,0:T(8,128)(2,1)S(1)}, bf16[128,128]{1,0:T(8,128)(2,1)}, u32[]{:S(2)}) copy-start(bf16[128,128]{1,0:T(8,128)(2,1)} %param.12) | copy-start | bytes 98308
  2.9 20.1 %copy-start.3 = (s32[1024]{0:T(1024)S(1)}, s32[1024]{0:T(1024)}, u32[]{:S(2)}) copy-start(s32[1024]{0:T(1024)} %param.13) | copy-start | bytes 12292
  2.9 20.5 %copy-start.1 = (bf16[128,16,128]{2,1,0:T(8,128)(2,1)S(1)}, bf16[128,16,128]{2,1,0:T(8,128)(2,1)}, u32[]{:S(2)}) copy-start(bf16[128,16,128]{2,1,0:T(8,128)(2,1)} %param.10) | copy-start | bytes 1572868
  2.9 20.5 %copy-start.2 = (bf16[128,16,128]{2,1,0:T(8,128)(2,1)S(1)}, bf16[128,16,128]{2,1,0:T(8,128)(2,1)}, u32[]{:S(2)}) copy-start(bf16[128,16,128]{2,1,0:T(8,128)(2,1)} %param.9) | copy-start | bytes 1572868
  2.9 75.2 %all-to-all-start = ((bf16[128,32,128]{2,1,0:T(8,128)(2,1)}), bf16[128,32,128]{2,1,0:T(8,128)(2,1)S(1)}, u32[]{:S(2)}, u32[]{:S(2)}) async-start(bf16[128,32,128]{2,1,0:T(8,128)(2,1)} %pad_maximum_fusion), calls=%async_computation | async-start | bytes 2097152 | tf_op jit(solution)/shard_map/all_to_all | solution.py:180
  23.9 0.7 copy-start.4
  78.5 3.4 %collective-permute-start = (bf16[16,4,16,128]{3,2,1,0:T(8,128)(2,1)S(1)}, bf16[16,4,16,128]{3,2,1,0:T(8,128)(2,1)S(1)}, u32[]{:S(2)}, u32[]{:S(2)}) collective-permute-start(bf16[16,4,16,128]{3,2,1,0:T(8,128)(2,1)S(1)} %bitcast.41), channel_id=1, source_target_pairs={{0,1},{1,0},{2,3},{3,2},{4,5},{5,4},{6,7},{7,6},{8,9},{9,8},{10,11... | collective-permute-start | bytes 786440 | tf_op jit(solution)/shard_map/ppermute | solution.py:171
  82.0 11.0 %collective-permute-start.1 = (bf16[2,16,4,16,128]{4,3,2,1,0:T(8,128)(2,1)S(1)}, bf16[2,16,4,16,128]{4,3,2,1,0:T(8,128)(2,1)S(1)}, u32[]{:S(2)}, u32[]{:S(2)}) collective-permute-start(bf16[2,16,4,16,128]{4,3,2,1,0:T(8,128)(2,1)S(1)} %pad_maximum_fusion.1.near_ref), channel_id=1, source_target_pairs={{1,17},{17,1},{3,19},{19,3},{5,21},{21,5},{7,23},{23,7},{9,25},{25... | collective-permute-start | bytes 1572872 | tf_op jit(solution)/shard_map/ppermute | solution.py:176
  82.7 7.7 %collective-permute-start.2 = (bf16[16,4,16,128]{3,2,1,0:T(8,128)(2,1)S(1)}, bf16[16,4,16,128]{3,2,1,0:T(8,128)(2,1)S(1)}, u32[]{:S(2)}, u32[]{:S(2)}) collective-permute-start(bf16[16,4,16,128]{3,2,1,0:T(8,128)(2,1)S(1)} %get-tuple-element.28), channel_id=1, source_target_pairs={{0,1},{1,0},{2,3},{3,2},{4,5},{5,4},{6,7},{7,6},{8,9},{9,8},{10,11... | collective-permute-start | bytes 786440 | tf_op jit(solution)/shard_map/ppermute | solution.py:171
  88.5 3.4 %collective-permute-start.3 = (bf16[16,4,16,128]{3,2,1,0:T(8,128)(2,1)S(1)}, bf16[16,4,16,128]{3,2,1,0:T(8,128)(2,1)S(1)}, u32[]{:S(2)}, u32[]{:S(2)}) collective-permute-start(bf16[16,4,16,128]{3,2,1,0:T(8,128)(2,1)S(1)} %get-tuple-element.29), channel_id=1, source_target_pairs={{0,1},{1,0},{2,3},{3,2},{4,5},{5,4},{6,7},{7,6},{8,9},{9,8},{10,11... | collective-permute-start | bytes 786440 | tf_op jit(solution)/shard_map/ppermute | solution.py:171
  93.0 12.7 %collective-permute-start.4 = (bf16[2,16,4,16,128]{4,3,2,1,0:T(8,128)(2,1)S(1)}, bf16[2,16,4,16,128]{4,3,2,1,0:T(8,128)(2,1)S(1)}, u32[]{:S(2)}, u32[]{:S(2)}) collective-permute-start(bf16[2,16,4,16,128]{4,3,2,1,0:T(8,128)(2,1)S(1)} %pad_maximum_fusion.1.near_ref), channel_id=1, source_target_pairs={{0,16},{16,0},{2,18},{18,2},{4,20},{20,4},{6,22},{22,6},{8,24},{24... | collective-permute-start | bytes 1572872 | tf_op jit(solution)/shard_map/ppermute | solution.py:176
  169.1 12.6 %collective-permute-start.6 = (bf16[2,16,4,16,128]{4,3,2,1,0:T(8,128)(2,1)S(1)}, bf16[2,16,4,16,128]{4,3,2,1,0:T(8,128)(2,1)S(1)}, u32[]{:S(2)}, u32[]{:S(2)}) collective-permute-start(bf16[2,16,4,16,128]{4,3,2,1,0:T(8,128)(2,1)S(1)} %get-tuple-element.42), channel_id=1, source_target_pairs={{0,16},{16,0},{1,17},{17,1},{2,18},{18,2},{3,19},{19,3},{4,20},{20... | collective-permute-start | bytes 1572872 | tf_op jit(solution)/shard_map/ppermute | solution.py:171
  174.0 9.7 %collective-permute-start.5 = (bf16[32,4,16,128]{3,2,1,0:T(8,128)(2,1)S(1)}, bf16[32,4,16,128]{3,2,1,0:T(8,128)(2,1)S(1)}, u32[]{:S(2)}, u32[]{:S(2)}) collective-permute-start(bf16[32,4,16,128]{3,2,1,0:T(8,128)(2,1)S(1)} %get-tuple-element.40), channel_id=1, source_target_pairs={{0,1},{1,0},{2,3},{3,2},{4,5},{5,4},{6,7},{7,6},{8,9},{9,8},{10,11... | collective-permute-start | bytes 1572872 | tf_op jit(solution)/shard_map/ppermute | solution.py:171
  181.8 3.4 %collective-permute-start.7 = (bf16[16,4,16,128]{3,2,1,0:T(8,128)(2,1)S(1)}, bf16[16,4,16,128]{3,2,1,0:T(8,128)(2,1)S(1)}, u32[]{:S(2)}, u32[]{:S(2)}) collective-permute-start(bf16[16,4,16,128]{3,2,1,0:T(8,128)(2,1)S(1)} %fusion.3), channel_id=1, source_target_pairs={{0,1},{1,0},{2,3},{3,2},{4,5},{5,4},{6,7},{7,6},{8,9},{9,8},{10,11... | collective-permute-start | bytes 786440 | tf_op jit(solution)/shard_map/ppermute | solution.py:171

commit v6 on v5

--- a/solution.py
+++ b/solution.py
@@ -38,10 +38,11 @@
     for z in range(4):
         ends = [ref[:, z, :, :].reshape(256, 128) for ref in (left_low_ref, left_high_ref)]
         parts.append(jnp.concatenate(ends, axis=0))
-    i_mask = i_mask_ref[...]
+    i_mask = i_mask_ref[...].reshape(32, 16, 128)
     for n, part in enumerate(parts):
         cols = slice(128 * n, 128 * (n + 1))
-        out_ref[:, cols] = part * (i_mask * k_mask_ref[0:1, cols])
+        mask = (i_mask * k_mask_ref[:, cols][None]).reshape(512, 128)
+        out_ref[:, cols] = part * mask
     place_rows(place_ref[0], near_ref, j_mask_ref, right_ref)
     zeros = jnp.zeros((4, 2, 2, 16, 1024), BF16)
     right_ref[:, :, 1 - place_ref[0], :, :, :] = zeros

time: 249 us -> 249 us (level)
  no operation moved by 1% of the time
where the time goes in v6:
time: 249 us
  blocking collectives  122 us (49%)
  waiting for transfers between devices  72.9 us (29%)
  starting transfers between devices  40.5 us (16%)
  Pallas kernels  6.48 us (3%)
  other arithmetic  3.91 us (2%)
    all_to_all x3, blocking collectives, to_owners(): return lax.all_to_all(x, OWNERS, split_axis=0, concat_axis=0, tiled=True)  122 us
    all_to_all x1, waiting for transfers between devices, to_owners(): return lax.all_to_all(x, OWNERS, split_axis=0, concat_axis=0, tiled=True)  53.3 us
    all_to_all x1, starting transfers between devices, to_owners(): return lax.all_to_all(x, OWNERS, split_axis=0, concat_axis=0, tiled=True)  20.1 us
    ppermute x6, starting transfers between devices, swap(): return lax.ppermute(x, axis, [(0, 1), (1, 0)])  17 us
    ppermute x2, waiting for transfers between devices, swap_pair(): return lax.ppermute(x, (PAIR, 'c'), [(at[0], at[1]), (at[1], at[0])])  10 us
    ppermute x6, waiting for transfers between devices, swap(): return lax.ppermute(x, axis, [(0, 1), (1, 0)])  9.54 us
    pallas_call x6, Pallas kernels, call(): pl.pallas_call(kernel, out_shape=outs, in_specs=[smem()] * scalars + [vme...  6.48 us
  transfers between devices with their start and end apart: 9, of which 6 were waited for; matrix products, arithmetic and copies ran while one was open for 1% of the time, Pallas kernels for 1%

profile of v6, /device:TPU:64, one launch (start us, length us, event | category | flops | bytes accessed | tf_op | source)
XLA Modules:
  0.0 248.5 jit_solution(13113803597788572949)
XLA Ops:
  0.6 2.3 pad_maximum_fusion
  2.9 20.1 %all-to-all-start = ((bf16[128,32,128]{2,1,0:T(8,128)(2,1)}), bf16[128,32,128]{2,1,0:T(8,128)(2,1)S(1)}, u32[]{:S(2)}, u32[]{:S(2)}) async-start(bf16[128,32,128]{2,1,0:T(8,128)(2,1)} %pad_maximum_fusion), calls=%async_computation | async-start | bytes 2097152 | tf_op jit(solution)/shard_map/all_to_all | solution.py:181
  24.8 53.3 %all-to-all-done = bf16[128,32,128]{2,1,0:T(8,128)(2,1)S(1)} async-done(((bf16[128,32,128]{2,1,0:T(8,128)(2,1)}), bf16[128,32,128]{2,1,0:T(8,128)(2,1)S(1)}, u32[]{:S(2)}, u32[]{:S(2)}) %all-to-all-start) | async-done | bytes 1048608 | tf_op jit(solution)/shard_map/all_to_all | solution.py:181
  78.5 1.9 collective-permute-start
  80.4 1.5 collective-permute-done
  82.7 5.7 %collective-permute-start.2 = (bf16[16,4,16,128]{3,2,1,0:T(8,128)(2,1)S(1)}, bf16[16,4,16,128]{3,2,1,0:T(8,128)(2,1)S(1)}, u32[]{:S(2)}, u32[]{:S(2)}) collective-permute-start(bf16[16,4,16,128]{3,2,1,0:T(8,128)(2,1)S(1)} %get-tuple-element.28), channel_id=1, source_target_pairs={{0,1},{1,0},{2,3},{3,2},{4,5},{5,4},{6,7},{7,6},{8,9},{9,8},{10,11... | collective-permute-start | bytes 786440 | tf_op jit(solution)/shard_map/ppermute | solution.py:172
  88.5 1.9 collective-permute-start.3
  90.5 1.4 collective-permute-done.3.left_high_ref
  91.9 1.0 shard_map.86
  93.0 2.7 %collective-permute-start.4 = (bf16[2,16,4,16,128]{4,3,2,1,0:T(8,128)(2,1)S(1)}, bf16[2,16,4,16,128]{4,3,2,1,0:T(8,128)(2,1)S(1)}, u32[]{:S(2)}, u32[]{:S(2)}) collective-permute-start(bf16[2,16,4,16,128]{4,3,2,1,0:T(8,128)(2,1)S(1)} %pad_maximum_fusion.1.near_ref), channel_id=1, source_target_pairs={{0,16},{16,0},{2,18},{18,2},{4,20},{20,4},{6,22},{22,6},{8,24},{24... | collective-permute-start | bytes 1572872 | tf_op jit(solution)/shard_map/ppermute | solution.py:177
  95.7 10.0 %collective-permute-done.4.far_0_ref = bf16[2,16,4,16,128]{4,3,2,1,0:T(8,128)(2,1)S(1)} collective-permute-done((bf16[2,16,4,16,128]{4,3,2,1,0:T(8,128)(2,1)S(1)}, bf16[2,16,4,16,128]{4,3,2,1,0:T(8,128)(2,1)S(1)}, u32[]{:S(2)}, u32[]{:S(2)}) %collective-permute-start.4) | collective-permute-done | bytes 524320 | tf_op jit(solution)/shard_map/ppermute | solution.py:177
  105.7 1.4 shard_map.87
  107.1 29.7 %all_to_all.20.product_ref = bf16[128,16,128]{2,1,0:T(8,128)(2,1)S(1)} all-to-all(bf16[128,16,128]{2,1,0:T(8,128)(2,1)S(1)} %bitcast.37), channel_id=1, replica_groups=mesh['zl'=4,'y'=4,'xh'=2,'xl'=2,'zh'=4,'c'=2] {'zl','y','xl','zh'}, dimensions={0} | all-to-all | bytes 1048576 | tf_op jit(solution)/shard_map/all_to_all | solution.py:181
  136.8 0.8 shard_map.88
  137.6 30.2 %all_to_all.21 = bf16[128,16,128]{2,1,0:T(8,128)(2,1)S(1)} all-to-all(bf16[128,16,128]{2,1,0:T(8,128)(2,1)S(1)} %shard_map.88), channel_id=1, replica_groups=mesh['zl'=4,'y'=4,'xh'=2,'xl'=2,'zh'=4,'c'=2] {'zl','y','xl','zh'}, dimensions={0} | all-to-all | bytes 1048576 | tf_op jit(solution)/shard_map/all_to_all | solution.py:181
  167.8 1.3 shard_map.90
  169.1 3.6 %collective-permute-start.6 = (bf16[2,16,4,16,128]{4,3,2,1,0:T(8,128)(2,1)S(1)}, bf16[2,16,4,16,128]{4,3,2,1,0:T(8,128)(2,1)S(1)}, u32[]{:S(2)}, u32[]{:S(2)}) collective-permute-start(bf16[2,16,4,16,128]{4,3,2,1,0:T(8,128)(2,1)S(1)} %get-tuple-element.42), channel_id=1, source_target_pairs={{0,16},{16,0},{1,17},{17,1},{2,18},{18,2},{3,19},{19,3},{4,20},{20... | collective-permute-start | bytes 1572872 | tf_op jit(solution)/shard_map/ppermute | solution.py:172
  172.7 1.3 shard_map.89
  174.0 1.9 collective-permute-start.5
  175.9 5.8 %collective-permute-done.6.right_got_ref = bf16[2,16,4,16,128]{4,3,2,1,0:T(8,128)(2,1)S(1)} collective-permute-done((bf16[2,16,4,16,128]{4,3,2,1,0:T(8,128)(2,1)S(1)}, bf16[2,16,4,16,128]{4,3,2,1,0:T(8,128)(2,1)S(1)}, u32[]{:S(2)}, u32[]{:S(2)}) %collective-permute-start.6) | collective-permute-done | bytes 524320 | tf_op jit(solution)/shard_map/ppermute | solution.py:172
  181.8 1.9 collective-permute-start.7
  184.4 0.8 collective-permute-done.7
  185.2 62.3 %all_to_all.22 = bf16[128,32,128]{2,1,0:T(8,128)(2,1)S(1)} all-to-all(bf16[128,32,128]{2,1,0:T(8,128)(2,1)S(1)} %bitcast.34), channel_id=1, replica_groups=mesh['zl'=4,'y'=4,'xh'=2,'xl'=2,'zh'=4,'c'=2] {'zl','y','xl','zh'}, dimensions={0} | all-to-all | bytes 2097152 | tf_op jit(solution)/shard_map/all_to_all | solution.py:181
  247.5 1.0 slice_multiply_fusion
  (38 shorter events, 3.7 us)
Async XLA Ops:
  0.6 22.9 %copy-start = (bf16[128,128]{1,0:T(8,128)(2,1)S(1)}, bf16[128,128]{1,0:T(8,128)(2,1)}, u32[]{:S(2)}) copy-start(bf16[128,128]{1,0:T(8,128)(2,1)} %param.12) | copy-start | bytes 98308
  2.9 20.1 %copy-start.3 = (s32[1024]{0:T(1024)S(1)}, s32[1024]{0:T(1024)}, u32[]{:S(2)}) copy-start(s32[1024]{0:T(1024)} %param.13) | copy-start | bytes 12292
  2.9 20.5 %copy-start.1 = (bf16[128,16,128]{2,1,0:T(8,128)(2,1)S(1)}, bf16[128,16,128]{2,1,0:T(8,128)(2,1)}, u32[]{:S(2)}) copy-start(bf16[128,16,128]{2,1,0:T(8,128)(2,1)} %param.10) | copy-start | bytes 1572868
  2.9 20.5 %copy-start.2 = (bf16[128,16,128]{2,1,0:T(8,128)(2,1)S(1)}, bf16[128,16,128]{2,1,0:T(8,128)(2,1)}, u32[]{:S(2)}) copy-start(bf16[128,16,128]{2,1,0:T(8,128)(2,1)} %param.9) | copy-start | bytes 1572868
  2.9 75.2 %all-to-all-start = ((bf16[128,32,128]{2,1,0:T(8,128)(2,1)}), bf16[128,32,128]{2,1,0:T(8,128)(2,1)S(1)}, u32[]{:S(2)}, u32[]{:S(2)}) async-start(bf16[128,32,128]{2,1,0:T(8,128)(2,1)} %pad_maximum_fusion), calls=%async_computation | async-start | bytes 2097152 | tf_op jit(solution)/shard_map/all_to_all | solution.py:181
  23.9 0.7 copy-start.4
  78.5 3.4 %collective-permute-start = (bf16[16,4,16,128]{3,2,1,0:T(8,128)(2,1)S(1)}, bf16[16,4,16,128]{3,2,1,0:T(8,128)(2,1)S(1)}, u32[]{:S(2)}, u32[]{:S(2)}) collective-permute-start(bf16[16,4,16,128]{3,2,1,0:T(8,128)(2,1)S(1)} %bitcast.41), channel_id=1, source_target_pairs={{0,1},{1,0},{2,3},{3,2},{4,5},{5,4},{6,7},{7,6},{8,9},{9,8},{10,11... | collective-permute-start | bytes 786440 | tf_op jit(solution)/shard_map/ppermute | solution.py:172
  82.0 11.0 %collective-permute-start.1 = (bf16[2,16,4,16,128]{4,3,2,1,0:T(8,128)(2,1)S(1)}, bf16[2,16,4,16,128]{4,3,2,1,0:T(8,128)(2,1)S(1)}, u32[]{:S(2)}, u32[]{:S(2)}) collective-permute-start(bf16[2,16,4,16,128]{4,3,2,1,0:T(8,128)(2,1)S(1)} %pad_maximum_fusion.1.near_ref), channel_id=1, source_target_pairs={{1,17},{17,1},{3,19},{19,3},{5,21},{21,5},{7,23},{23,7},{9,25},{25... | collective-permute-start | bytes 1572872 | tf_op jit(solution)/shard_map/ppermute | solution.py:177
  82.7 7.7 %collective-permute-start.2 = (bf16[16,4,16,128]{3,2,1,0:T(8,128)(2,1)S(1)}, bf16[16,4,16,128]{3,2,1,0:T(8,128)(2,1)S(1)}, u32[]{:S(2)}, u32[]{:S(2)}) collective-permute-start(bf16[16,4,16,128]{3,2,1,0:T(8,128)(2,1)S(1)} %get-tuple-element.28), channel_id=1, source_target_pairs={{0,1},{1,0},{2,3},{3,2},{4,5},{5,4},{6,7},{7,6},{8,9},{9,8},{10,11... | collective-permute-start | bytes 786440 | tf_op jit(solution)/shard_map/ppermute | solution.py:172
  88.5 3.4 %collective-permute-start.3 = (bf16[16,4,16,128]{3,2,1,0:T(8,128)(2,1)S(1)}, bf16[16,4,16,128]{3,2,1,0:T(8,128)(2,1)S(1)}, u32[]{:S(2)}, u32[]{:S(2)}) collective-permute-start(bf16[16,4,16,128]{3,2,1,0:T(8,128)(2,1)S(1)} %get-tuple-element.29), channel_id=1, source_target_pairs={{0,1},{1,0},{2,3},{3,2},{4,5},{5,4},{6,7},{7,6},{8,9},{9,8},{10,11... | collective-permute-start | bytes 786440 | tf_op jit(solution)/shard_map/ppermute | solution.py:172
  93.0 12.7 %collective-permute-start.4 = (bf16[2,16,4,16,128]{4,3,2,1,0:T(8,128)(2,1)S(1)}, bf16[2,16,4,16,128]{4,3,2,1,0:T(8,128)(2,1)S(1)}, u32[]{:S(2)}, u32[]{:S(2)}) collective-permute-start(bf16[2,16,4,16,128]{4,3,2,1,0:T(8,128)(2,1)S(1)} %pad_maximum_fusion.1.near_ref), channel_id=1, source_target_pairs={{0,16},{16,0},{2,18},{18,2},{4,20},{20,4},{6,22},{22,6},{8,24},{24... | collective-permute-start | bytes 1572872 | tf_op jit(solution)/shard_map/ppermute | solution.py:177
  169.1 12.6 %collective-permute-start.6 = (bf16[2,16,4,16,128]{4,3,2,1,0:T(8,128)(2,1)S(1)}, bf16[2,16,4,16,128]{4,3,2,1,0:T(8,128)(2,1)S(1)}, u32[]{:S(2)}, u32[]{:S(2)}) collective-permute-start(bf16[2,16,4,16,128]{4,3,2,1,0:T(8,128)(2,1)S(1)} %get-tuple-element.42), channel_id=1, source_target_pairs={{0,16},{16,0},{1,17},{17,1},{2,18},{18,2},{3,19},{19,3},{4,20},{20... | collective-permute-start | bytes 1572872 | tf_op jit(solution)/shard_map/ppermute | solution.py:172
  174.0 9.7 %collective-permute-start.5 = (bf16[32,4,16,128]{3,2,1,0:T(8,128)(2,1)S(1)}, bf16[32,4,16,128]{3,2,1,0:T(8,128)(2,1)S(1)}, u32[]{:S(2)}, u32[]{:S(2)}) collective-permute-start(bf16[32,4,16,128]{3,2,1,0:T(8,128)(2,1)S(1)} %get-tuple-element.40), channel_id=1, source_target_pairs={{0,1},{1,0},{2,3},{3,2},{4,5},{5,4},{6,7},{7,6},{8,9},{9,8},{10,11... | collective-permute-start | bytes 1572872 | tf_op jit(solution)/shard_map/ppermute | solution.py:172
  181.8 3.4 %collective-permute-start.7 = (bf16[16,4,16,128]{3,2,1,0:T(8,128)(2,1)S(1)}, bf16[16,4,16,128]{3,2,1,0:T(8,128)(2,1)S(1)}, u32[]{:S(2)}, u32[]{:S(2)}) collective-permute-start(bf16[16,4,16,128]{3,2,1,0:T(8,128)(2,1)S(1)} %fusion.3), channel_id=1, source_target_pairs={{0,1},{1,0},{2,3},{3,2},{4,5},{5,4},{6,7},{7,6},{8,9},{9,8},{10,11... | collective-permute-start | bytes 786440 | tf_op jit(solution)/shard_map/ppermute | solution.py:172

commit v7 on v6

--- a/solution.py
+++ b/solution.py
@@ -100,15 +100,6 @@
     for z in range(4):
         keep_ref[:, z, :, :] = part[:, lanes(z)].reshape(32, 16, 128)
         send_ref[:, z, :, :] = part[:, lanes(z, 1)].reshape(32, 16, 128).astype(BF16)
-
-
-def gather_kernel(place_ref, left_keep_ref, left_got_ref, right_keep_ref, right_got_ref, out_ref):
-    core = place_ref[1]
-    out_ref[:, :, :, :, 0:16, :] = (
-        (left_keep_ref[...] + left_got_ref[...].astype(F32)).astype(BF16).reshape(4, 2, 4, 4, 16, 128)
-    )
-    right = (right_keep_ref[0] + right_got_ref[0].astype(F32)).astype(BF16).reshape(4, 4, 4, 16, 128)
-    out_ref[:, core, :, :, 16:32, :] = right
 
 
 def norm_kernel(product_ref, scaled_ref, grad_ref):
@@ -250,20 +241,23 @@
         [place, left_whole, grad],
         flops=flops,
     )
-    right_got = swap(right_send, PAIR)
-    right_other = (right_keep[1] + right_got[1].astype(F32)).astype(BF16)
+    got_1 = swap_pair(right_send, 1)
     left_send, left_keep = call(
         left_grad_kernel, [shape(blocks, BF16), shape(blocks, F32)], [place, grad, right_whole], flops=flops
     )
-    right_other = swap(right_other, "c").reshape(4, 1, 4, 4, 16, 128)
-    (sums,) = call(
-        gather_kernel,
-        [shape((4, 2, 4, 4, 32, 128), BF16)],
-        [place, left_keep, swap(left_send, "c"), right_keep, right_got],
-    )
-    sums = lax.dynamic_update_slice(sums, right_other, (0, 1 - core, 0, 0, 16, 0))
-    home = to_owners(sums.reshape(128, 32, 128))
-    return (home[:, :16] * tile_mask, home[:, 16:] * tile_mask)
+    left_got = swap(left_send, "c")
+    right_send, got_1 = lax.optimization_barrier((right_send, got_1))
+    got_0 = swap_pair(right_send, 0)
+    left_sum = (left_keep + left_got.astype(F32)).astype(BF16)
+    left_sum, got_0 = lax.optimization_barrier((left_sum, got_0))
+    left_home = to_owners(left_sum.reshape(left.shape))
+    total = (right_keep + got_1.astype(F32) + got_0.astype(F32)).astype(BF16).reshape(2, 4, 4, 4, 16, 128)
+    across = swap(total[1], "c")
+    right_sum = jnp.where(
+        core == 0, jnp.stack([total[0], across], axis=1), jnp.stack([across, total[0]], axis=1)
+    )
+    right_home = to_owners(right_sum.reshape(left.shape))
+    return (left_home * tile_mask, right_home * tile_mask)
 
 
 def solution(mesh):

time: 249 us -> 248 us (level)
  the two profiles are of different devices: /device:TPU:64 before, /device:TPU:8 now
where the time goes in v7:
time: 248 us
  waiting for transfers between devices  93.4 us (38%)
  blocking collectives  89.9 us (36%)
  starting transfers between devices  50.7 us (20%)
  Pallas kernels  5.8 us (2%)
  other arithmetic  5.13 us (2%)
    all_to_all x3, blocking collectives, to_owners(): return lax.all_to_all(x, OWNERS, split_axis=0, concat_axis=0, tiled=True)  89.9 us
    all_to_all x2, waiting for transfers between devices, to_owners(): return lax.all_to_all(x, OWNERS, split_axis=0, concat_axis=0, tiled=True)  71.8 us
    all_to_all x2, starting transfers between devices, to_owners(): return lax.all_to_all(x, OWNERS, split_axis=0, concat_axis=0, tiled=True)  28.9 us
    ppermute x4, waiting for transfers between devices, swap_pair(): return lax.ppermute(x, (PAIR, 'c'), [(at[0], at[1]), (at[1], at[0])])  17.2 us
    ppermute x5, starting transfers between devices, swap(): return lax.ppermute(x, axis, [(0, 1), (1, 0)])  13.4 us
    ppermute x4, starting transfers between devices, swap_pair(): return lax.ppermute(x, (PAIR, 'c'), [(at[0], at[1]), (at[1], at[0])])  8.38 us
    pallas_call x5, Pallas kernels, call(): pl.pallas_call(kernel, out_shape=outs, in_specs=[smem()] * scalars + [vme...  5.8 us
  transfers between devices with their start and end apart: 11, of which 7 were waited for; matrix products, arithmetic and copies ran while one was open for 1% of the time, Pallas kernels for 1%

profile of v7, /device:TPU:8, one launch (start us, length us, event | category | flops | bytes accessed | tf_op | source)
XLA Modules:
  0.0 247.6 jit_solution(8142591660554903598)
XLA Ops:
  0.6 2.3 pad_maximum_fusion
  2.9 20.6 %all-to-all-start = ((bf16[128,32,128]{2,1,0:T(8,128)(2,1)}), bf16[128,32,128]{2,1,0:T(8,128)(2,1)S(1)}, u32[]{:S(2)}, u32[]{:S(2)}) async-start(bf16[128,32,128]{2,1,0:T(8,128)(2,1)} %pad_maximum_fusion), calls=%async_computation | async-start | bytes 2097152 | tf_op jit(solution)/shard_map/all_to_all | solution.py:172
  25.3 52.5 %all-to-all-done = bf16[128,32,128]{2,1,0:T(8,128)(2,1)S(1)} async-done(((bf16[128,32,128]{2,1,0:T(8,128)(2,1)}), bf16[128,32,128]{2,1,0:T(8,128)(2,1)S(1)}, u32[]{:S(2)}, u32[]{:S(2)}) %all-to-all-start) | async-done | bytes 1048608 | tf_op jit(solution)/shard_map/all_to_all | solution.py:172
  78.1 1.9 collective-permute-start
  80.1 1.5 collective-permute-done
  82.4 5.7 %collective-permute-start.2 = (bf16[16,4,16,128]{3,2,1,0:T(8,128)(2,1)S(1)}, bf16[16,4,16,128]{3,2,1,0:T(8,128)(2,1)S(1)}, u32[]{:S(2)}, u32[]{:S(2)}) collective-permute-start(bf16[16,4,16,128]{3,2,1,0:T(8,128)(2,1)S(1)} %get-tuple-element.32), channel_id=1, source_target_pairs={{0,1},{1,0},{2,3},{3,2},{4,5},{5,4},{6,7},{7,6},{8,9},{9,8},{10,11... | collective-permute-start | bytes 786440 | tf_op jit(solution)/shard_map/ppermute | solution.py:163
  88.1 1.9 collective-permute-start.3
  90.1 1.4 collective-permute-done.3.left_high_ref
  91.5 1.0 shard_map.86
  92.6 2.7 %collective-permute-start.4 = (bf16[2,16,4,16,128]{4,3,2,1,0:T(8,128)(2,1)S(1)}, bf16[2,16,4,16,128]{4,3,2,1,0:T(8,128)(2,1)S(1)}, u32[]{:S(2)}, u32[]{:S(2)}) collective-permute-start(bf16[2,16,4,16,128]{4,3,2,1,0:T(8,128)(2,1)S(1)} %pad_maximum_fusion.1.near_ref), channel_id=1, source_target_pairs={{0,16},{16,0},{2,18},{18,2},{4,20},{20,4},{6,22},{22,6},{8,24},{24... | collective-permute-start | bytes 1572872 | tf_op jit(solution)/shard_map/ppermute | solution.py:168
  95.3 9.9 %collective-permute-done.4.far_0_ref = bf16[2,16,4,16,128]{4,3,2,1,0:T(8,128)(2,1)S(1)} collective-permute-done((bf16[2,16,4,16,128]{4,3,2,1,0:T(8,128)(2,1)S(1)}, bf16[2,16,4,16,128]{4,3,2,1,0:T(8,128)(2,1)S(1)}, u32[]{:S(2)}, u32[]{:S(2)}) %collective-permute-start.4) | collective-permute-done | bytes 524320 | tf_op jit(solution)/shard_map/ppermute | solution.py:168
  105.2 1.4 shard_map.87
  106.6 30.1 %all_to_all.25.product_ref = bf16[128,16,128]{2,1,0:T(8,128)(2,1)S(1)} all-to-all(bf16[128,16,128]{2,1,0:T(8,128)(2,1)S(1)} %bitcast.35), channel_id=1, replica_groups=mesh['zl'=4,'y'=4,'xh'=2,'xl'=2,'zh'=4,'c'=2] {'zl','y','xl','zh'}, dimensions={0} | all-to-all | bytes 1048576 | tf_op jit(solution)/shard_map/all_to_all | solution.py:172
  137.5 29.5 %all_to_all.26 = bf16[128,16,128]{2,1,0:T(8,128)(2,1)S(1)} all-to-all(bf16[128,16,128]{2,1,0:T(8,128)(2,1)S(1)} %shard_map.88), channel_id=1, replica_groups=mesh['zl'=4,'y'=4,'xh'=2,'xl'=2,'zh'=4,'c'=2] {'zl','y','xl','zh'}, dimensions={0} | all-to-all | bytes 1048576 | tf_op jit(solution)/shard_map/all_to_all | solution.py:172
  167.1 1.3 shard_map.90
  169.1 1.3 shard_map.89
  170.3 1.9 collective-permute-start.5
  172.3 4.3 %collective-permute-start.7 = (bf16[2,16,4,16,128]{4,3,2,1,0:T(8,128)(2,1)S(1)}, bf16[2,16,4,16,128]{4,3,2,1,0:T(8,128)(2,1)S(1)}, u32[]{:S(2)}, u32[]{:S(2)}) collective-permute-start(bf16[2,16,4,16,128]{4,3,2,1,0:T(8,128)(2,1)S(1)} %get-tuple-element.46), channel_id=1, source_target_pairs={{0,16},{16,0},{2,18},{18,2},{4,20},{20,4},{6,22},{22,6},{8,24},{24... | collective-permute-start | bytes 1572872 | tf_op jit(solution)/shard_map/ppermute | solution.py:168
  177.5 7.3 %collective-permute-done.7 = bf16[2,16,4,16,128]{4,3,2,1,0:T(8,128)(2,1)S(1)} collective-permute-done((bf16[2,16,4,16,128]{4,3,2,1,0:T(8,128)(2,1)S(1)}, bf16[2,16,4,16,128]{4,3,2,1,0:T(8,128)(2,1)S(1)}, u32[]{:S(2)}, u32[]{:S(2)}) %collective-permute-start.7) | collective-permute-done | bytes 524320 | tf_op jit(solution)/shard_map/ppermute | solution.py:168
  184.9 8.3 %all-to-all-start.3 = ((bf16[128,16,128]{2,1,0:T(8,128)(2,1)}), bf16[128,16,128]{2,1,0:T(8,128)(2,1)S(1)}, u32[]{:S(2)}, u32[]{:S(2)}) async-start(bf16[128,16,128]{2,1,0:T(8,128)(2,1)} %bitcast.12), calls=%async_computation.3 | async-start | bytes 1048576 | tf_op jit(solution)/shard_map/all_to_all | solution.py:172
  193.5 1.9 collective-permute-start.8
  195.4 1.5 collective-permute-done.8
  197.0 19.3 %all-to-all-done.3 = bf16[128,16,128]{2,1,0:T(8,128)(2,1)S(1)} async-done(((bf16[128,16,128]{2,1,0:T(8,128)(2,1)}), bf16[128,16,128]{2,1,0:T(8,128)(2,1)S(1)}, u32[]{:S(2)}, u32[]{:S(2)}) %all-to-all-start.3) | async-done | bytes 524320 | tf_op jit(solution)/shard_map/all_to_all | solution.py:172
  216.3 30.2 %all_to_all.27 = bf16[128,16,128]{2,1,0:T(8,128)(2,1)S(1)} all-to-all(bf16[128,16,128]{2,1,0:T(8,128)(2,1)S(1)} %bitcast.38), channel_id=1, replica_groups=mesh['zl'=4,'y'=4,'xh'=2,'xl'=2,'zh'=4,'c'=2] {'zl','y','xl','zh'}, dimensions={0} | all-to-all | bytes 1048576 | tf_op jit(solution)/shard_map/all_to_all | solution.py:172
  (44 shorter events, 6.8 us)
Async XLA Ops:
  0.6 23.4 %copy-start = (bf16[128,128]{1,0:T(8,128)(2,1)S(1)}, bf16[128,128]{1,0:T(8,128)(2,1)}, u32[]{:S(2)}) copy-start(bf16[128,128]{1,0:T(8,128)(2,1)} %param.12) | copy-start | bytes 98308
  2.9 20.6 %copy-start.3 = (s32[1024]{0:T(1024)S(1)}, s32[1024]{0:T(1024)}, u32[]{:S(2)}) copy-start(s32[1024]{0:T(1024)} %param.13) | copy-start | bytes 12292
  2.9 21.0 %copy-start.1 = (bf16[128,16,128]{2,1,0:T(8,128)(2,1)S(1)}, bf16[128,16,128]{2,1,0:T(8,128)(2,1)}, u32[]{:S(2)}) copy-start(bf16[128,16,128]{2,1,0:T(8,128)(2,1)} %param.10) | copy-start | bytes 1572868
  2.9 21.0 %copy-start.2 = (bf16[128,16,128]{2,1,0:T(8,128)(2,1)S(1)}, bf16[128,16,128]{2,1,0:T(8,128)(2,1)}, u32[]{:S(2)}) copy-start(bf16[128,16,128]{2,1,0:T(8,128)(2,1)} %param.9) | copy-start | bytes 1572868
  2.9 74.8 %all-to-all-start = ((bf16[128,32,128]{2,1,0:T(8,128)(2,1)}), bf16[128,32,128]{2,1,0:T(8,128)(2,1)S(1)}, u32[]{:S(2)}, u32[]{:S(2)}) async-start(bf16[128,32,128]{2,1,0:T(8,128)(2,1)} %pad_maximum_fusion), calls=%async_computation | async-start | bytes 2097152 | tf_op jit(solution)/shard_map/all_to_all | solution.py:172
  24.4 0.7 copy-start.4
  78.1 3.4 %collective-permute-start = (bf16[16,4,16,128]{3,2,1,0:T(8,128)(2,1)S(1)}, bf16[16,4,16,128]{3,2,1,0:T(8,128)(2,1)S(1)}, u32[]{:S(2)}, u32[]{:S(2)}) collective-permute-start(bf16[16,4,16,128]{3,2,1,0:T(8,128)(2,1)S(1)} %bitcast.41), channel_id=1, source_target_pairs={{0,1},{1,0},{2,3},{3,2},{4,5},{5,4},{6,7},{7,6},{8,9},{9,8},{10,11... | collective-permute-start | bytes 786440 | tf_op jit(solution)/shard_map/ppermute | solution.py:163
  81.6 11.0 %collective-permute-start.1 = (bf16[2,16,4,16,128]{4,3,2,1,0:T(8,128)(2,1)S(1)}, bf16[2,16,4,16,128]{4,3,2,1,0:T(8,128)(2,1)S(1)}, u32[]{:S(2)}, u32[]{:S(2)}) collective-permute-start(bf16[2,16,4,16,128]{4,3,2,1,0:T(8,128)(2,1)S(1)} %pad_maximum_fusion.1.near_ref), channel_id=1, source_target_pairs={{1,17},{17,1},{3,19},{19,3},{5,21},{21,5},{7,23},{23,7},{9,25},{25... | collective-permute-start | bytes 1572872 | tf_op jit(solution)/shard_map/ppermute | solution.py:168
  82.4 7.7 %collective-permute-start.2 = (bf16[16,4,16,128]{3,2,1,0:T(8,128)(2,1)S(1)}, bf16[16,4,16,128]{3,2,1,0:T(8,128)(2,1)S(1)}, u32[]{:S(2)}, u32[]{:S(2)}) collective-permute-start(bf16[16,4,16,128]{3,2,1,0:T(8,128)(2,1)S(1)} %get-tuple-element.32), channel_id=1, source_target_pairs={{0,1},{1,0},{2,3},{3,2},{4,5},{5,4},{6,7},{7,6},{8,9},{9,8},{10,11... | collective-permute-start | bytes 786440 | tf_op jit(solution)/shard_map/ppermute | solution.py:163
  88.1 3.4 %collective-permute-start.3 = (bf16[16,4,16,128]{3,2,1,0:T(8,128)(2,1)S(1)}, bf16[16,4,16,128]{3,2,1,0:T(8,128)(2,1)S(1)}, u32[]{:S(2)}, u32[]{:S(2)}) collective-permute-start(bf16[16,4,16,128]{3,2,1,0:T(8,128)(2,1)S(1)} %get-tuple-element.33), channel_id=1, source_target_pairs={{0,1},{1,0},{2,3},{3,2},{4,5},{5,4},{6,7},{7,6},{8,9},{9,8},{10,11... | collective-permute-start | bytes 786440 | tf_op jit(solution)/shard_map/ppermute | solution.py:163
  92.6 12.6 %collective-permute-start.4 = (bf16[2,16,4,16,128]{4,3,2,1,0:T(8,128)(2,1)S(1)}, bf16[2,16,4,16,128]{4,3,2,1,0:T(8,128)(2,1)S(1)}, u32[]{:S(2)}, u32[]{:S(2)}) collective-permute-start(bf16[2,16,4,16,128]{4,3,2,1,0:T(8,128)(2,1)S(1)} %pad_maximum_fusion.1.near_ref), channel_id=1, source_target_pairs={{0,16},{16,0},{2,18},{18,2},{4,20},{20,4},{6,22},{22,6},{8,24},{24... | collective-permute-start | bytes 1572872 | tf_op jit(solution)/shard_map/ppermute | solution.py:168
  168.4 3.9 %collective-permute-start.6 = (bf16[2,16,4,16,128]{4,3,2,1,0:T(8,128)(2,1)S(1)}, bf16[2,16,4,16,128]{4,3,2,1,0:T(8,128)(2,1)S(1)}, u32[]{:S(2)}, u32[]{:S(2)}) collective-permute-start(bf16[2,16,4,16,128]{4,3,2,1,0:T(8,128)(2,1)S(1)} %get-tuple-element.46), channel_id=1, source_target_pairs={{1,17},{17,1},{3,19},{19,3},{5,21},{21,5},{7,23},{23,7},{9,25},{25... | collective-permute-start | bytes 1572872 | tf_op jit(solution)/shard_map/ppermute | solution.py:168
  170.3 6.2 %collective-permute-start.5 = (bf16[32,4,16,128]{3,2,1,0:T(8,128)(2,1)S(1)}, bf16[32,4,16,128]{3,2,1,0:T(8,128)(2,1)S(1)}, u32[]{:S(2)}, u32[]{:S(2)}) collective-permute-start(bf16[32,4,16,128]{3,2,1,0:T(8,128)(2,1)S(1)} %get-tuple-element.44), channel_id=1, source_target_pairs={{0,1},{1,0},{2,3},{3,2},{4,5},{5,4},{6,7},{7,6},{8,9},{9,8},{10,11... | collective-permute-start | bytes 1572872 | tf_op jit(solution)/shard_map/ppermute | solution.py:163
  172.3 12.6 %collective-permute-start.7 = (bf16[2,16,4,16,128]{4,3,2,1,0:T(8,128)(2,1)S(1)}, bf16[2,16,4,16,128]{4,3,2,1,0:T(8,128)(2,1)S(1)}, u32[]{:S(2)}, u32[]{:S(2)}) collective-permute-start(bf16[2,16,4,16,128]{4,3,2,1,0:T(8,128)(2,1)S(1)} %get-tuple-element.46), channel_id=1, source_target_pairs={{0,16},{16,0},{2,18},{18,2},{4,20},{20,4},{6,22},{22,6},{8,24},{24... | collective-permute-start | bytes 1572872 | tf_op jit(solution)/shard_map/ppermute | solution.py:168
  184.9 31.5 %all-to-all-start.3 = ((bf16[128,16,128]{2,1,0:T(8,128)(2,1)}), bf16[128,16,128]{2,1,0:T(8,128)(2,1)S(1)}, u32[]{:S(2)}, u32[]{:S(2)}) async-start(bf16[128,16,128]{2,1,0:T(8,128)(2,1)} %bitcast.12), calls=%async_computation.3 | async-start | bytes 1048576 | tf_op jit(solution)/shard_map/all_to_all | solution.py:172
  193.5 3.4 %collective-permute-start.8 = (bf16[4,4,4,16,128]{4,3,2,1,0:T(8,128)(2,1)S(1)}, bf16[4,4,4,16,128]{4,3,2,1,0:T(8,128)(2,1)S(1)}, u32[]{:S(2)}, u32[]{:S(2)}) collective-permute-start(bf16[4,4,4,16,128]{4,3,2,1,0:T(8,128)(2,1)S(1)} %bitcast.42), channel_id=1, source_target_pairs={{0,1},{1,0},{2,3},{3,2},{4,5},{5,4},{6,7},{7,6},{8,9},{9,8},{10,11... | collective-permute-start | bytes 786440 | tf_op jit(solution)/shard_map/ppermute | solution.py:163

commit v8 on v7

--- a/solution.py
+++ b/solution.py
@@ -109,19 +109,18 @@
         return product_ref[c].astype(F32)
 
     zeros = jnp.zeros(product_ref.shape[1:], F32)
+    first = load(0)
 
     def sums(c, carry):
-        return carry[0] + load(c), carry[1] + scaled_ref[c]
-
-    total, scaled_total = lax.fori_loop(0, count, sums, (zeros, zeros), unroll=8)
-    mean = total * (1.0 / count)
+        off, scaled = load(c) - first, scaled_ref[c]
+        return carry[0] + off, carry[1] + off * off, carry[2] + scaled, carry[3] + scaled * off
+
+    total, square, scaled_total, cross = lax.fori_loop(0, count, sums, (zeros,) * 4, unroll=8)
+    off_mean = total * (1.0 / count)
+    mean = first + off_mean
     scaled_mean = scaled_total * (1.0 / count)
-
-    def squares(c, carry):
-        center = load(c) - mean
-        return carry[0] + center * center, carry[1] + scaled_ref[c] * center
-
-    square, cross = lax.fori_loop(0, count, squares, (zeros, zeros), unroll=8)
+    square = jnp.maximum(square - off_mean * total, 0.0)
+    cross = cross - off_mean * scaled_total
     inv_std = lax.rsqrt(square * (1.0 / count) + norm_eps)
     slope = inv_std * inv_std * cross * (1.0 / count)
 

time: 248 us -> 248 us (level)
  no operation moved by 1% of the time
where the time goes in v8:
time: 248 us; the launch traced here: 247 us
  waiting for transfers between devices  93.4 us (38%)
  blocking collectives  89.9 us (36%)
  starting transfers between devices  50.7 us (20%)
  Pallas kernels  5.67 us (2%)
  other arithmetic  5.13 us (2%)
    all_to_all x3, blocking collectives, to_owners(): return lax.all_to_all(x, OWNERS, split_axis=0, concat_axis=0, tiled=True)  89.9 us
    all_to_all x2, waiting for transfers between devices, to_owners(): return lax.all_to_all(x, OWNERS, split_axis=0, concat_axis=0, tiled=True)  71.8 us
    all_to_all x2, starting transfers between devices, to_owners(): return lax.all_to_all(x, OWNERS, split_axis=0, concat_axis=0, tiled=True)  28.9 us
    ppermute x4, waiting for transfers between devices, swap_pair(): return lax.ppermute(x, (PAIR, 'c'), [(at[0], at[1]), (at[1], at[0])])  17.2 us
    ppermute x5, starting transfers between devices, swap(): return lax.ppermute(x, axis, [(0, 1), (1, 0)])  13.4 us
    ppermute x4, starting transfers between devices, swap_pair(): return lax.ppermute(x, (PAIR, 'c'), [(at[0], at[1]), (at[1], at[0])])  8.36 us
    pallas_call x5, Pallas kernels, call(): pl.pallas_call(kernel, out_shape=outs, in_specs=[smem()] * scalars + [vme...  5.67 us
  transfers between devices with their start and end apart: 11, of which 7 were waited for; matrix products, arithmetic and copies ran while one was open for 1% of the time, Pallas kernels for 1%

profile of v8, /device:TPU:8, one launch (start us, length us, event | category | flops | bytes accessed | tf_op | source)
XLA Modules:
  0.0 247.5 jit_solution(3934834161508446666)
XLA Ops:
  0.6 2.3 pad_maximum_fusion
  2.9 20.6 %all-to-all-start = ((bf16[128,32,128]{2,1,0:T(8,128)(2,1)}), bf16[128,32,128]{2,1,0:T(8,128)(2,1)S(1)}, u32[]{:S(2)}, u32[]{:S(2)}) async-start(bf16[128,32,128]{2,1,0:T(8,128)(2,1)} %pad_maximum_fusion), calls=%async_computation | async-start | bytes 2097152 | tf_op jit(solution)/shard_map/all_to_all | solution.py:171
  25.3 52.5 %all-to-all-done = bf16[128,32,128]{2,1,0:T(8,128)(2,1)S(1)} async-done(((bf16[128,32,128]{2,1,0:T(8,128)(2,1)}), bf16[128,32,128]{2,1,0:T(8,128)(2,1)S(1)}, u32[]{:S(2)}, u32[]{:S(2)}) %all-to-all-start) | async-done | bytes 1048608 | tf_op jit(solution)/shard_map/all_to_all | solution.py:171
  78.1 1.9 collective-permute-start
  80.1 1.5 collective-permute-done
  82.4 5.7 %collective-permute-start.2 = (bf16[16,4,16,128]{3,2,1,0:T(8,128)(2,1)S(1)}, bf16[16,4,16,128]{3,2,1,0:T(8,128)(2,1)S(1)}, u32[]{:S(2)}, u32[]{:S(2)}) collective-permute-start(bf16[16,4,16,128]{3,2,1,0:T(8,128)(2,1)S(1)} %get-tuple-element.32), channel_id=1, source_target_pairs={{0,1},{1,0},{2,3},{3,2},{4,5},{5,4},{6,7},{7,6},{8,9},{9,8},{10,11... | collective-permute-start | bytes 786440 | tf_op jit(solution)/shard_map/ppermute | solution.py:162
  88.1 1.9 collective-permute-start.3
  90.1 1.4 collective-permute-done.3.left_high_ref
  91.5 1.0 shard_map.86
  92.6 2.7 %collective-permute-start.4 = (bf16[2,16,4,16,128]{4,3,2,1,0:T(8,128)(2,1)S(1)}, bf16[2,16,4,16,128]{4,3,2,1,0:T(8,128)(2,1)S(1)}, u32[]{:S(2)}, u32[]{:S(2)}) collective-permute-start(bf16[2,16,4,16,128]{4,3,2,1,0:T(8,128)(2,1)S(1)} %pad_maximum_fusion.1.near_ref), channel_id=1, source_target_pairs={{0,16},{16,0},{2,18},{18,2},{4,20},{20,4},{6,22},{22,6},{8,24},{24... | collective-permute-start | bytes 1572872 | tf_op jit(solution)/shard_map/ppermute | solution.py:167
  95.3 9.9 %collective-permute-done.4.far_0_ref = bf16[2,16,4,16,128]{4,3,2,1,0:T(8,128)(2,1)S(1)} collective-permute-done((bf16[2,16,4,16,128]{4,3,2,1,0:T(8,128)(2,1)S(1)}, bf16[2,16,4,16,128]{4,3,2,1,0:T(8,128)(2,1)S(1)}, u32[]{:S(2)}, u32[]{:S(2)}) %collective-permute-start.4) | collective-permute-done | bytes 524320 | tf_op jit(solution)/shard_map/ppermute | solution.py:167
  105.2 1.4 shard_map.87
  106.6 30.1 %all_to_all.25.product_ref = bf16[128,16,128]{2,1,0:T(8,128)(2,1)S(1)} all-to-all(bf16[128,16,128]{2,1,0:T(8,128)(2,1)S(1)} %bitcast.35), channel_id=1, replica_groups=mesh['zl'=4,'y'=4,'xh'=2,'xl'=2,'zh'=4,'c'=2] {'zl','y','xl','zh'}, dimensions={0} | all-to-all | bytes 1048576 | tf_op jit(solution)/shard_map/all_to_all | solution.py:171
  137.4 29.5 %all_to_all.26 = bf16[128,16,128]{2,1,0:T(8,128)(2,1)S(1)} all-to-all(bf16[128,16,128]{2,1,0:T(8,128)(2,1)S(1)} %shard_map.88), channel_id=1, replica_groups=mesh['zl'=4,'y'=4,'xh'=2,'xl'=2,'zh'=4,'c'=2] {'zl','y','xl','zh'}, dimensions={0} | all-to-all | bytes 1048576 | tf_op jit(solution)/shard_map/all_to_all | solution.py:171
  167.0 1.3 shard_map.90
  168.9 1.3 shard_map.89
  170.2 1.9 collective-permute-start.5
  172.1 4.3 %collective-permute-start.7 = (bf16[2,16,4,16,128]{4,3,2,1,0:T(8,128)(2,1)S(1)}, bf16[2,16,4,16,128]{4,3,2,1,0:T(8,128)(2,1)S(1)}, u32[]{:S(2)}, u32[]{:S(2)}) collective-permute-start(bf16[2,16,4,16,128]{4,3,2,1,0:T(8,128)(2,1)S(1)} %get-tuple-element.46), channel_id=1, source_target_pairs={{0,16},{16,0},{2,18},{18,2},{4,20},{20,4},{6,22},{22,6},{8,24},{24... | collective-permute-start | bytes 1572872 | tf_op jit(solution)/shard_map/ppermute | solution.py:167
  177.4 7.3 %collective-permute-done.7 = bf16[2,16,4,16,128]{4,3,2,1,0:T(8,128)(2,1)S(1)} collective-permute-done((bf16[2,16,4,16,128]{4,3,2,1,0:T(8,128)(2,1)S(1)}, bf16[2,16,4,16,128]{4,3,2,1,0:T(8,128)(2,1)S(1)}, u32[]{:S(2)}, u32[]{:S(2)}) %collective-permute-start.7) | collective-permute-done | bytes 524320 | tf_op jit(solution)/shard_map/ppermute | solution.py:167
  184.7 8.3 %all-to-all-start.3 = ((bf16[128,16,128]{2,1,0:T(8,128)(2,1)}), bf16[128,16,128]{2,1,0:T(8,128)(2,1)S(1)}, u32[]{:S(2)}, u32[]{:S(2)}) async-start(bf16[128,16,128]{2,1,0:T(8,128)(2,1)} %bitcast.12), calls=%async_computation.3 | async-start | bytes 1048576 | tf_op jit(solution)/shard_map/all_to_all | solution.py:171
  193.4 1.9 collective-permute-start.8
  195.3 1.5 collective-permute-done.8
  196.9 19.3 %all-to-all-done.3 = bf16[128,16,128]{2,1,0:T(8,128)(2,1)S(1)} async-done(((bf16[128,16,128]{2,1,0:T(8,128)(2,1)}), bf16[128,16,128]{2,1,0:T(8,128)(2,1)S(1)}, u32[]{:S(2)}, u32[]{:S(2)}) %all-to-all-start.3) | async-done | bytes 524320 | tf_op jit(solution)/shard_map/all_to_all | solution.py:171
  216.2 30.2 %all_to_all.27 = bf16[128,16,128]{2,1,0:T(8,128)(2,1)S(1)} all-to-all(bf16[128,16,128]{2,1,0:T(8,128)(2,1)S(1)} %bitcast.38), channel_id=1, replica_groups=mesh['zl'=4,'y'=4,'xh'=2,'xl'=2,'zh'=4,'c'=2] {'zl','y','xl','zh'}, dimensions={0} | all-to-all | bytes 1048576 | tf_op jit(solution)/shard_map/all_to_all | solution.py:171
  (44 shorter events, 6.7 us)
Async XLA Ops:
  0.6 23.4 %copy-start = (bf16[128,128]{1,0:T(8,128)(2,1)S(1)}, bf16[128,128]{1,0:T(8,128)(2,1)}, u32[]{:S(2)}) copy-start(bf16[128,128]{1,0:T(8,128)(2,1)} %param.12) | copy-start | bytes 98308
  2.9 20.6 %copy-start.3 = (s32[1024]{0:T(1024)S(1)}, s32[1024]{0:T(1024)}, u32[]{:S(2)}) copy-start(s32[1024]{0:T(1024)} %param.13) | copy-start | bytes 12292
  2.9 21.0 %copy-start.1 = (bf16[128,16,128]{2,1,0:T(8,128)(2,1)S(1)}, bf16[128,16,128]{2,1,0:T(8,128)(2,1)}, u32[]{:S(2)}) copy-start(bf16[128,16,128]{2,1,0:T(8,128)(2,1)} %param.10) | copy-start | bytes 1572868
  2.9 21.0 %copy-start.2 = (bf16[128,16,128]{2,1,0:T(8,128)(2,1)S(1)}, bf16[128,16,128]{2,1,0:T(8,128)(2,1)}, u32[]{:S(2)}) copy-start(bf16[128,16,128]{2,1,0:T(8,128)(2,1)} %param.9) | copy-start | bytes 1572868
  2.9 74.8 %all-to-all-start = ((bf16[128,32,128]{2,1,0:T(8,128)(2,1)}), bf16[128,32,128]{2,1,0:T(8,128)(2,1)S(1)}, u32[]{:S(2)}, u32[]{:S(2)}) async-start(bf16[128,32,128]{2,1,0:T(8,128)(2,1)} %pad_maximum_fusion), calls=%async_computation | async-start | bytes 2097152 | tf_op jit(solution)/shard_map/all_to_all | solution.py:171
  24.4 0.7 copy-start.4
  78.1 3.4 %collective-permute-start = (bf16[16,4,16,128]{3,2,1,0:T(8,128)(2,1)S(1)}, bf16[16,4,16,128]{3,2,1,0:T(8,128)(2,1)S(1)}, u32[]{:S(2)}, u32[]{:S(2)}) collective-permute-start(bf16[16,4,16,128]{3,2,1,0:T(8,128)(2,1)S(1)} %bitcast.41), channel_id=1, source_target_pairs={{0,1},{1,0},{2,3},{3,2},{4,5},{5,4},{6,7},{7,6},{8,9},{9,8},{10,11... | collective-permute-start | bytes 786440 | tf_op jit(solution)/shard_map/ppermute | solution.py:162
  81.6 11.0 %collective-permute-start.1 = (bf16[2,16,4,16,128]{4,3,2,1,0:T(8,128)(2,1)S(1)}, bf16[2,16,4,16,128]{4,3,2,1,0:T(8,128)(2,1)S(1)}, u32[]{:S(2)}, u32[]{:S(2)}) collective-permute-start(bf16[2,16,4,16,128]{4,3,2,1,0:T(8,128)(2,1)S(1)} %pad_maximum_fusion.1.near_ref), channel_id=1, source_target_pairs={{1,17},{17,1},{3,19},{19,3},{5,21},{21,5},{7,23},{23,7},{9,25},{25... | collective-permute-start | bytes 1572872 | tf_op jit(solution)/shard_map/ppermute | solution.py:167
  82.4 7.7 %collective-permute-start.2 = (bf16[16,4,16,128]{3,2,1,0:T(8,128)(2,1)S(1)}, bf16[16,4,16,128]{3,2,1,0:T(8,128)(2,1)S(1)}, u32[]{:S(2)}, u32[]{:S(2)}) collective-permute-start(bf16[16,4,16,128]{3,2,1,0:T(8,128)(2,1)S(1)} %get-tuple-element.32), channel_id=1, source_target_pairs={{0,1},{1,0},{2,3},{3,2},{4,5},{5,4},{6,7},{7,6},{8,9},{9,8},{10,11... | collective-permute-start | bytes 786440 | tf_op jit(solution)/shard_map/ppermute | solution.py:162
  88.1 3.4 %collective-permute-start.3 = (bf16[16,4,16,128]{3,2,1,0:T(8,128)(2,1)S(1)}, bf16[16,4,16,128]{3,2,1,0:T(8,128)(2,1)S(1)}, u32[]{:S(2)}, u32[]{:S(2)}) collective-permute-start(bf16[16,4,16,128]{3,2,1,0:T(8,128)(2,1)S(1)} %get-tuple-element.33), channel_id=1, source_target_pairs={{0,1},{1,0},{2,3},{3,2},{4,5},{5,4},{6,7},{7,6},{8,9},{9,8},{10,11... | collective-permute-start | bytes 786440 | tf_op jit(solution)/shard_map/ppermute | solution.py:162
  92.6 12.6 %collective-permute-start.4 = (bf16[2,16,4,16,128]{4,3,2,1,0:T(8,128)(2,1)S(1)}, bf16[2,16,4,16,128]{4,3,2,1,0:T(8,128)(2,1)S(1)}, u32[]{:S(2)}, u32[]{:S(2)}) collective-permute-start(bf16[2,16,4,16,128]{4,3,2,1,0:T(8,128)(2,1)S(1)} %pad_maximum_fusion.1.near_ref), channel_id=1, source_target_pairs={{0,16},{16,0},{2,18},{18,2},{4,20},{20,4},{6,22},{22,6},{8,24},{24... | collective-permute-start | bytes 1572872 | tf_op jit(solution)/shard_map/ppermute | solution.py:167
  168.2 3.9 %collective-permute-start.6 = (bf16[2,16,4,16,128]{4,3,2,1,0:T(8,128)(2,1)S(1)}, bf16[2,16,4,16,128]{4,3,2,1,0:T(8,128)(2,1)S(1)}, u32[]{:S(2)}, u32[]{:S(2)}) collective-permute-start(bf16[2,16,4,16,128]{4,3,2,1,0:T(8,128)(2,1)S(1)} %get-tuple-element.46), channel_id=1, source_target_pairs={{1,17},{17,1},{3,19},{19,3},{5,21},{21,5},{7,23},{23,7},{9,25},{25... | collective-permute-start | bytes 1572872 | tf_op jit(solution)/shard_map/ppermute | solution.py:167
  170.2 6.2 %collective-permute-start.5 = (bf16[32,4,16,128]{3,2,1,0:T(8,128)(2,1)S(1)}, bf16[32,4,16,128]{3,2,1,0:T(8,128)(2,1)S(1)}, u32[]{:S(2)}, u32[]{:S(2)}) collective-permute-start(bf16[32,4,16,128]{3,2,1,0:T(8,128)(2,1)S(1)} %get-tuple-element.44), channel_id=1, source_target_pairs={{0,1},{1,0},{2,3},{3,2},{4,5},{5,4},{6,7},{7,6},{8,9},{9,8},{10,11... | collective-permute-start | bytes 1572872 | tf_op jit(solution)/shard_map/ppermute | solution.py:162
  172.1 12.6 %collective-permute-start.7 = (bf16[2,16,4,16,128]{4,3,2,1,0:T(8,128)(2,1)S(1)}, bf16[2,16,4,16,128]{4,3,2,1,0:T(8,128)(2,1)S(1)}, u32[]{:S(2)}, u32[]{:S(2)}) collective-permute-start(bf16[2,16,4,16,128]{4,3,2,1,0:T(8,128)(2,1)S(1)} %get-tuple-element.46), channel_id=1, source_target_pairs={{0,16},{16,0},{2,18},{18,2},{4,20},{20,4},{6,22},{22,6},{8,24},{24... | collective-permute-start | bytes 1572872 | tf_op jit(solution)/shard_map/ppermute | solution.py:167
  184.7 31.5 %all-to-all-start.3 = ((bf16[128,16,128]{2,1,0:T(8,128)(2,1)}), bf16[128,16,128]{2,1,0:T(8,128)(2,1)S(1)}, u32[]{:S(2)}, u32[]{:S(2)}) async-start(bf16[128,16,128]{2,1,0:T(8,128)(2,1)} %bitcast.12), calls=%async_computation.3 | async-start | bytes 1048576 | tf_op jit(solution)/shard_map/all_to_all | solution.py:171
  193.4 3.4 %collective-permute-start.8 = (bf16[4,4,4,16,128]{4,3,2,1,0:T(8,128)(2,1)S(1)}, bf16[4,4,4,16,128]{4,3,2,1,0:T(8,128)(2,1)S(1)}, u32[]{:S(2)}, u32[]{:S(2)}) collective-permute-start(bf16[4,4,4,16,128]{4,3,2,1,0:T(8,128)(2,1)S(1)} %bitcast.42), channel_id=1, source_target_pairs={{0,1},{1,0},{2,3},{3,2},{4,5},{5,4},{6,7},{7,6},{8,9},{9,8},{10,11... | collective-permute-start | bytes 786440 | tf_op jit(solution)/shard_map/ppermute | solution.py:162

commit v9 on v7

--- a/solution.py
+++ b/solution.py
@@ -44,8 +44,6 @@
         mask = (i_mask * k_mask_ref[:, cols][None]).reshape(512, 128)
         out_ref[:, cols] = part * mask
     place_rows(place_ref[0], near_ref, j_mask_ref, right_ref)
-    zeros = jnp.zeros((4, 2, 2, 16, 1024), BF16)
-    right_ref[:, :, 1 - place_ref[0], :, :, :] = zeros
 
 
 def whole_grad(grad_ref):

time: 248 us -> 248 us (level)
  no operation moved by 1% of the time
where the time goes in v9:
time: 248 us
  waiting for transfers between devices  93.4 us (38%)
  blocking collectives  90 us (36%)
  starting transfers between devices  50.6 us (20%)
  Pallas kernels  5.76 us (2%)
  other arithmetic  5.13 us (2%)
    all_to_all x3, blocking collectives, to_owners(): return lax.all_to_all(x, OWNERS, split_axis=0, concat_axis=0, tiled=True)  90 us
    all_to_all x2, waiting for transfers between devices, to_owners(): return lax.all_to_all(x, OWNERS, split_axis=0, concat_axis=0, tiled=True)  71.8 us
    all_to_all x2, starting transfers between devices, to_owners(): return lax.all_to_all(x, OWNERS, split_axis=0, concat_axis=0, tiled=True)  28.9 us
    ppermute x4, waiting for transfers between devices, swap_pair(): return lax.ppermute(x, (PAIR, 'c'), [(at[0], at[1]), (at[1], at[0])])  17.2 us
    ppermute x5, starting transfers between devices, swap(): return lax.ppermute(x, axis, [(0, 1), (1, 0)])  13.4 us
    ppermute x4, starting transfers between devices, swap_pair(): return lax.ppermute(x, (PAIR, 'c'), [(at[0], at[1]), (at[1], at[0])])  8.34 us
    pallas_call x5, Pallas kernels, call(): pl.pallas_call(kernel, out_shape=outs, in_specs=[smem()] * scalars + [vme...  5.76 us
  transfers between devices with their start and end apart: 11, of which 7 were waited for; matrix products, arithmetic and copies ran while one was open for 1% of the time, Pallas kernels for 1%

profile of v9, /device:TPU:8, one launch (start us, length us, event | category | flops | bytes accessed | tf_op | source)
XLA Modules:
  0.0 247.6 jit_solution(14990009801397109882)
XLA Ops:
  0.6 2.3 pad_maximum_fusion
  2.9 20.6 %all-to-all-start = ((bf16[128,32,128]{2,1,0:T(8,128)(2,1)}), bf16[128,32,128]{2,1,0:T(8,128)(2,1)S(1)}, u32[]{:S(2)}, u32[]{:S(2)}) async-start(bf16[128,32,128]{2,1,0:T(8,128)(2,1)} %pad_maximum_fusion), calls=%async_computation | async-start | bytes 2097152 | tf_op jit(solution)/shard_map/all_to_all | solution.py:170
  25.3 52.5 %all-to-all-done = bf16[128,32,128]{2,1,0:T(8,128)(2,1)S(1)} async-done(((bf16[128,32,128]{2,1,0:T(8,128)(2,1)}), bf16[128,32,128]{2,1,0:T(8,128)(2,1)S(1)}, u32[]{:S(2)}, u32[]{:S(2)}) %all-to-all-start) | async-done | bytes 1048608 | tf_op jit(solution)/shard_map/all_to_all | solution.py:170
  78.1 1.9 collective-permute-start
  80.1 1.5 collective-permute-done
  82.4 5.7 %collective-permute-start.2 = (bf16[16,4,16,128]{3,2,1,0:T(8,128)(2,1)S(1)}, bf16[16,4,16,128]{3,2,1,0:T(8,128)(2,1)S(1)}, u32[]{:S(2)}, u32[]{:S(2)}) collective-permute-start(bf16[16,4,16,128]{3,2,1,0:T(8,128)(2,1)S(1)} %get-tuple-element.32), channel_id=1, source_target_pairs={{0,1},{1,0},{2,3},{3,2},{4,5},{5,4},{6,7},{7,6},{8,9},{9,8},{10,11... | collective-permute-start | bytes 786440 | tf_op jit(solution)/shard_map/ppermute | solution.py:161
  88.1 1.9 collective-permute-start.3
  90.1 1.4 collective-permute-done.3.left_high_ref
  92.5 2.7 %collective-permute-start.4 = (bf16[2,16,4,16,128]{4,3,2,1,0:T(8,128)(2,1)S(1)}, bf16[2,16,4,16,128]{4,3,2,1,0:T(8,128)(2,1)S(1)}, u32[]{:S(2)}, u32[]{:S(2)}) collective-permute-start(bf16[2,16,4,16,128]{4,3,2,1,0:T(8,128)(2,1)S(1)} %pad_maximum_fusion.1.near_ref), channel_id=1, source_target_pairs={{0,16},{16,0},{2,18},{18,2},{4,20},{20,4},{6,22},{22,6},{8,24},{24... | collective-permute-start | bytes 1572872 | tf_op jit(solution)/shard_map/ppermute | solution.py:166
  95.3 9.9 %collective-permute-done.4.far_0_ref = bf16[2,16,4,16,128]{4,3,2,1,0:T(8,128)(2,1)S(1)} collective-permute-done((bf16[2,16,4,16,128]{4,3,2,1,0:T(8,128)(2,1)S(1)}, bf16[2,16,4,16,128]{4,3,2,1,0:T(8,128)(2,1)S(1)}, u32[]{:S(2)}, u32[]{:S(2)}) %collective-permute-start.4) | collective-permute-done | bytes 524320 | tf_op jit(solution)/shard_map/ppermute | solution.py:166
  105.1 1.4 shard_map.87
  106.6 30.2 %all_to_all.25.product_ref = bf16[128,16,128]{2,1,0:T(8,128)(2,1)S(1)} all-to-all(bf16[128,16,128]{2,1,0:T(8,128)(2,1)S(1)} %bitcast.35), channel_id=1, replica_groups=mesh['zl'=4,'y'=4,'xh'=2,'xl'=2,'zh'=4,'c'=2] {'zl','y','xl','zh'}, dimensions={0} | all-to-all | bytes 1048576 | tf_op jit(solution)/shard_map/all_to_all | solution.py:170
  137.6 29.5 %all_to_all.26 = bf16[128,16,128]{2,1,0:T(8,128)(2,1)S(1)} all-to-all(bf16[128,16,128]{2,1,0:T(8,128)(2,1)S(1)} %shard_map.88), channel_id=1, replica_groups=mesh['zl'=4,'y'=4,'xh'=2,'xl'=2,'zh'=4,'c'=2] {'zl','y','xl','zh'}, dimensions={0} | all-to-all | bytes 1048576 | tf_op jit(solution)/shard_map/all_to_all | solution.py:170
  167.1 1.3 shard_map.90
  169.1 1.3 shard_map.89
  170.3 1.9 collective-permute-start.5
  172.3 4.2 %collective-permute-start.7 = (bf16[2,16,4,16,128]{4,3,2,1,0:T(8,128)(2,1)S(1)}, bf16[2,16,4,16,128]{4,3,2,1,0:T(8,128)(2,1)S(1)}, u32[]{:S(2)}, u32[]{:S(2)}) collective-permute-start(bf16[2,16,4,16,128]{4,3,2,1,0:T(8,128)(2,1)S(1)} %get-tuple-element.46), channel_id=1, source_target_pairs={{0,16},{16,0},{2,18},{18,2},{4,20},{20,4},{6,22},{22,6},{8,24},{24... | collective-permute-start | bytes 1572872 | tf_op jit(solution)/shard_map/ppermute | solution.py:166
  177.5 7.4 %collective-permute-done.7 = bf16[2,16,4,16,128]{4,3,2,1,0:T(8,128)(2,1)S(1)} collective-permute-done((bf16[2,16,4,16,128]{4,3,2,1,0:T(8,128)(2,1)S(1)}, bf16[2,16,4,16,128]{4,3,2,1,0:T(8,128)(2,1)S(1)}, u32[]{:S(2)}, u32[]{:S(2)}) %collective-permute-start.7) | collective-permute-done | bytes 524320 | tf_op jit(solution)/shard_map/ppermute | solution.py:166
  184.8 8.3 %all-to-all-start.3 = ((bf16[128,16,128]{2,1,0:T(8,128)(2,1)}), bf16[128,16,128]{2,1,0:T(8,128)(2,1)S(1)}, u32[]{:S(2)}, u32[]{:S(2)}) async-start(bf16[128,16,128]{2,1,0:T(8,128)(2,1)} %bitcast.12), calls=%async_computation.3 | async-start | bytes 1048576 | tf_op jit(solution)/shard_map/all_to_all | solution.py:170
  193.5 1.9 collective-permute-start.8
  195.4 1.5 collective-permute-done.8
  197.0 19.3 %all-to-all-done.3 = bf16[128,16,128]{2,1,0:T(8,128)(2,1)S(1)} async-done(((bf16[128,16,128]{2,1,0:T(8,128)(2,1)}), bf16[128,16,128]{2,1,0:T(8,128)(2,1)S(1)}, u32[]{:S(2)}, u32[]{:S(2)}) %all-to-all-start.3) | async-done | bytes 524320 | tf_op jit(solution)/shard_map/all_to_all | solution.py:170
  216.3 30.2 %all_to_all.27 = bf16[128,16,128]{2,1,0:T(8,128)(2,1)S(1)} all-to-all(bf16[128,16,128]{2,1,0:T(8,128)(2,1)S(1)} %bitcast.38), channel_id=1, replica_groups=mesh['zl'=4,'y'=4,'xh'=2,'xl'=2,'zh'=4,'c'=2] {'zl','y','xl','zh'}, dimensions={0} | all-to-all | bytes 1048576 | tf_op jit(solution)/shard_map/all_to_all | solution.py:170
  246.6 1.0 broadcast_multiply_fusion.1
  (44 shorter events, 6.8 us)
Async XLA Ops:
  0.6 23.4 %copy-start = (bf16[128,128]{1,0:T(8,128)(2,1)S(1)}, bf16[128,128]{1,0:T(8,128)(2,1)}, u32[]{:S(2)}) copy-start(bf16[128,128]{1,0:T(8,128)(2,1)} %param.12) | copy-start | bytes 98308
  2.9 20.6 %copy-start.3 = (s32[1024]{0:T(1024)S(1)}, s32[1024]{0:T(1024)}, u32[]{:S(2)}) copy-start(s32[1024]{0:T(1024)} %param.13) | copy-start | bytes 12292
  2.9 21.0 %copy-start.1 = (bf16[128,16,128]{2,1,0:T(8,128)(2,1)S(1)}, bf16[128,16,128]{2,1,0:T(8,128)(2,1)}, u32[]{:S(2)}) copy-start(bf16[128,16,128]{2,1,0:T(8,128)(2,1)} %param.10) | copy-start | bytes 1572868
  2.9 21.0 %copy-start.2 = (bf16[128,16,128]{2,1,0:T(8,128)(2,1)S(1)}, bf16[128,16,128]{2,1,0:T(8,128)(2,1)}, u32[]{:S(2)}) copy-start(bf16[128,16,128]{2,1,0:T(8,128)(2,1)} %param.9) | copy-start | bytes 1572868
  2.9 74.8 %all-to-all-start = ((bf16[128,32,128]{2,1,0:T(8,128)(2,1)}), bf16[128,32,128]{2,1,0:T(8,128)(2,1)S(1)}, u32[]{:S(2)}, u32[]{:S(2)}) async-start(bf16[128,32,128]{2,1,0:T(8,128)(2,1)} %pad_maximum_fusion), calls=%async_computation | async-start | bytes 2097152 | tf_op jit(solution)/shard_map/all_to_all | solution.py:170
  24.4 0.7 copy-start.4
  78.1 3.4 %collective-permute-start = (bf16[16,4,16,128]{3,2,1,0:T(8,128)(2,1)S(1)}, bf16[16,4,16,128]{3,2,1,0:T(8,128)(2,1)S(1)}, u32[]{:S(2)}, u32[]{:S(2)}) collective-permute-start(bf16[16,4,16,128]{3,2,1,0:T(8,128)(2,1)S(1)} %bitcast.41), channel_id=1, source_target_pairs={{0,1},{1,0},{2,3},{3,2},{4,5},{5,4},{6,7},{7,6},{8,9},{9,8},{10,11... | collective-permute-start | bytes 786440 | tf_op jit(solution)/shard_map/ppermute | solution.py:161
  81.6 10.9 %collective-permute-start.1 = (bf16[2,16,4,16,128]{4,3,2,1,0:T(8,128)(2,1)S(1)}, bf16[2,16,4,16,128]{4,3,2,1,0:T(8,128)(2,1)S(1)}, u32[]{:S(2)}, u32[]{:S(2)}) collective-permute-start(bf16[2,16,4,16,128]{4,3,2,1,0:T(8,128)(2,1)S(1)} %pad_maximum_fusion.1.near_ref), channel_id=1, source_target_pairs={{1,17},{17,1},{3,19},{19,3},{5,21},{21,5},{7,23},{23,7},{9,25},{25... | collective-permute-start | bytes 1572872 | tf_op jit(solution)/shard_map/ppermute | solution.py:166
  82.4 7.7 %collective-permute-start.2 = (bf16[16,4,16,128]{3,2,1,0:T(8,128)(2,1)S(1)}, bf16[16,4,16,128]{3,2,1,0:T(8,128)(2,1)S(1)}, u32[]{:S(2)}, u32[]{:S(2)}) collective-permute-start(bf16[16,4,16,128]{3,2,1,0:T(8,128)(2,1)S(1)} %get-tuple-element.32), channel_id=1, source_target_pairs={{0,1},{1,0},{2,3},{3,2},{4,5},{5,4},{6,7},{7,6},{8,9},{9,8},{10,11... | collective-permute-start | bytes 786440 | tf_op jit(solution)/shard_map/ppermute | solution.py:161
  88.1 3.4 %collective-permute-start.3 = (bf16[16,4,16,128]{3,2,1,0:T(8,128)(2,1)S(1)}, bf16[16,4,16,128]{3,2,1,0:T(8,128)(2,1)S(1)}, u32[]{:S(2)}, u32[]{:S(2)}) collective-permute-start(bf16[16,4,16,128]{3,2,1,0:T(8,128)(2,1)S(1)} %get-tuple-element.33), channel_id=1, source_target_pairs={{0,1},{1,0},{2,3},{3,2},{4,5},{5,4},{6,7},{7,6},{8,9},{9,8},{10,11... | collective-permute-start | bytes 786440 | tf_op jit(solution)/shard_map/ppermute | solution.py:161
  92.5 12.6 %collective-permute-start.4 = (bf16[2,16,4,16,128]{4,3,2,1,0:T(8,128)(2,1)S(1)}, bf16[2,16,4,16,128]{4,3,2,1,0:T(8,128)(2,1)S(1)}, u32[]{:S(2)}, u32[]{:S(2)}) collective-permute-start(bf16[2,16,4,16,128]{4,3,2,1,0:T(8,128)(2,1)S(1)} %pad_maximum_fusion.1.near_ref), channel_id=1, source_target_pairs={{0,16},{16,0},{2,18},{18,2},{4,20},{20,4},{6,22},{22,6},{8,24},{24... | collective-permute-start | bytes 1572872 | tf_op jit(solution)/shard_map/ppermute | solution.py:166
  168.4 3.9 %collective-permute-start.6 = (bf16[2,16,4,16,128]{4,3,2,1,0:T(8,128)(2,1)S(1)}, bf16[2,16,4,16,128]{4,3,2,1,0:T(8,128)(2,1)S(1)}, u32[]{:S(2)}, u32[]{:S(2)}) collective-permute-start(bf16[2,16,4,16,128]{4,3,2,1,0:T(8,128)(2,1)S(1)} %get-tuple-element.46), channel_id=1, source_target_pairs={{1,17},{17,1},{3,19},{19,3},{5,21},{21,5},{7,23},{23,7},{9,25},{25... | collective-permute-start | bytes 1572872 | tf_op jit(solution)/shard_map/ppermute | solution.py:166
  170.3 6.2 %collective-permute-start.5 = (bf16[32,4,16,128]{3,2,1,0:T(8,128)(2,1)S(1)}, bf16[32,4,16,128]{3,2,1,0:T(8,128)(2,1)S(1)}, u32[]{:S(2)}, u32[]{:S(2)}) collective-permute-start(bf16[32,4,16,128]{3,2,1,0:T(8,128)(2,1)S(1)} %get-tuple-element.44), channel_id=1, source_target_pairs={{0,1},{1,0},{2,3},{3,2},{4,5},{5,4},{6,7},{7,6},{8,9},{9,8},{10,11... | collective-permute-start | bytes 1572872 | tf_op jit(solution)/shard_map/ppermute | solution.py:161
  172.3 12.6 %collective-permute-start.7 = (bf16[2,16,4,16,128]{4,3,2,1,0:T(8,128)(2,1)S(1)}, bf16[2,16,4,16,128]{4,3,2,1,0:T(8,128)(2,1)S(1)}, u32[]{:S(2)}, u32[]{:S(2)}) collective-permute-start(bf16[2,16,4,16,128]{4,3,2,1,0:T(8,128)(2,1)S(1)} %get-tuple-element.46), channel_id=1, source_target_pairs={{0,16},{16,0},{2,18},{18,2},{4,20},{20,4},{6,22},{22,6},{8,24},{24... | collective-permute-start | bytes 1572872 | tf_op jit(solution)/shard_map/ppermute | solution.py:166
  184.8 31.5 %all-to-all-start.3 = ((bf16[128,16,128]{2,1,0:T(8,128)(2,1)}), bf16[128,16,128]{2,1,0:T(8,128)(2,1)S(1)}, u32[]{:S(2)}, u32[]{:S(2)}) async-start(bf16[128,16,128]{2,1,0:T(8,128)(2,1)} %bitcast.12), calls=%async_computation.3 | async-start | bytes 1048576 | tf_op jit(solution)/shard_map/all_to_all | solution.py:170
  193.5 3.4 %collective-permute-start.8 = (bf16[4,4,4,16,128]{4,3,2,1,0:T(8,128)(2,1)S(1)}, bf16[4,4,4,16,128]{4,3,2,1,0:T(8,128)(2,1)S(1)}, u32[]{:S(2)}, u32[]{:S(2)}) collective-permute-start(bf16[4,4,4,16,128]{4,3,2,1,0:T(8,128)(2,1)S(1)} %bitcast.42), channel_id=1, source_target_pairs={{0,1},{1,0},{2,3},{3,2},{4,5},{5,4},{6,7},{7,6},{8,9},{9,8},{10,11... | collective-permute-start | bytes 786440 | tf_op jit(solution)/shard_map/ppermute | solution.py:161
